TPU v7x, 128 devices: a whole 4x4x4 slice. The times are simulated.
128 devices in a mesh: row: 8 (over x, z_lo), col: 16 (over z_hi, y, core).
Axes of the slice: x: 4, y: 4, z: 4 (z_hi: 2, z_lo: 2; z = z_hi * 2 + z_lo), core: 2. Of those that a mesh axis runs over, the one named last changes fastest.
Arguments:
- object_field: float32 [2, 2, 4096, 8192], P(None, None, 'row', 'col'), may hold values from -4 to 4
- probe: float32 [2, 256, 256], replicated, may hold values from -5 to 5
- measured: float32 [1024, 256, 256], P(('row', 'col')), may hold values from 0.2 to 4
- offsets: int32 [1024, 2], P(('row', 'col')), may hold values from 0 to 511, as said below
- counts: int32 [128], P(('row', 'col')), may hold values from 1 to 8, as said below
Outputs:
- object_grad: float32 [2, 2, 4096, 8192], P(None, None, 'row', 'col')
- probe_grad: float32 [2, 256, 256], replicated
Inputs may be any that keep to these rules, and one draw needn't show every extreme that they name: Every patch of 256 x 256 pixels lies inside the object; offsets reach the largest value of their range. `counts`: some device has all 8 slots live in every draw.
All inputs are finite; a program needn't handle non-finite values.
Results may differ from a plain program's by a relative error of at most 0.00013.
Values sent between devices are 32-bit elements; how exact they have to be, the bound alone decides.
No kernel may reach another device: no remote copies, remote signals or barrier semaphores. Data moves between devices by JAX's collectives and lax.ppermute only.
A program may use at most 128 MiB of HBM per device.

v0:
```python
import math

import jax
import jax.numpy as jnp
from jax import lax
from jax.sharding import PartitionSpec as P

fresnel = 40.0


def passed_along(shard, axis, by):
    length = lax.axis_size(axis)
    pairs = [(i, i + by) for i in range(length) if 0 <= i + by < length]
    return lax.ppermute(shard, axis, pairs)


def matmul(left, right):
    return jnp.dot(left, right, precision=lax.Precision.HIGHEST, preferred_element_type=jnp.float32)


def make_tables(pattern_side):
    indices = jnp.arange(pattern_side, dtype=jnp.int32)
    product = indices[:, None] * indices[None, :] % pattern_side
    angles = 2.0 * math.pi / pattern_side * product.astype(jnp.float32)
    scale = 1.0 / math.sqrt(pattern_side)
    cos_table = jnp.cos(angles) * scale
    sin_table = jnp.sin(angles) * scale
    freqs = (indices + pattern_side // 2) % pattern_side - pattern_side // 2
    squared = freqs * freqs
    phase = (
        fresnel
        * math.pi
        / (pattern_side * pattern_side)
        * (squared[:, None] + squared[None, :]).astype(jnp.float32)
    )
    return (cos_table, sin_table, jnp.cos(phase), jnp.sin(phase))


def transform(real_part, imag_part, mat_real, mat_imag):
    left_re = matmul(mat_real, real_part) - matmul(mat_imag, imag_part)
    left_im = matmul(mat_real, imag_part) + matmul(mat_imag, real_part)
    out_re = matmul(left_re, mat_real) - matmul(left_im, mat_imag)
    out_im = matmul(left_re, mat_imag) + matmul(left_im, mat_real)
    return (out_re, out_im)


def slot_loss(sample_patch, probe, pattern, weight, tables):
    cos_table, sin_table, prop_re, prop_im = tables
    wave_re = probe[0] * sample_patch[0, 0] - probe[1] * sample_patch[1, 0]
    wave_im = probe[0] * sample_patch[1, 0] + probe[1] * sample_patch[0, 0]
    freq_re, freq_im = transform(wave_re, wave_im, cos_table, -sin_table)
    moved_re = freq_re * prop_re - freq_im * prop_im
    moved_im = freq_re * prop_im + freq_im * prop_re
    back_re, back_im = transform(moved_re, moved_im, cos_table, sin_table)
    wave_re = back_re * sample_patch[0, 1] - back_im * sample_patch[1, 1]
    wave_im = back_re * sample_patch[1, 1] + back_im * sample_patch[0, 1]
    far_re, far_im = transform(wave_re, wave_im, cos_table, -sin_table)
    misfit = far_re * far_re + far_im * far_im - pattern
    return 0.5 * weight * jnp.sum(misfit * misfit)


def per_device(object_field, probe, measured, offsets, counts):
    layers = object_field.shape[1]
    height = object_field.shape[2]
    width = object_field.shape[3]
    side = probe.shape[1]
    slots_here = measured.shape[0]
    right_rim = passed_along(object_field[:, :, :, :side], "col", -1)
    widened = jnp.concatenate([object_field, right_rim], axis=3)
    lower_rim = passed_along(widened[:, :, :side, :], "row", -1)
    extended = jnp.concatenate([widened, lower_rim], axis=2)
    tables = make_tables(side)
    weights = (jnp.arange(slots_here, dtype=jnp.int32) < counts[0]).astype(jnp.float32)

    def slot_grad(offset, pattern, weight):
        start = (jnp.int32(0), jnp.int32(0), offset[0], offset[1])
        sample_patch = lax.dynamic_slice(extended, start, (2, layers, side, side))

        def local_loss(patch_arg, probe_arg):
            return slot_loss(patch_arg, probe_arg, pattern, weight, tables)

        unused, pull = jax.vjp(local_loss, sample_patch, probe)
        return pull(jnp.ones((), jnp.float32))

    patch_grads, probe_terms = jax.vmap(slot_grad)(offsets, measured, weights)
    probe_grad = lax.psum(jnp.sum(probe_terms, axis=0), ("row", "col"))
    grid = jnp.zeros(extended.shape, jnp.float32)
    for slot_index in range(slots_here):
        start = (jnp.int32(0), jnp.int32(0), offsets[slot_index, 0], offsets[slot_index, 1])
        current = lax.dynamic_slice(grid, start, (2, layers, side, side))
        grid = lax.dynamic_update_slice(grid, current + patch_grads[slot_index], start)
    from_above = passed_along(grid[:, :, height:, :], "row", 1)
    upper = grid[:, :, :height, :]
    upper = upper.at[:, :, :side, :].add(from_above)
    from_left = passed_along(upper[:, :, :, width:], "col", 1)
    tile_grad = upper[:, :, :, :width]
    tile_grad = tile_grad.at[:, :, :, :side].add(from_left)
    return (tile_grad, probe_grad)


def solution(mesh):
    placed = (
        P(None, None, "row", "col"),
        P(),
        P(("row", "col"), None, None),
        P(("row", "col"), None),
        P(("row", "col")),
    )
    return jax.shard_map(
        per_device,
        mesh=mesh,
        in_specs=placed,
        out_specs=(P(None, None, "row", "col"), P()),
        check_vma=False,
    )
```

profile of v0, /device:TPU:3, one launch (start us, length us, event | category | flops | bytes accessed | tf_op | source)
XLA Modules:
  0.0 709.1 jit_solution(12508662015494097057)
XLA Ops:
  12.2 24.8 %collective-permute-done = f32[2,2,512,256]{3,2,1,0:T(8,128)S(1)} collective-permute-done((f32[2,2,512,256]{3,2,1,0:T(8,128)S(1)}, f32[2,2,512,256]{3,2,1,0:T(8,128)S(1)}, u32[]{:S(2)}, u32[]{:S(2)}) %collective-permute-start) | collective-permute-done | bytes 2097184 | tf_op jit(solution)/shard_map/ppermute | solution.py:14
  40.8 3.6 collective-permute-start.1
  77.5 14.7 %collective-permute-done.1 = f32[2,2,256,768]{3,2,1,0:T(8,128)} collective-permute-done((f32[2,2,256,768]{3,2,1,0:T(8,128)}, f32[2,2,256,768]{3,2,1,0:T(8,128)}, u32[]{:S(2)}, u32[]{:S(2)}) %collective-permute-start.1) | collective-permute-done | bytes 3145760 | tf_op jit(solution)/shard_map/ppermute | solution.py:14
  92.2 8.0 %pad_maximum_fusion = f32[2,2,768,768]{3,2,1,0:T(8,128)} fusion(f32[2,2,256,768]{3,2,1,0:T(8,128)} %collective-permute-done.1, f32[2,2,512,768]{3,2,1,0:T(8,128)} %copy-done.2), kind=kLoop, calls=%fused_computation.2 | loop fusion | flops 2359296 | bytes 18874368 | tf_op jit(solution)/shard_map/concatenate | solution.py:71
  100.3 37.7 %while.3 = (s32[]{:T(128)}, f32[2,2,768,768]{3,2,1,0:T(8,128)}, s32[8,4]{0,1:T(4,128)S(1)}, f32[8,2,2,256,256]{4,3,0,2,1:T(8,128)}, s32[]{:T(128)}) while((s32[]{:T(128)}, f32[2,2,768,768]{3,2,1,0:T(8,128)}, s32[8,4]{0,1:T(4,128)S(1)}, f32[8,2,2,256,256]{4,3,0,2,1:T(8,128)}, s32[]{:T(128)}) %tuple.66), condition=%wide.while_cond.2, body=%wide.while_body.2.sunk | while | flops 2 | bytes 2098801 | solution.py:77
  100.9 4.1 bitcast_dynamic-update-slice_fusion.2
  105.6 4.0 bitcast_dynamic-update-slice_fusion.2
  110.2 4.1 bitcast_dynamic-update-slice_fusion.2
  114.9 4.1 bitcast_dynamic-update-slice_fusion.2
  119.6 4.1 bitcast_dynamic-update-slice_fusion.2
  124.3 4.1 bitcast_dynamic-update-slice_fusion.2
  129.0 4.1 bitcast_dynamic-update-slice_fusion.2
  133.7 4.1 bitcast_dynamic-update-slice_fusion.2
  138.0 5.4 fusion.146
  143.4 5.2 fusion.150
  148.7 3.1 convolution_subtract_fusion.4
  151.7 3.3 fusion.148
  157.9 3.1 convolution_add_fusion.10
  166.8 3.3 fusion.21
  170.1 3.1 fusion.23
  173.2 3.2 fusion.62
  182.3 3.1 fusion.65
  188.3 3.7 fusion.19
  212.3 3.5 bitcast_multiply_fusion.15
  227.6 4.7 fusion.100
  235.2 4.4 fusion.47
  239.6 8.1 %fusion.13 = (f32[8,1,1,256,256]{4,3,0,2,1:T(8,128)S(1)}, f32[8,1,1,256,256]{4,3,0,2,1:T(8,128)S(1)}, f32[8,256,256]{2,1,0:T(8,128)S(1)}, f32[8,256,256]{2,1,0:T...) fusion(f32[8,256,256]{1,2,0:T(8,128)} %fusion.47, ...), kind=kOutput, calls=%fused_computation.38 | convolution fusion | flops 1617887232 | bytes 27262976 | tf_op jit(solution)/shard_map/vmap(transpose(jvp()))/dot_general | solution.py:18
  256.2 4.6 fusion.123
  260.8 4.3 fusion.84
  267.9 5.0 fusion.53
  272.9 4.5 convolution_add_fusion.2
  277.4 4.5 fusion.77
  281.9 4.7 fusion.79
  286.6 4.7 fusion.56
  294.3 4.5 fusion.95
  298.8 4.5 convolution_add_fusion.1
  303.3 4.4 fusion.59
  307.7 9.6 %fusion.6 = (f32[8,1,256,256]{3,2,0,1:T(8,128)S(1)}, f32[8,1,256,256]{3,2,0,1:T(8,128)}, f32[8,1,256,256]{3,2,0,1:T(8,128)}, f32[8,1,256,256]{3,2,0,1:T(8,128)},...) fusion(f32[8,256,256]{1,2,0:T(8,128)} %fusion.59, ...), kind=kOutput, calls=%fused_computation.20 | convolution fusion | flops 1616838656 | bytes 27787264 | tf_op jit(solution)/shard_map/vmap(transpose(jvp()))/dot_general | solution.py:18
  317.3 4.1 pad_add_fusion
  321.5 3.3 copy-done.1
  325.8 4.5 broadcast_in_dim.56
  330.3 10.9 %dynamic_update_slice.24 = f32[2,2,768,768]{3,2,1,0:T(8,128)} dynamic-update-slice(f32[2,2,768,768]{3,2,1,0:T(8,128)} %broadcast_in_dim.56, f32[2,2,256,256]{3,2,1,0:T(8,128)} %slice_bitcast_fusion.7, s32[]{:T(128)} %constant.88.clone.1, s32[]{:T(128)} %constant.88.clone.1, s32[]{:T(128)S(6)} %select_n.203, s32[]{:T(128)S(6)} %select_n.204) | dynamic-update-slice | bytes 2097156 | tf_op jit(solution)/shard_map/dynamic_update_slice | solution.py:91
  341.2 3.1 fusion.74
  344.3 12.3 %dynamic_update_slice.25 = f32[2,2,768,768]{3,2,1,0:T(8,128)} dynamic-update-slice(f32[2,2,768,768]{3,2,1,0:T(8,128)} %dynamic_update_slice.24, f32[2,2,256,256]{3,2,1,0:T(8,128)} %fusion.74, s32[]{:T(128)} %constant.88.clone.1, s32[]{:T(128)} %constant.88.clone.1, s32[]{:T(128)S(6)} %select_n.205, s32[]{:T(128)S(6)} %select_n.206) | dynamic-update-slice | bytes 2097156 | tf_op jit(solution)/shard_map/dynamic_update_slice | solution.py:91
  356.6 3.1 fusion.73
  359.7 12.3 %dynamic_update_slice.26 = f32[2,2,768,768]{3,2,1,0:T(8,128)} dynamic-update-slice(f32[2,2,768,768]{3,2,1,0:T(8,128)} %dynamic_update_slice.25, f32[2,2,256,256]{3,2,1,0:T(8,128)} %fusion.73, s32[]{:T(128)} %constant.88.clone.1, s32[]{:T(128)} %constant.88.clone.1, s32[]{:T(128)S(6)} %select_n.207, s32[]{:T(128)S(6)} %select_n.208) | dynamic-update-slice | bytes 2097156 | tf_op jit(solution)/shard_map/dynamic_update_slice | solution.py:91
  372.0 3.1 fusion.72
  375.1 12.0 %dynamic_update_slice.27 = f32[2,2,768,768]{3,2,1,0:T(8,128)} dynamic-update-slice(f32[2,2,768,768]{3,2,1,0:T(8,128)} %dynamic_update_slice.26, f32[2,2,256,256]{3,2,1,0:T(8,128)} %fusion.72, s32[]{:T(128)} %constant.88.clone.1, s32[]{:T(128)} %constant.88.clone.1, s32[]{:T(128)S(6)} %select_n.209, s32[]{:T(128)S(6)} %select_n.210) | dynamic-update-slice | bytes 2097156 | tf_op jit(solution)/shard_map/dynamic_update_slice | solution.py:91
  387.0 3.1 fusion.71
  390.1 12.3 %dynamic_update_slice.28 = f32[2,2,768,768]{3,2,1,0:T(8,128)} dynamic-update-slice(f32[2,2,768,768]{3,2,1,0:T(8,128)} %dynamic_update_slice.27, f32[2,2,256,256]{3,2,1,0:T(8,128)} %fusion.71, s32[]{:T(128)} %constant.88.clone.1, s32[]{:T(128)} %constant.88.clone.1, s32[]{:T(128)S(6)} %select_n.211, s32[]{:T(128)S(6)} %select_n.212) | dynamic-update-slice | bytes 2097156 | tf_op jit(solution)/shard_map/dynamic_update_slice | solution.py:91
  402.4 3.1 fusion.70
  405.5 12.2 %dynamic_update_slice.29 = f32[2,2,768,768]{3,2,1,0:T(8,128)} dynamic-update-slice(f32[2,2,768,768]{3,2,1,0:T(8,128)} %dynamic_update_slice.28, f32[2,2,256,256]{3,2,1,0:T(8,128)} %fusion.70, s32[]{:T(128)} %constant.88.clone.1, s32[]{:T(128)} %constant.88.clone.1, s32[]{:T(128)S(6)} %select_n.213, s32[]{:T(128)S(6)} %select_n.214) | dynamic-update-slice | bytes 2097156 | tf_op jit(solution)/shard_map/dynamic_update_slice | solution.py:91
  417.6 3.1 fusion.69
  420.7 12.1 %dynamic_update_slice.30 = f32[2,2,768,768]{3,2,1,0:T(8,128)} dynamic-update-slice(f32[2,2,768,768]{3,2,1,0:T(8,128)} %dynamic_update_slice.29, f32[2,2,256,256]{3,2,1,0:T(8,128)} %fusion.69, s32[]{:T(128)} %constant.88.clone.1, s32[]{:T(128)} %constant.88.clone.1, s32[]{:T(128)S(6)} %select_n.215, s32[]{:T(128)S(6)} %select_n.216) | dynamic-update-slice | bytes 2097156 | tf_op jit(solution)/shard_map/dynamic_update_slice | solution.py:91
  432.9 3.1 fusion.68
  435.9 12.2 %dynamic_update_slice.31 = f32[2,2,768,768]{3,2,1,0:T(8,128)} dynamic-update-slice(f32[2,2,768,768]{3,2,1,0:T(8,128)} %dynamic_update_slice.30, f32[2,2,256,256]{3,2,1,0:T(8,128)} %fusion.68, s32[]{:T(128)} %constant.88.clone.1, s32[]{:T(128)} %constant.88.clone.1, s32[]{:T(128)S(6)} %select_n.217, s32[]{:T(128)S(6)} %select_n.218) | dynamic-update-slice | bytes 2097156 | tf_op jit(solution)/shard_map/dynamic_update_slice | solution.py:91
  450.3 3.2 collective-permute-start.2
  453.6 3.3 slice.248
  456.9 45.1 %collective-permute-done.2 = f32[2,2,256,768]{3,2,1,0:T(8,128)S(1)} collective-permute-done((f32[2,2,256,768]{3,2,1,0:T(8,128)S(1)}, f32[2,2,256,768]{3,2,1,0:T(8,128)S(1)}, u32[]{:S(2)}, u32[]{:S(2)}) %collective-permute-start.2) | collective-permute-done | bytes 3145760 | tf_op jit(solution)/shard_map/ppermute | solution.py:14
  508.8 42.7 %collective-permute-start.3 = (f32[2,2,512,256]{3,2,1,0:T(8,128)}, f32[2,2,512,256]{3,2,1,0:T(8,128)}, u32[]{:S(2)}, u32[]{:S(2)}) collective-permute-start(f32[2,2,512,256]{3,2,1,0:T(8,128)} %slice.253), channel_id=1, source_target_pairs={{0,1},{1,2},{2,3},{3,4},{4,5},{5,6},{6,7},{7,8},{8,9},{9,10},{10,1... | collective-permute-start | bytes 6291464 | tf_op jit(solution)/shard_map/ppermute | solution.py:14
  553.1 4.6 slice.251
  557.8 17.4 %collective-permute-done.3 = f32[2,2,512,256]{3,2,1,0:T(8,128)} collective-permute-done((f32[2,2,512,256]{3,2,1,0:T(8,128)}, f32[2,2,512,256]{3,2,1,0:T(8,128)}, u32[]{:S(2)}, u32[]{:S(2)}) %collective-permute-start.3) | collective-permute-done | bytes 2097184 | tf_op jit(solution)/shard_map/ppermute | solution.py:14
  575.2 3.8 fusion.1
  579.0 120.9 %all-reduce.14.cloned.1.call-done = f32[2,256,256]{2,1,0:T(8,128)} async-done(((f32[2,256,256]{2,1,0:T(8,128)}), f32[2,256,256]{2,1,0:T(8,128)}) %all-reduce.14.cloned.1.call-update) | async-done | bytes 524304 | tf_op jit(solution)/shard_map/psum | solution.py:86
  (89 shorter events, 96.0 us)
Async XLA Ops:
  7.2 692.8 %all-reduce.14.cloned.1.call-start = ((), (), s32[]{:S(2)}) async-start(), calls=%async_computation | async-start | bytes 1048576 | tf_op jit(solution)/shard_map/psum | solution.py:86
  7.2 4.5 copy-start.4
  9.1 27.9 %collective-permute-start = (f32[2,2,512,256]{3,2,1,0:T(8,128)S(1)}, f32[2,2,512,256]{3,2,1,0:T(8,128)S(1)}, u32[]{:S(2)}, u32[]{:S(2)}) collective-permute-start(f32[2,2,512,256]{3,2,1,0:T(8,128)S(1)} %slice.181), channel_id=1, source_target_pairs={{1,0},{2,1},{3,2},{4,3},{5,4},{6,5},{7,6},{8,7},{9,8},{10,9},{11,1... | collective-permute-start | bytes 6291464 | tf_op jit(solution)/shard_map/ppermute | solution.py:14
  37.2 3.6 copy-start.2
  37.2 7.3 %copy-start.12 = (s32[8,2]{0,1:T(2,128)S(1)}, s32[8,2]{0,1:T(2,128)}, u32[]{:S(2)}) copy-start(s32[8,2]{0,1:T(2,128)} %param.12) | copy-start | bytes 196
  40.8 36.7 %copy-start.11 = (f32[2,256,256]{2,1,0:T(8,128)S(1)}, f32[2,256,256]{2,1,0:T(8,128)}, u32[]{:S(2)}) copy-start(f32[2,256,256]{2,1,0:T(8,128)} %param.10) | copy-start | bytes 1572868
  40.8 51.5 %collective-permute-start.1 = (f32[2,2,256,768]{3,2,1,0:T(8,128)}, f32[2,2,256,768]{3,2,1,0:T(8,128)}, u32[]{:S(2)}, u32[]{:S(2)}) collective-permute-start(f32[2,2,256,768]{3,2,1,0:T(8,128)} %slice.239), channel_id=1, source_target_pairs={{16,0},{32,16},{48,32},{64,48},{80,64},{96,80},{112,96},{17,1},{33... | collective-permute-start | bytes 9437192 | tf_op jit(solution)/shard_map/ppermute | solution.py:14
  138.0 10.7 %copy-start.3 = (f32[8,2,2,256,256]{4,3,0,2,1:T(8,128)S(1)}, f32[8,2,2,256,256]{4,3,0,2,1:T(8,128)}, u32[]{:S(2)}) copy-start(f32[8,2,2,256,256]{4,3,0,2,1:T(8,128)} %get-tuple-element.33) | copy-start | bytes 25165828
  209.5 2.8 copy-start.10
  307.7 9.6 %copy-start.8 = (f32[8,1,1,256,256]{4,3,0,2,1:T(8,128)S(1)}, f32[8,1,1,256,256]{4,3,0,2,1:T(8,128)}, u32[]{:S(2)}) copy-start(f32[8,1,1,256,256]{4,3,0,2,1:T(8,128)} %get-tuple-element.64) | copy-start | bytes 6291460
  307.7 9.6 %copy-start.9 = (f32[8,1,1,256,256]{4,3,0,2,1:T(8,128)S(1)}, f32[8,1,1,256,256]{4,3,0,2,1:T(8,128)}, u32[]{:S(2)}) copy-start(f32[8,1,1,256,256]{4,3,0,2,1:T(8,128)} %get-tuple-element.65) | copy-start | bytes 6291460
  321.5 3.3 copy-start.1
  450.3 51.6 %collective-permute-start.2 = (f32[2,2,256,768]{3,2,1,0:T(8,128)S(1)}, f32[2,2,256,768]{3,2,1,0:T(8,128)S(1)}, u32[]{:S(2)}, u32[]{:S(2)}) collective-permute-start(f32[2,2,256,768]{3,2,1,0:T(8,128)S(1)} %slice.250), channel_id=1, source_target_pairs={{0,16},{16,32},{32,48},{48,64},{64,80},{80,96},{96,112},{1,17},{17... | collective-permute-start | bytes 9437192 | tf_op jit(solution)/shard_map/ppermute | solution.py:14
  501.9 49.5 %copy-start.7 = (f32[8,1,256,256]{3,2,0,1:T(8,128)S(1)}, f32[8,1,256,256]{3,2,0,1:T(8,128)}, u32[]{:S(2)}) copy-start(f32[8,1,256,256]{3,2,0,1:T(8,128)} %get-tuple-element.53) | copy-start | bytes 6291460
  504.6 2.7 copy-start
  507.2 44.3 %copy-start.5 = (f32[8,1,256,256]{3,2,0,1:T(8,128)S(1)}, f32[8,1,256,256]{3,2,0,1:T(8,128)}, u32[]{:S(2)}) copy-start(f32[8,1,256,256]{3,2,0,1:T(8,128)} %get-tuple-element.49) | copy-start | bytes 6291460
  507.2 44.3 %copy-start.6 = (f32[8,1,256,256]{3,2,0,1:T(8,128)S(1)}, f32[8,1,256,256]{3,2,0,1:T(8,128)}, u32[]{:S(2)}) copy-start(f32[8,1,256,256]{3,2,0,1:T(8,128)} %get-tuple-element.52) | copy-start | bytes 6291460
  508.8 66.4 %collective-permute-start.3 = (f32[2,2,512,256]{3,2,1,0:T(8,128)}, f32[2,2,512,256]{3,2,1,0:T(8,128)}, u32[]{:S(2)}, u32[]{:S(2)}) collective-permute-start(f32[2,2,512,256]{3,2,1,0:T(8,128)} %slice.253), channel_id=1, source_target_pairs={{0,1},{1,2},{2,3},{3,4},{4,5},{5,6},{6,7},{7,8},{8,9},{9,10},{10,1... | collective-permute-start | bytes 6291464 | tf_op jit(solution)/shard_map/ppermute | solution.py:14
Sparse Core Ops, SparseCore 0:
  553.2 146.6 all-reduce.13
where the time goes:
time: 719 us; the launch traced here: 709 us
  waiting for transfers between devices  223 us (31%)
  matrix products  179 us (25%)
  local copies, waits for them, and re-layouts  166 us (23%)
  starting transfers between devices  52.1 us (7%)
  between operations  46 us (6%)
  other arithmetic  42.8 us (6%)
    dot_general x48, matrix products, matmul(): jnp.dot(left, right, precision=lax.Precision.HIGHEST, preferred_element_t...  179 us
    psum x1, waiting for transfers between devices, per_device(): probe_grad = lax.psum(jnp.sum(probe_terms, axis=0), ('row', 'col'))  121 us
    ppermute x4, waiting for transfers between devices, passed_along(): return lax.ppermute(shard, axis, pairs)  102 us
    dynamic_update_slice x8, local copies, waits for them, and re-layouts, per_device(): lax.dynamic_update_slice(grid, current + patch_grads[slot_index], start)  96.3 us
    ppermute x4, starting transfers between devices, passed_along(): return lax.ppermute(shard, axis, pairs)  52.1 us
    gather x24, local copies, waits for them, and re-layouts  37.5 us
    add x7, other arithmetic, per_device(): current + patch_grads[slot_index]  21.5 us
  transfers between devices with their start and end apart: 5, of which 5 were waited for; matrix products, arithmetic and copies ran while one was open for 2% of the time, Pallas kernels for 0%

commit v1 on v0

v1 whole, which is shorter than its diff:
```python
import math

import jax
import jax.numpy as jnp
import ml_dtypes
import numpy as np
from jax import lax
from jax.experimental import pallas as pl
from jax.experimental.pallas import tpu as pltpu
from jax.sharding import PartitionSpec as P

fresnel = 40.0


def passed_along(shard, axis, by):
    length = lax.axis_size(axis)
    pairs = [(i, i + by) for i in range(length) if 0 <= i + by < length]
    return lax.ppermute(shard, axis, pairs)


def real_form(matrix):
    return np.block([[matrix.real, -matrix.imag], [matrix.imag, matrix.real]])


def make_tables(side):
    half = side // 2
    index = np.arange(side)
    dft = np.exp(-2j * np.pi * ((index[:, None] * index[None, :]) % side) / side) / math.sqrt(side)
    freqs = (index + half) % side - half
    chirp = np.exp(1j * fresnel * np.pi * (freqs * freqs) / (side * side))
    circulant = (dft.conj() * chirp[None, :]) @ dft
    near, far = circulant[:half, :half], circulant[:half, half:]
    mats = [real_form((near + far) / 2), real_form((near - far) / 2)]
    mats += [real_form(dft[0::2, :half]), real_form(dft[1::2, :half])]
    full = np.stack([mats[0], mats[1], mats[0].T, mats[1].T, mats[2], mats[3], mats[2].T, mats[3].T])
    full = full.astype(np.float32)
    high = full.astype(ml_dtypes.bfloat16)
    low = (full - high.astype(np.float32)).astype(ml_dtypes.bfloat16)
    return np.stack([high, low], axis=1)


def split(x):
    high = x.astype(jnp.bfloat16)
    return high, (x - high.astype(jnp.float32)).astype(jnp.bfloat16)


def dot(a, b):
    return jnp.dot(a, b, preferred_element_type=jnp.float32)


def fold(x):
    half = x.shape[0] // 2
    rows = (x[:half] + x[half:], x[:half] - x[half:])
    return [(r[:, :half] + r[:, half:], r[:, :half] - r[:, half:]) for r in rows]


def unfold(quads):
    (uu, uv), (vu, vv) = quads
    rows_u = jnp.concatenate([uu + uv, uu - uv], axis=1)
    rows_v = jnp.concatenate([vu + vv, vu - vv], axis=1)
    return jnp.concatenate([rows_u + rows_v, rows_u - rows_v], axis=0)


def two_sided(quads_re, quads_im, tables, left, right):
    half = quads_re[0][0].shape[0]
    lefts = []
    for p in range(2):
        z = jnp.concatenate(
            [jnp.concatenate(quads_re[p], axis=1), jnp.concatenate(quads_im[p], axis=1)], axis=0
        )
        z_hi, z_lo = split(z)
        m_hi, m_lo = tables[left + p, 0], tables[left + p, 1]
        lefts.append(
            dot(
                jnp.concatenate([m_hi, m_hi, m_lo], axis=1),
                jnp.concatenate([z_hi, z_lo, z_hi], axis=0),
            )
        )
    out_re = [[None, None], [None, None]]
    out_im = [[None, None], [None, None]]
    for q in range(2):
        cols = slice(q * half, (q + 1) * half)
        v = jnp.concatenate(
            [jnp.concatenate([w[:half, cols], w[half:, cols]], axis=1) for w in lefts], axis=0
        )
        v_hi, v_lo = split(v)
        m_hi, m_lo = tables[right + q, 0], tables[right + q, 1]
        y = dot(
            jnp.concatenate([v_hi, v_hi, v_lo], axis=1),
            jnp.concatenate([m_hi, m_lo, m_hi], axis=0),
        )
        for p in range(2):
            out_re[p][q] = y[p * half : (p + 1) * half, :half]
            out_im[p][q] = y[p * half : (p + 1) * half, half:]
    return out_re, out_im


def whole(quads):
    return jnp.concatenate([jnp.concatenate(r, axis=1) for r in quads], axis=0)


def quarters(x):
    half = x.shape[0] // 2
    return [(r[:, :half], r[:, half:]) for r in (x[:half], x[half:])]


LANES = 128
ROWS = 8


def gradient_kernel(
    offsets, counts, obj, right, lower, corner, probe, measured, tables,
    main_out, right_out, corner_out, lower_out, probe_out,
    ext, grid,
):
    side = probe.shape[1]
    height, width = obj.shape[2], obj.shape[3]
    layers = obj.shape[1]
    ext[:, :, :height, :width] = obj[...]
    ext[:, :, :height, width:] = right[...]
    ext[:, :, height:, :width] = lower[...]
    ext[:, :, height:, width:] = corner[...]
    grid[...] = jnp.zeros_like(grid)
    probe_out[...] = jnp.zeros_like(probe_out)
    blocks, tiles = side // LANES, side // ROWS
    lane = lax.broadcasted_iota(jnp.int32, (tiles, ROWS, LANES), 2)
    row = lax.broadcasted_iota(jnp.int32, (tiles, ROWS, LANES), 1)
    row_more = lax.broadcasted_iota(jnp.int32, (tiles + 1, ROWS, LANES), 1)

    def place(part, layer, top, edge, k):
        first = pl.multiple_of(top // ROWS * ROWS, ROWS)
        start = pl.multiple_of(edge // LANES * LANES + k * LANES, LANES)
        return (part, layer, pl.ds(first, side + ROWS), pl.ds(start, LANES))

    def patch(part, layer, top, edge):
        down, over = top % ROWS, edge % LANES
        turned = []
        for k in range(blocks + 1):
            x = ext[place(part, layer, top, edge, k)].reshape(tiles + 1, ROWS, LANES)
            x = pltpu.roll(x, (ROWS - down) % ROWS, 1)
            x = jnp.where(row < ROWS - down, x[:-1], x[1:])
            turned.append(pltpu.roll(x, (LANES - over) % LANES, 2))
        keep = lane < LANES - over
        return jnp.concatenate(
            [jnp.where(keep, turned[k], turned[k + 1]).reshape(side, LANES) for k in range(blocks)], axis=1
        )

    def add_patch(part, layer, top, edge, value):
        down, over = top % ROWS, edge % LANES
        turned = []
        zero = jnp.zeros((tiles, ROWS, LANES), jnp.float32)
        none = jnp.zeros((1, ROWS, LANES), jnp.float32)
        for k in range(blocks):
            x = value[:, k * LANES : (k + 1) * LANES].reshape(tiles, ROWS, LANES)
            turned.append(pltpu.roll(x, over, 2))
        for k in range(blocks + 1):
            after = turned[k] if k < blocks else zero
            before = turned[k - 1] if k > 0 else zero
            x = pltpu.roll(jnp.where(lane >= over, after, before), down, 1)
            x = jnp.where(
                row_more >= down, jnp.concatenate([x, none], axis=0), jnp.concatenate([none, x], axis=0)
            )
            at = place(part, layer, top, edge, k)
            grid[at] = grid[at] + x.reshape(side + ROWS, LANES)

    def visit(slot, carry):
        top = offsets[slot, 0]
        where = (top, offsets[slot, 1])

        p_re, p_im = probe[0], probe[1]
        a_re, a_im = patch(0, 0, *where), patch(1, 0, *where)
        psi_re = p_re * a_re - p_im * a_im
        psi_im = p_re * a_im + p_im * a_re
        y_re, y_im = two_sided(fold(psi_re), fold(psi_im), tables, 0, 2)
        phi_re, phi_im = unfold(y_re), unfold(y_im)

        b_re, b_im = patch(0, 1, *where), patch(1, 1, *where)
        psi_re = phi_re * b_re - phi_im * b_im
        psi_im = phi_re * b_im + phi_im * b_re
        y_re, y_im = two_sided(fold(psi_re), fold(psi_im), tables, 4, 6)
        far_re, far_im = whole(y_re), whole(y_im)
        misfit = 2.0 * (far_re * far_re + far_im * far_im - measured[slot])
        y_re, y_im = two_sided(quarters(misfit * far_re), quarters(misfit * far_im), tables, 6, 4)
        d_re, d_im = unfold(y_re), unfold(y_im)
        add_patch(0, 1, *where, phi_re * d_re + phi_im * d_im)
        add_patch(1, 1, *where, phi_re * d_im - phi_im * d_re)

        e_re = b_re * d_re + b_im * d_im
        e_im = b_re * d_im - b_im * d_re
        y_re, y_im = two_sided(fold(e_re), fold(e_im), tables, 2, 0)
        d_re, d_im = unfold(y_re), unfold(y_im)
        add_patch(0, 0, *where, p_re * d_re + p_im * d_im)
        add_patch(1, 0, *where, p_re * d_im - p_im * d_re)
        a_re, a_im = patch(0, 0, *where), patch(1, 0, *where)
        probe_out[0] += a_re * d_re + a_im * d_im
        probe_out[1] += a_re * d_im - a_im * d_re
        return carry

    lax.fori_loop(0, jnp.minimum(counts[0], measured.shape[0]), visit, 0)
    main_out[...] = grid[:, :, :height, :width]
    right_out[...] = grid[:, :, :height, width:]
    lower_out[...] = grid[:, :, height:, :width]
    corner_out[...] = grid[:, :, height:, width:]


def sum_over_all(value):
    rows, cols = lax.axis_size("row"), lax.axis_size("col")
    flat = value.reshape(cols, -1, LANES)
    share = jnp.sum(lax.all_to_all(flat, "col", 0, 0, tiled=True), axis=0)
    share = jnp.sum(lax.all_to_all(share.reshape(rows, -1, LANES), "row", 0, 0, tiled=True), axis=0)
    share = lax.all_to_all(jnp.broadcast_to(share, (rows, *share.shape)), "row", 0, 0, tiled=True)
    share = share.reshape(-1, LANES)
    share = lax.all_to_all(jnp.broadcast_to(share, (cols, *share.shape)), "col", 0, 0, tiled=True)
    return share.reshape(value.shape)


def per_device(object_field, probe, measured, offsets, counts):
    _, layers, height, width = object_field.shape
    side = probe.shape[1]
    slots_here = measured.shape[0]

    lower_left = passed_along(object_field[:, :, :side, :side], "row", -1)
    right_rim = passed_along(object_field[:, :, :, :side], "col", -1)
    lower_right = passed_along(object_field[:, :, :side, side:], "row", -1)
    corner = passed_along(lower_left, "col", -1)
    lower = jnp.concatenate([lower_left, lower_right], axis=3)

    order = np.concatenate([np.arange(0, side, 2), np.arange(1, side, 2)])
    picks = jnp.asarray(np.eye(side, dtype=np.float32)[order])
    pattern = jnp.einsum("qab,db->qad", measured, picks, precision=lax.Precision.HIGHEST)
    pattern = jnp.einsum("ca,qad->qcd", picks, pattern, precision=lax.Precision.HIGHEST)
    tables = jnp.asarray(make_tables(side))

    f32 = jnp.float32
    vmem = pl.BlockSpec(memory_space=pltpu.VMEM)
    smem = pl.BlockSpec(memory_space=pltpu.SMEM)
    passes = 4 * 4 * 3 * slots_here
    main, right_grad, corner_grad, lower_grad, probe_terms = pl.pallas_call(
        gradient_kernel,
        in_specs=[smem, smem] + [vmem] * 7,
        out_specs=[vmem] * 5,
        out_shape=[
            jax.ShapeDtypeStruct((2, layers, height, width), f32),
            jax.ShapeDtypeStruct((2, layers, height, side), f32),
            jax.ShapeDtypeStruct((2, layers, side, side), f32),
            jax.ShapeDtypeStruct((2, layers, side, width), f32),
            jax.ShapeDtypeStruct((2, side, side), f32),
        ],
        scratch_shapes=[
            pltpu.VMEM((2, layers, height + side, width + side), f32),
            pltpu.VMEM((2, layers, height + side, width + side), f32),
        ],
        compiler_params=pltpu.CompilerParams(vmem_limit_bytes=60 * 1024 * 1024),
        cost_estimate=pl.CostEstimate(
            flops=passes * 2 * side**3, bytes_accessed=24 * 1024 * 1024, transcendentals=0
        ),
    )(offsets, counts, object_field, right_rim, lower, corner, probe, pattern, tables)

    down_right = passed_along(lower_grad[:, :, :, side:], "row", 1)
    from_corner = passed_along(corner_grad, "col", 1)
    from_left = passed_along(right_grad, "col", 1)
    down_left = passed_along(lower_grad[:, :, :, :side] + from_corner, "row", 1)
    probe_grad = sum_over_all(probe_terms)
    main = main.at[:, :, :, :side].add(from_left)
    main = main.at[:, :, :side, side:].add(down_right)
    main = main.at[:, :, :side, :side].add(down_left)
    return (main, probe_grad)


def solution(mesh):
    placed = (
        P(None, None, "row", "col"),
        P(),
        P(("row", "col"), None, None),
        P(("row", "col"), None),
        P(("row", "col")),
    )
    return jax.shard_map(
        per_device,
        mesh=mesh,
        in_specs=placed,
        out_specs=(P(None, None, "row", "col"), P()),
        check_vma=False,
    )
```

time: 719 us -> 265 us (0.37)
  the two profiles are of different devices: /device:TPU:3 before, /device:TPU:43 now
where the time goes in v1:
time: 265 us; the launch traced here: 263 us
  starting transfers between devices  95.9 us (36%)
  waiting for transfers between devices  55.4 us (21%)
  Pallas kernels  35.8 us (14%)
  blocking collectives  31.9 us (12%)
  local copies, waits for them, and re-layouts  20.5 us (8%)
  other arithmetic  17.3 us (7%)
  matrix products  5.3 us (2%)
    ppermute x8, starting transfers between devices, passed_along(): return lax.ppermute(shard, axis, pairs)  37.6 us
    pallas_call x1, Pallas kernels, per_device(): pl.pallas_call(gradient_kernel, in_specs=[smem, smem] + [vmem] * 7, out_s...  35.8 us
    all_to_all x1, starting transfers between devices, sum_over_all(): share = jnp.sum(lax.all_to_all(flat, 'col', 0, 0, tiled=True), axis=0)  32.7 us
    ppermute x8, waiting for transfers between devices, passed_along(): return lax.ppermute(shard, axis, pairs)  28.5 us
    all_to_all x1, waiting for transfers between devices, sum_over_all(): lax.all_to_all(jnp.broadcast_to(share, (cols, *share.shape)), 'col', 0, 0...  26.9 us
    all_to_all x1, starting transfers between devices, sum_over_all(): lax.all_to_all(jnp.broadcast_to(share, (cols, *share.shape)), 'col', 0, 0...  25.5 us
    all_to_all x1, blocking collectives, sum_over_all(): lax.all_to_all(share.reshape(rows, -1, LANES), 'row', 0, 0, tiled=True)  22.9 us
    scatter-add x1, local copies, waits for them, and re-layouts, per_device(): main = main.at[:, :, :side, side:].add(down_right)  11.1 us
  transfers between devices with their start and end apart: 10, of which 3 were waited for; matrix products, arithmetic and copies ran while one was open for 14% of the time, Pallas kernels for 0%

profile of v1, /device:TPU:43, one launch (start us, length us, event | category | flops | bytes accessed | tf_op | source)
XLA Modules:
  0.0 263.5 jit_solution(17273611010328469088)
XLA Ops:
  0.6 0.0 copy-start
  0.6 0.0 copy-start.1
  0.7 2.8 %fusion.6 = (f32[2,2,256,256]{3,2,1,0:T(8,128)S(1)}, f32[2,2,256,256]{3,2,1,0:T(8,128)}) fusion(f32[2,2,512,512]{3,2,1,0:T(8,128)} %obj.1), kind=kLoop, calls=%fused_computation.11 | loop fusion | bytes 4194304 | tf_op jit(solution)/shard_map/slice | solution.py:222
  3.5 0.0 copy-start.3
  3.5 0.0 copy-start.2
  3.5 2.0 collective-permute-start.1
  5.6 0.0 copy-done.1
  5.6 1.6 slice.113
  7.1 2.7 %collective-permute-start = (f32[2,2,512,256]{3,2,1,0:T(8,128)}, f32[2,2,512,256]{3,2,1,0:T(8,128)}, u32[]{:S(2)}, u32[]{:S(2)}) collective-permute-start(f32[2,2,512,256]{3,2,1,0:T(8,128)} %slice.113), channel_id=1, source_target_pairs={{1,0},{2,1},{3,2},{4,3},{5,4},{6,5},{7,6},{8,7},{9,8},{10,9},{11,1... | collective-permute-start | bytes 6291464 | tf_op jit(solution)/shard_map/ppermute | solution.py:18
  9.8 3.5 %collective-permute-start.2 = (f32[2,2,256,256]{3,2,1,0:T(8,128)}, f32[2,2,256,256]{3,2,1,0:T(8,128)}, u32[]{:S(2)}, u32[]{:S(2)}) collective-permute-start(f32[2,2,256,256]{3,2,1,0:T(8,128)} %get-tuple-element.49), channel_id=1, source_target_pairs={{16,0},{32,16},{48,32},{64,48},{80,64},{96,80},{112,96},{17,1},{33... | collective-permute-start | bytes 3145736 | tf_op jit(solution)/shard_map/ppermute | solution.py:18
  13.3 17.1 %collective-permute-done.1 = f32[2,2,256,256]{3,2,1,0:T(8,128)S(1)} collective-permute-done((f32[2,2,256,256]{3,2,1,0:T(8,128)S(1)}, f32[2,2,256,256]{3,2,1,0:T(8,128)S(1)}, u32[]{:S(2)}, u32[]{:S(2)}) %collective-permute-start.1) | collective-permute-done | bytes 1048608 | tf_op jit(solution)/shard_map/ppermute | solution.py:18
  30.4 4.6 %collective-permute-start.3 = (f32[2,2,256,256]{3,2,1,0:T(8,128)S(1)}, f32[2,2,256,256]{3,2,1,0:T(8,128)}, u32[]{:S(2)}, u32[]{:S(2)}) collective-permute-start(f32[2,2,256,256]{3,2,1,0:T(8,128)S(1)} %collective-permute-done.1), channel_id=1, source_target_pairs={{1,0},{2,1},{3,2},{4,3},{5,4},{6,5},{7,6},{8,7},{9,8},{10,9},{11,1... | collective-permute-start | bytes 3145736 | tf_op jit(solution)/shard_map/ppermute | solution.py:18
  35.0 0.0 copy-done.3
  35.1 0.7 copy.12.offsets
  36.4 0.0 copy-done
  36.4 0.0 copy-done.2
  36.4 1.9 fusion.8
  38.4 3.4 %fusion.2.measured = f32[8,256,256]{2,1,0:T(8,128)} fusion(f32[256,256,1]{1,0,2:T(8,128)S(1)} %copy-done.2, f32[256,8,256]{2,0,1:T(8,128)S(1)} %fusion.8), kind=kOutput, calls=%fused_computation.4 | convolution fusion | flops 1610612736 | bytes 4456448 | tf_op jit(solution)/shard_map/ca,qad->qcd/dot_general | solution.py:231
  41.7 11.3 %collective-permute-done.2 = f32[2,2,256,256]{3,2,1,0:T(8,128)} collective-permute-done((f32[2,2,256,256]{3,2,1,0:T(8,128)}, f32[2,2,256,256]{3,2,1,0:T(8,128)}, u32[]{:S(2)}, u32[]{:S(2)}) %collective-permute-start.2) | collective-permute-done | bytes 1048608 | tf_op jit(solution)/shard_map/ppermute | solution.py:18
  53.0 2.9 %pad_maximum_fusion.lower = f32[2,2,256,512]{3,2,1,0:T(8,128)} fusion(f32[2,2,256,256]{3,2,1,0:T(8,128)} %collective-permute-done.2, f32[2,2,256,256]{3,2,1,0:T(8,128)S(1)} %collective-permute-done.1), kind=kLoop, calls=%fused_computation | loop fusion | flops 524288 | bytes 4194304 | tf_op jit(solution)/shard_map/concatenate | solution.py:226
  55.9 0.0 collective-permute-done.3.corner
  55.9 0.0 collective-permute-done.right
  55.9 35.8 %shard_map.86 = (f32[2,2,512,512]{3,2,1,0:T(8,128)}, f32[2,2,512,256]{3,2,1,0:T(8,128)}, f32[2,2,256,256]{3,2,1,0:T(8,128)}, f32[2,2,256,512]{3,2,1,0:T(8,128)}, f32[2,256,256]{2,1,0:T(8,128)}) custom-call(s32[8,2]{1,0:T(8,128)} %copy.12.offsets, s32[1]{0:T(128)S(6)} %copy.17.counts, f32[2,2,512,512]{3,2,1,0:T(8,128)} %obj.1, ...), custom_call_target="tpu_custom_call" | custom-call | flops 12884901888 | bytes 25165824 | tf_op jit(solution)/shard_map/pallas_call | solution.py:238
  91.7 1.9 collective-permute-start.4
  93.6 1.9 collective-permute-start.6
  95.5 1.9 reshape.138
  97.4 32.7 %all-to-all-start = ((f32[16,64,128]{2,1,0:T(8,128)}), f32[16,64,128]{2,1,0:T(8,128)S(1)}, u32[]{:S(2)}, u32[]{:S(2)}) async-start(f32[16,64,128]{2,1,0:T(8,128)} %reshape.138), calls=%async_computation | async-start | bytes 1048576 | tf_op jit(solution)/shard_map/all_to_all | solution.py:209
  130.1 0.0 collective-permute-done.6
  130.1 3.4 %slice_add_fusion.1 = (f32[2,2,256,256]{3,2,1,0:T(8,128)}, f32[2,2,256,256]{3,2,1,0:T(8,128)}) fusion(f32[2,2,256,256]{3,2,1,0:T(8,128)} %collective-permute-done.6, f32[2,2,256,512]{3,2,1,0:T(8,128)} %get-tuple-element.45), kind=kLoop, calls=%fused_computation.8 | loop fusion | flops 262144 | bytes 5242880 | tf_op jit(solution)/shard_map/add | solution.py:262
  133.5 0.0 copy-start.4
  133.5 17.4 %collective-permute-start.5 = (f32[2,2,256,256]{3,2,1,0:T(8,128)}, f32[2,2,256,256]{3,2,1,0:T(8,128)}, u32[]{:S(2)}, u32[]{:S(2)}) collective-permute-start(f32[2,2,256,256]{3,2,1,0:T(8,128)} %get-tuple-element.51), channel_id=1, source_target_pairs={{0,16},{16,32},{32,48},{48,64},{64,80},{80,96},{96,112},{1,17},{17... | collective-permute-start | bytes 3145736 | tf_op jit(solution)/shard_map/ppermute | solution.py:18
  150.9 0.0 all-to-all-done
  150.9 22.9 %all_to_all.20 = f32[8,8,128]{2,1,0:T(8,128)S(1)} all-to-all(f32[8,8,128]{2,1,0:T(8,128)S(1)} %bitcast.15), channel_id=1, replica_groups=mesh['row'=8,'col'=16] {'row'}, dimensions={0} | all-to-all | bytes 65536 | tf_op jit(solution)/shard_map/all_to_all | solution.py:210
  173.9 9.0 %all_to_all.21 = f32[8,8,128]{2,1,0:T(8,128)S(1)} all-to-all(f32[8,8,128]{2,1,0:T(8,128)S(1)} %broadcast_in_dim.6), channel_id=1, replica_groups=mesh['row'=8,'col'=16] {'row'}, dimensions={0} | all-to-all | bytes 65536 | tf_op jit(solution)/shard_map/all_to_all | solution.py:211
  182.9 0.8 broadcast_in_dim.7
  183.7 25.5 %all-to-all-start.3 = ((f32[16,64,128]{2,1,0:T(8,128)}), f32[16,64,128]{2,1,0:T(8,128)S(1)}, u32[]{:S(2)}, u32[]{:S(2)}) async-start(f32[16,64,128]{2,1,0:T(8,128)} %broadcast_in_dim.7), calls=%async_computation.3 | async-start | bytes 1048576 | tf_op jit(solution)/shard_map/all_to_all | solution.py:213
  209.3 3.6 %collective-permute-start.7 = (f32[2,2,256,256]{3,2,1,0:T(8,128)}, f32[2,2,256,256]{3,2,1,0:T(8,128)}, u32[]{:S(2)}, u32[]{:S(2)}) collective-permute-start(f32[2,2,256,256]{3,2,1,0:T(8,128)} %get-tuple-element.50), channel_id=1, source_target_pairs={{0,16},{16,32},{32,48},{48,64},{64,80},{80,96},{96,112},{1,17},{17... | collective-permute-start | bytes 3145736 | tf_op jit(solution)/shard_map/ppermute | solution.py:18
  212.9 0.7 fusion.7
  213.6 0.0 copy-done.4
  213.6 0.7 and_reduce_fusion
  214.3 26.9 %all-to-all-done.3 = f32[16,64,128]{2,1,0:T(8,128)S(1)} async-done(((f32[16,64,128]{2,1,0:T(8,128)}), f32[16,64,128]{2,1,0:T(8,128)S(1)}, u32[]{:S(2)}, u32[]{:S(2)}) %all-to-all-start.3) | async-done | bytes 524320 | tf_op jit(solution)/shard_map/all_to_all | solution.py:213
  241.2 0.9 reshape.141
  242.1 0.0 collective-permute-done.4
  242.1 3.8 %add_dynamic-update-slice_fusion = f32[2,2,512,512]{3,2,1,0:T(8,128)} fusion(f32[2,2,512,512]{3,2,1,0:T(8,128)} %get-tuple-element.43, f32[2,2,512,256]{3,2,1,0:T(8,128)} %collective-permute-done.4), kind=kLoop, calls=%fused_computation.3 | loop fusion | flops 524288 | bytes 6291456 | tf_op jit(solution)/shard_map/scatter-add | solution.py:264
  246.0 0.0 collective-permute-done.5
  246.0 3.8 %add_select_fusion = f32[2,2,256,256]{3,2,1,0:T(8,128)S(1)} fusion(f32[2,2,256,256]{3,2,1,0:T(8,128)} %collective-permute-done.5, f32[2,2,512,512]{3,2,1,0:T(8,128)} %add_dynamic-update-slice_fusion, s32[]{:T(128)} %bitcast.3, s32[]{:T(128)} %bitcast.4, pred[]{:T(512)} %and_reduce_fusion), kind=kLoop, calls=%fused_computation.5 | loop fusion | flops 524288 | bytes 3145737 | tf_op jit(solution)/shard_map/select.4
  249.7 11.1 %scatter-add.11 = f32[2,2,512,512]{3,2,1,0:T(8,128)} dynamic-update-slice(f32[2,2,512,512]{3,2,1,0:T(8,128)} %add_dynamic-update-slice_fusion, f32[2,2,256,256]{3,2,1,0:T(8,128)S(1)} %add_select_fusion, s32[]{:T(128)} %constant.83.clone.1, s32[]{:T(128)} %constant.83.clone.1, s32[]{:T(128)} %bitcast.3, s32[]{:T(128)} %bitcast.4) | dynamic-update-slice | bytes 2097156 | tf_op jit(solution)/shard_map/scatter-add | solution.py:265
  260.8 0.0 collective-permute-done.7
  260.8 2.7 %fusion.5 = f32[2,2,512,512]{3,2,1,0:T(8,128)} fusion(f32[2,2,512,512]{3,2,1,0:T(8,128)} %scatter-add.11, f32[2,2,256,256]{3,2,1,0:T(8,128)} %collective-permute-done.7), kind=kLoop, calls=%fused_computation.7 | loop fusion | flops 262144 | bytes 3145728 | tf_op jit(solution)/shard_map/scatter-add | solution.py:266
  (4 shorter events, 0.1 us)
Async XLA Ops:
  0.6 35.8 %copy-start = (f32[8,256,256]{2,1,0:T(8,128)S(1)}, f32[8,256,256]{2,1,0:T(8,128)}, u32[]{:S(2)}) copy-start(f32[8,256,256]{2,1,0:T(8,128)} %param.15) | copy-start | bytes 6291460
  0.6 4.9 %copy-start.1 = (f32[2,2,512,512]{3,2,1,0:T(8,128)S(1)}, f32[2,2,512,512]{3,2,1,0:T(8,128)}, u32[]{:S(2)}) copy-start(f32[2,2,512,512]{3,2,1,0:T(8,128)} %obj.1) | copy-start | bytes 12582916
  3.5 31.5 %copy-start.3 = (s32[8,2]{0,1:T(2,128)S(1)}, s32[8,2]{0,1:T(2,128)}, u32[]{:S(2)}) copy-start(s32[8,2]{0,1:T(2,128)} %param.16) | copy-start | bytes 196
  3.5 32.9 %copy-start.2 = (f32[256,256,1]{1,0,2:T(8,128)S(1)}, f32[256,256,1]{1,0,2:T(8,128)}, u32[]{:S(2)}) copy-start(f32[256,256,1]{1,0,2:T(8,128)} %constant.94) | copy-start | bytes 786436
  3.5 26.9 %collective-permute-start.1 = (f32[2,2,256,256]{3,2,1,0:T(8,128)S(1)}, f32[2,2,256,256]{3,2,1,0:T(8,128)S(1)}, u32[]{:S(2)}, u32[]{:S(2)}) collective-permute-start(f32[2,2,256,256]{3,2,1,0:T(8,128)S(1)} %get-tuple-element.48), channel_id=1, source_target_pairs={{16,0},{32,16},{48,32},{64,48},{80,64},{96,80},{112,96},{17,1},{33... | collective-permute-start | bytes 3145736 | tf_op jit(solution)/shard_map/ppermute | solution.py:18
  7.1 48.8 %collective-permute-start = (f32[2,2,512,256]{3,2,1,0:T(8,128)}, f32[2,2,512,256]{3,2,1,0:T(8,128)}, u32[]{:S(2)}, u32[]{:S(2)}) collective-permute-start(f32[2,2,512,256]{3,2,1,0:T(8,128)} %slice.113), channel_id=1, source_target_pairs={{1,0},{2,1},{3,2},{4,3},{5,4},{6,5},{7,6},{8,7},{9,8},{10,9},{11,1... | collective-permute-start | bytes 6291464 | tf_op jit(solution)/shard_map/ppermute | solution.py:18
  9.8 43.2 %collective-permute-start.2 = (f32[2,2,256,256]{3,2,1,0:T(8,128)}, f32[2,2,256,256]{3,2,1,0:T(8,128)}, u32[]{:S(2)}, u32[]{:S(2)}) collective-permute-start(f32[2,2,256,256]{3,2,1,0:T(8,128)} %get-tuple-element.49), channel_id=1, source_target_pairs={{16,0},{32,16},{48,32},{64,48},{80,64},{96,80},{112,96},{17,1},{33... | collective-permute-start | bytes 3145736 | tf_op jit(solution)/shard_map/ppermute | solution.py:18
  30.4 25.4 %collective-permute-start.3 = (f32[2,2,256,256]{3,2,1,0:T(8,128)S(1)}, f32[2,2,256,256]{3,2,1,0:T(8,128)}, u32[]{:S(2)}, u32[]{:S(2)}) collective-permute-start(f32[2,2,256,256]{3,2,1,0:T(8,128)S(1)} %collective-permute-done.1), channel_id=1, source_target_pairs={{1,0},{2,1},{3,2},{4,3},{5,4},{6,5},{7,6},{8,7},{9,8},{10,9},{11,1... | collective-permute-start | bytes 3145736 | tf_op jit(solution)/shard_map/ppermute | solution.py:18
  91.7 150.5 %collective-permute-start.4 = (f32[2,2,512,256]{3,2,1,0:T(8,128)}, f32[2,2,512,256]{3,2,1,0:T(8,128)}, u32[]{:S(2)}, u32[]{:S(2)}) collective-permute-start(f32[2,2,512,256]{3,2,1,0:T(8,128)} %get-tuple-element.44), channel_id=1, source_target_pairs={{0,1},{1,2},{2,3},{3,4},{4,5},{5,6},{6,7},{7,8},{8,9},{9,10},{10,1... | collective-permute-start | bytes 6291464 | tf_op jit(solution)/shard_map/ppermute | solution.py:18
  93.6 36.6 %collective-permute-start.6 = (f32[2,2,256,256]{3,2,1,0:T(8,128)}, f32[2,2,256,256]{3,2,1,0:T(8,128)}, u32[]{:S(2)}, u32[]{:S(2)}) collective-permute-start(f32[2,2,256,256]{3,2,1,0:T(8,128)} %get-tuple-element.46), channel_id=1, source_target_pairs={{0,1},{1,2},{2,3},{3,4},{4,5},{5,6},{6,7},{7,8},{8,9},{9,10},{10,1... | collective-permute-start | bytes 3145736 | tf_op jit(solution)/shard_map/ppermute | solution.py:18
  97.4 53.5 %all-to-all-start = ((f32[16,64,128]{2,1,0:T(8,128)}), f32[16,64,128]{2,1,0:T(8,128)S(1)}, u32[]{:S(2)}, u32[]{:S(2)}) async-start(f32[16,64,128]{2,1,0:T(8,128)} %reshape.138), calls=%async_computation | async-start | bytes 1048576 | tf_op jit(solution)/shard_map/all_to_all | solution.py:209
  133.5 80.1 %copy-start.4 = (s32[4]{0:T(128)S(1)}, s32[4]{0:T(128)}, u32[]{:S(2)}) copy-start(s32[4]{0:T(128)} %constant.86.clone.1) | copy-start | bytes 52
  133.5 112.4 %collective-permute-start.5 = (f32[2,2,256,256]{3,2,1,0:T(8,128)}, f32[2,2,256,256]{3,2,1,0:T(8,128)}, u32[]{:S(2)}, u32[]{:S(2)}) collective-permute-start(f32[2,2,256,256]{3,2,1,0:T(8,128)} %get-tuple-element.51), channel_id=1, source_target_pairs={{0,16},{16,32},{32,48},{48,64},{64,80},{80,96},{96,112},{1,17},{17... | collective-permute-start | bytes 3145736 | tf_op jit(solution)/shard_map/ppermute | solution.py:18
  183.7 57.5 %all-to-all-start.3 = ((f32[16,64,128]{2,1,0:T(8,128)}), f32[16,64,128]{2,1,0:T(8,128)S(1)}, u32[]{:S(2)}, u32[]{:S(2)}) async-start(f32[16,64,128]{2,1,0:T(8,128)} %broadcast_in_dim.7), calls=%async_computation.3 | async-start | bytes 1048576 | tf_op jit(solution)/shard_map/all_to_all | solution.py:213
  209.3 51.5 %collective-permute-start.7 = (f32[2,2,256,256]{3,2,1,0:T(8,128)}, f32[2,2,256,256]{3,2,1,0:T(8,128)}, u32[]{:S(2)}, u32[]{:S(2)}) collective-permute-start(f32[2,2,256,256]{3,2,1,0:T(8,128)} %get-tuple-element.50), channel_id=1, source_target_pairs={{0,16},{16,32},{32,48},{48,64},{64,80},{80,96},{96,112},{1,17},{17... | collective-permute-start | bytes 3145736 | tf_op jit(solution)/shard_map/ppermute | solution.py:18

commit v2 on v1

v2 whole, which is shorter than its diff:
```python
import math

import jax
import jax.numpy as jnp
import ml_dtypes
import numpy as np
from jax import lax
from jax.experimental import pallas as pl
from jax.experimental.pallas import tpu as pltpu
from jax.sharding import PartitionSpec as P

fresnel = 40.0


def passed_along(shard, axis, by):
    length = lax.axis_size(axis)
    pairs = [(i, i + by) for i in range(length) if 0 <= i + by < length]
    return lax.ppermute(shard, axis, pairs)


def real_form(matrix):
    return np.block([[matrix.real, -matrix.imag], [matrix.imag, matrix.real]])


def make_tables(side):
    half = side // 2
    index = np.arange(side)
    dft = np.exp(-2j * np.pi * ((index[:, None] * index[None, :]) % side) / side) / math.sqrt(side)
    freqs = (index + half) % side - half
    chirp = np.exp(1j * fresnel * np.pi * (freqs * freqs) / (side * side))
    circulant = (dft.conj() * chirp[None, :]) @ dft
    near, far = circulant[:half, :half], circulant[:half, half:]
    mats = [real_form((near + far) / 2), real_form((near - far) / 2)]
    mats += [real_form(dft[0::2, :half]), real_form(dft[1::2, :half])]
    full = np.stack([mats[0], mats[1], mats[0].T, mats[1].T, mats[2], mats[3], mats[2].T, mats[3].T])
    full = full.astype(np.float32)
    high = full.astype(ml_dtypes.bfloat16)
    low = (full - high.astype(np.float32)).astype(ml_dtypes.bfloat16)
    return np.stack([high, low], axis=1)


def split(x):
    high = x.astype(jnp.bfloat16)
    return high, (x - high.astype(jnp.float32)).astype(jnp.bfloat16)


def dot(a, b):
    return jnp.dot(a, b, preferred_element_type=jnp.float32)


def fold(x):
    half = x.shape[0] // 2
    rows = (x[:half] + x[half:], x[:half] - x[half:])
    return [(r[:, :half] + r[:, half:], r[:, :half] - r[:, half:]) for r in rows]


def unfold(quads):
    (uu, uv), (vu, vv) = quads
    rows_u = jnp.concatenate([uu + uv, uu - uv], axis=1)
    rows_v = jnp.concatenate([vu + vv, vu - vv], axis=1)
    return jnp.concatenate([rows_u + rows_v, rows_u - rows_v], axis=0)


def two_sided(quads_re, quads_im, tables, left, right):
    half = quads_re[0][0].shape[0]
    lefts = []
    for p in range(2):
        z = jnp.concatenate(
            [jnp.concatenate(quads_re[p], axis=1), jnp.concatenate(quads_im[p], axis=1)], axis=0
        )
        z_hi, z_lo = split(z)
        m_hi, m_lo = tables[left + p, 0], tables[left + p, 1]
        lefts.append(
            dot(
                jnp.concatenate([m_hi, m_hi, m_lo], axis=1),
                jnp.concatenate([z_hi, z_lo, z_hi], axis=0),
            )
        )
    out_re = [[None, None], [None, None]]
    out_im = [[None, None], [None, None]]
    for q in range(2):
        cols = slice(q * half, (q + 1) * half)
        v = jnp.concatenate(
            [jnp.concatenate([w[:half, cols], w[half:, cols]], axis=1) for w in lefts], axis=0
        )
        v_hi, v_lo = split(v)
        m_hi, m_lo = tables[right + q, 0], tables[right + q, 1]
        y = dot(
            jnp.concatenate([v_hi, v_hi, v_lo], axis=1),
            jnp.concatenate([m_hi, m_lo, m_hi], axis=0),
        )
        for p in range(2):
            out_re[p][q] = y[p * half : (p + 1) * half, :half]
            out_im[p][q] = y[p * half : (p + 1) * half, half:]
    return out_re, out_im


def whole(quads):
    return jnp.concatenate([jnp.concatenate(r, axis=1) for r in quads], axis=0)


def quarters(x):
    half = x.shape[0] // 2
    return [(r[:, :half], r[:, half:]) for r in (x[:half], x[half:])]


LANES = 128
ROWS = 8
MIB = 1024 * 1024


def places(top, edge, side):
    first = pl.multiple_of(top // ROWS * ROWS, ROWS)
    start = pl.multiple_of(edge // LANES * LANES, LANES)
    return [(pl.ds(first, side + ROWS), pl.ds(pl.multiple_of(start + k * LANES, LANES), LANES)) for k in range(3)]


def iotas(rows):
    return (
        lax.broadcasted_iota(jnp.int32, (ROWS, LANES), 0),
        lax.broadcasted_iota(jnp.int32, (rows, LANES), 1),
    )


def window(ext, at, top, edge, side):
    down, over = top % ROWS, edge % LANES
    row, lane = iotas(side + ROWS)
    x = [ext[(*at, *place)] for place in places(top, edge, side)]
    blocks = [jnp.where(lane >= over, x[0], x[2]), x[1]]
    return jnp.concatenate(
        [
            jnp.concatenate([jnp.where(row >= down, y[:ROWS], y[side:]), y[ROWS:side]], axis=0)
            for y in blocks
        ],
        axis=1,
    )


def add_window(grid, at, top, edge, value):
    side = value.shape[0]
    down, over = top % ROWS, edge % LANES
    row, lane = iotas(side)
    x, y = value[:, :LANES], value[:, LANES:]
    blocks = [jnp.where(lane >= over, x, 0.0), y, jnp.where(lane < over, x, 0.0)]
    for place, block in zip(places(top, edge, side), blocks):
        low = jnp.where(row >= down, block[:ROWS], 0.0)
        high = jnp.where(row < down, block[:ROWS], 0.0)
        here = (*at, *place)
        grid[here] = grid[here] + jnp.concatenate([low, block[ROWS:], high], axis=0)


def turned(x, down, over):
    side = x.shape[0]
    tiles = side // ROWS
    row = lax.broadcasted_iota(jnp.int32, (tiles, ROWS, LANES), 1)
    lane = lax.broadcasted_iota(jnp.int32, (side, LANES), 1)
    blocks = []
    for k in range(2):
        y = pltpu.roll(x[:, k * LANES : (k + 1) * LANES].reshape(tiles, ROWS, LANES), down, 1)
        before = jnp.concatenate([y[-1:], y[:-1]], axis=0)
        blocks.append(pltpu.roll(jnp.where(row >= down, y, before).reshape(side, LANES), over, 1))
    return jnp.concatenate([jnp.where(lane >= over, blocks[k], blocks[1 - k]) for k in range(2)], axis=1)


def turned_back(x, down, over):
    side = x.shape[0]
    tiles = side // ROWS
    row = lax.broadcasted_iota(jnp.int32, (tiles, ROWS, LANES), 1)
    lane = lax.broadcasted_iota(jnp.int32, (side, LANES), 1)
    blocks = [pltpu.roll(x[:, k * LANES : (k + 1) * LANES], (LANES - over) % LANES, 1) for k in range(2)]
    out = []
    for k in range(2):
        y = jnp.where(lane < LANES - over, blocks[k], blocks[1 - k]).reshape(tiles, ROWS, LANES)
        y = pltpu.roll(y, (ROWS - down) % ROWS, 1)
        following = jnp.concatenate([y[1:], y[:1]], axis=0)
        out.append(jnp.where(row < ROWS - down, y, following).reshape(side, LANES))
    return jnp.concatenate(out, axis=1)


def gradient_kernel(
    offsets, counts, obj, right0, right1, lower, corner, middle, probe, measured, tables,
    main_out, right0_out, right1_out, low_left_out, low_right_out, corner_out, probe_out, ext, grid,
):
    height, width = obj.shape[2:]
    side = probe.shape[1]
    ext[:, :, :height, :width] = obj[...]
    ext[:, 0, :height, width:] = right0[...]
    ext[:, 1, :height, width:] = right1[...]
    ext[:, :, height:, :width] = lower[...]
    ext[:, :, height:, width:] = corner[...] + middle[...]
    grid[...] = jnp.zeros_like(grid)
    probe_out[...] = jnp.zeros_like(probe_out)

    def visit(slot, carry):
        top, edge = offsets[slot, 0], offsets[slot, 1]
        p_re, p_im = (turned(probe[i], top % ROWS, edge % LANES) for i in range(2))
        a_re, a_im = (window(ext, (i, 0), top, edge, side) for i in range(2))
        psi_re = p_re * a_re - p_im * a_im
        psi_im = p_re * a_im + p_im * a_re
        y_re, y_im = two_sided(fold(psi_re), fold(psi_im), tables, 0, 2)
        phi_re, phi_im = unfold(y_re), unfold(y_im)
        b_re, b_im = (window(ext, (i, 1), top, edge, side) for i in range(2))
        psi_re = phi_re * b_re - phi_im * b_im
        psi_im = phi_re * b_im + phi_im * b_re
        y_re, y_im = two_sided(fold(psi_re), fold(psi_im), tables, 4, 6)
        far_re, far_im = whole(y_re), whole(y_im)
        misfit = 2.0 * (far_re * far_re + far_im * far_im - measured[slot])
        y_re, y_im = two_sided(quarters(misfit * far_re), quarters(misfit * far_im), tables, 6, 4)
        d_re, d_im = unfold(y_re), unfold(y_im)
        add_window(grid, (0, 1), top, edge, phi_re * d_re + phi_im * d_im)
        add_window(grid, (1, 1), top, edge, phi_re * d_im - phi_im * d_re)
        e_re = b_re * d_re + b_im * d_im
        e_im = b_re * d_im - b_im * d_re
        y_re, y_im = two_sided(fold(e_re), fold(e_im), tables, 2, 0)
        d_re, d_im = unfold(y_re), unfold(y_im)
        add_window(grid, (0, 0), top, edge, p_re * d_re + p_im * d_im)
        add_window(grid, (1, 0), top, edge, p_re * d_im - p_im * d_re)
        probe_out[0] += turned_back(a_re * d_re + a_im * d_im, top % ROWS, edge % LANES)
        probe_out[1] += turned_back(a_re * d_im - a_im * d_re, top % ROWS, edge % LANES)
        return carry

    lax.fori_loop(0, jnp.minimum(counts[0], measured.shape[0]), visit, 0)
    main_out[...] = grid[:, :, :height, :width]
    right0_out[...] = grid[:, 0, :height, width:]
    right1_out[...] = grid[:, 1, :height, width:]
    low_left_out[...] = grid[:, :, height:, :side]
    low_right_out[...] = grid[:, :, height:, side:width]
    corner_out[...] = grid[:, :, height:, width:]


def side_kernel(held, left0, left1, out):
    for layer, left in enumerate((left0, left1)):

        @pl.when(layer == pl.program_id(1))
        def _():
            out[...] = held[...] + left[...]


def top_kernel(held, middle, low_left, low_right, out):
    side = low_right.shape[1]
    out[:, :side] = held[:, :side] + (low_left[...] + middle[...])
    out[:, side:] = held[:, side:] + low_right[...]


def order_kernel(measured, picks, out):
    def parts(x):
        high = x.astype(jnp.bfloat16)
        rest = x - high.astype(jnp.float32)
        return (high, *split(rest))

    rows = sum(dot(picks[...], x) for x in parts(measured[...]))
    out[...] = sum(
        lax.dot_general(x, picks[...], (((1,), (1,)), ((), ())), preferred_element_type=jnp.float32)
        for x in parts(rows)
    )


def add_kernel(*refs):
    *terms, out = refs
    out[...] = sum(term[...] for term in terms)


def own_kernel(mine, value, own, other):
    own[...] = value[mine[0]]
    other[...] = value[1 - mine[0]]


BESIDE = pl.CostEstimate(flops=0, bytes_accessed=400 * MIB, transcendentals=0)
SMALL = pl.CostEstimate(flops=0, bytes_accessed=1024, transcendentals=0)


def fixed(shape):
    return pl.BlockSpec(shape, lambda q: (0,) * len(shape))


def per_slot(*shape):
    return pl.BlockSpec((None, *shape), lambda q: (q,) + (0,) * len(shape))


SCALARS = pl.BlockSpec(memory_space=pltpu.SMEM)


def struct(*shape):
    return jax.ShapeDtypeStruct(shape, jnp.float32)


def moved(shard, pairs):
    cols = lax.axis_size("col")
    flat = [(a * cols + b, c * cols + d) for (a, b), (c, d) in pairs]
    return lax.ppermute(shard, ("row", "col"), flat)


def along_columns(shard, by, middle):
    rows, cols = lax.axis_size("row"), lax.axis_size("col")
    cut, end = cols // 2, 0 if by < 0 else cols - 1
    first, second = (cut, cut - 1) if by < 0 else (cut - 1, cut)
    pairs = [(c, c + by) for c in range(cols) if c not in (first, end)]
    pairs += [(first, second)] if middle == "direct" else []
    pairs = [((r, c), (r, to)) for r in range(rows) for c, to in pairs]
    pairs += [((r ^ 1, end), (r, second)) for r in range(rows)] if middle == "relay" else []
    return moved(shard, pairs)


def to_end(shard, by):
    rows, cols = lax.axis_size("row"), lax.axis_size("col")
    first, end = (cols // 2, 0) if by < 0 else (cols // 2 - 1, cols - 1)
    return moved(shard, [((r, first), (r ^ 1, end)) for r in range(rows)])


def across_middle(shard, by):
    rows, cols = lax.axis_size("row"), lax.axis_size("col")
    first, second = (cols // 2, cols // 2 - 1) if by < 0 else (cols // 2 - 1, cols // 2)
    return moved(shard, [((r, first), (r + by, second)) for r in range(rows) if 0 <= r + by < rows])


def after(first, then):
    return lax.optimization_barrier((first, then))


PHYSICAL = {"core": 2, "y": 4, "x": 4, "z_lo": 2, "z_hi": 2}


def physical(r, c):
    return {"x": r // 2, "z_lo": r % 2, "z_hi": c // 8, "y": c // 2 % 4, "core": c % 2}


def exchanged(shard, **flips):
    pairs = []
    for r in range(lax.axis_size("row")):
        for c in range(lax.axis_size("col")):
            to = physical(r, c)
            for which, flip in flips.items():
                to[which] ^= flip
            pairs.append(((r, c), (to["x"] * 2 + to["z_lo"], to["z_hi"] * 8 + to["y"] * 2 + to["core"])))
    return moved(shard, pairs)


def added(*terms):
    return pl.pallas_call(add_kernel, out_shape=struct(*terms[0].shape), cost_estimate=BESIDE)(*terms)


def halved(bit, value):
    return pl.pallas_call(
        own_kernel, in_specs=[SCALARS, pl.BlockSpec(memory_space=pltpu.VMEM)],
        out_shape=[struct(*value.shape[1:])] * 2, cost_estimate=BESIDE,
    )(bit.reshape(1), value)


def split_rows(value, bit):
    first, second = value[: value.shape[0] // 2], value[value.shape[0] // 2 :]
    return jnp.where(bit == 1, second, first), jnp.where(bit == 1, first, second)


def joined(bit, own, other):
    return jnp.concatenate([jnp.where(bit == 1, other, own), jnp.where(bit == 1, own, other)], axis=0)


def per_device(object_field, probe, measured, offsets, counts):
    _, layers, height, width = object_field.shape
    side = probe.shape[1]
    slots = measured.shape[0]
    cols = lax.axis_size("col")
    cut = cols // 2

    here = lax.axis_index("col")
    wait = lax.optimization_barrier
    lower = passed_along(object_field[:, :, :side], "row", -1)
    rim = [object_field[:, i, :, :side] for i in range(layers)]
    half = to_end(rim[1], -1)
    right0 = along_columns(rim[0], -1, "direct")
    right1 = along_columns(jnp.where(here == 0, half, rim[1]), -1, "relay")
    middle = across_middle(object_field[:, :, :side, :side], -1)
    order = np.concatenate([np.arange(0, side, 2), np.arange(1, side, 2)])
    picks = jnp.asarray(np.eye(side)[order].astype(ml_dtypes.bfloat16))
    pattern = pl.pallas_call(
        order_kernel, grid=(slots,), in_specs=[per_slot(side, side), fixed((side, side))],
        out_specs=per_slot(side, side), out_shape=struct(slots, side, side), cost_estimate=BESIDE,
    )(measured, picks)
    pattern, lower = wait((pattern, lower))
    corner = along_columns(lower[:, :, :, :side], -1, "nothing")

    vmem = pl.BlockSpec(memory_space=pltpu.VMEM)
    extended = pltpu.VMEM((2, layers, height + side, width + side), jnp.float32)
    main, rim0, rim1, low_left, low_right, corner, probe_terms = pl.pallas_call(
        gradient_kernel,
        in_specs=[SCALARS, SCALARS] + [vmem] * 9,
        out_specs=[vmem] * 7,
        out_shape=[
            struct(2, layers, height, width), struct(2, height, side), struct(2, height, side),
            *[struct(2, layers, side, side)] * 3, struct(2, side, side),
        ],
        scratch_shapes=[extended, extended],
        compiler_params=pltpu.CompilerParams(vmem_limit_bytes=60 * MIB),
        cost_estimate=BESIDE,
    )(
        offsets, counts, object_field, right0, right1, lower, corner, middle, probe, pattern,
        jnp.asarray(make_tables(side)),
    )

    me = physical(lax.axis_index("row"), lax.axis_index("col"))
    low_bit, high_bit = me["y"] % 2 ^ me["y"] // 2, me["y"] // 2
    down_right = passed_along(low_right, "row", 1)
    from_corner = along_columns(corner, 1, "nothing")
    half = to_end(rim1, 1)
    own, other = halved(me["core"], probe_terms)
    own, other = split_rows(own + exchanged(other, core=1), low_bit)
    own, other = split_rows(own + exchanged(other, y=1), high_bit)
    arrived, down_right, from_corner, half, rim0, rim1, corner = wait(
        (exchanged(other, y=3), down_right, from_corner, half, rim0, rim1, corner)
    )
    from_left0 = along_columns(rim0, 1, "direct")
    from_left1 = along_columns(jnp.where(here == cols - 1, half, rim1), 1, "relay")
    middle = across_middle(corner, 1)
    share = own + arrived
    share = share + exchanged(share, x=1)
    share = share + exchanged(share, x=3)
    share = share + exchanged(share, z_lo=1)
    arrived, from_left0, from_left1, middle, low_left = wait(
        (exchanged(share, z_lo=1, z_hi=1), from_left0, from_left1, middle, low_left + from_corner)
    )
    down_left = passed_along(low_left, "row", 1)
    share = added(share, arrived)
    share = joined(high_bit, share, exchanged(share, y=3))
    share = joined(low_bit, share, exchanged(share, y=1))
    share, down_left = wait((share, down_left))
    probe_grad = joined(me["core"], share, exchanged(share, core=1)).reshape(probe.shape)

    edge = pl.BlockSpec((None, height, side), lambda i, j: (i, 0, 0))
    corner = pl.BlockSpec((None, None, side, side), lambda i, j: (i, j, 0, 0))
    upper = pl.BlockSpec((None, None, side, width), lambda i, j: (i, j, 0, 0))
    left = pl.BlockSpec((None, None, height, side), lambda i, j: (i, j, 0, 0))
    result = pl.pallas_call(
        side_kernel, grid=(2, layers), in_specs=[left, edge, edge], out_specs=left,
        out_shape=struct(*object_field.shape), input_output_aliases={0: 0}, cost_estimate=SMALL,
    )(main, from_left0, from_left1)
    result = pl.pallas_call(
        top_kernel, grid=(2, layers), in_specs=[upper, corner, corner, corner], out_specs=upper,
        out_shape=struct(*object_field.shape), input_output_aliases={0: 0},
    )(result, middle, down_left, down_right)
    return (result, probe_grad)


def solution(mesh):
    placed = (
        P(None, None, "row", "col"),
        P(),
        P(("row", "col"), None, None),
        P(("row", "col"), None),
        P(("row", "col")),
    )
    return jax.shard_map(
        per_device,
        mesh=mesh,
        in_specs=placed,
        out_specs=(P(None, None, "row", "col"), P()),
        check_vma=False,
    )
```

time: 265 us -> 225 us (0.85)
  the two profiles are of different devices: /device:TPU:43 before, /device:TPU:3 now
where the time goes in v2:
time: 225 us; the launch traced here: 222 us
  starting transfers between devices  79 us (35%)
  waiting for transfers between devices  73.5 us (33%)
  Pallas kernels  52.7 us (23%)
  local copies, waits for them, and re-layouts  7.84 us (3%)
  other arithmetic  7.71 us (3%)
    ppermute x20, starting transfers between devices, moved(): return lax.ppermute(shard, ('row', 'col'), flat)  71.6 us
    ppermute x20, waiting for transfers between devices, moved(): return lax.ppermute(shard, ('row', 'col'), flat)  44.1 us
    pallas_call x1, Pallas kernels, per_device(): pl.pallas_call(gradient_kernel, in_specs=[SCALARS, SCALARS] + [vmem] * 9,...  32.7 us
    ppermute x3, waiting for transfers between devices, passed_along(): return lax.ppermute(shard, axis, pairs)  29.5 us
    pallas_call x1, Pallas kernels, per_device(): pl.pallas_call(order_kernel, grid=(slots,), in_specs=[per_slot(side, side...  8 us
    ppermute x3, starting transfers between devices, passed_along(): return lax.ppermute(shard, axis, pairs)  7.33 us
  transfers between devices with their start and end apart: 23, of which 11 were waited for; matrix products, arithmetic and copies ran while one was open for 5% of the time, Pallas kernels for 8%

profile of v2, /device:TPU:3, one launch (start us, length us, event | category | flops | bytes accessed | tf_op | source)
XLA Modules:
  0.0 222.3 jit_solution(180410921593256999)
XLA Ops:
  0.6 0.0 copy-start
  0.6 3.2 %slice.29 = f32[2,2,256,512]{3,2,1,0:T(8,128)} slice(f32[2,2,512,512]{3,2,1,0:T(8,128)} %obj.1), slice={[0:2], [0:2], [0:256], [0:512]} | slice | bytes 4194304 | tf_op jit(solution)/shard_map/slice | solution.py:367
  3.9 3.5 %collective-permute-start.3 = (f32[2,2,256,512]{3,2,1,0:T(8,128)}, f32[2,2,256,512]{3,2,1,0:T(8,128)S(1)}, u32[]{:S(2)}, u32[]{:S(2)}) collective-permute-start(f32[2,2,256,512]{3,2,1,0:T(8,128)} %slice.29), channel_id=1, source_target_pairs={{16,0},{32,16},{48,32},{64,48},{80,64},{96,80},{112,96},{17,1},{33... | collective-permute-start | bytes 6291464 | tf_op jit(solution)/shard_map/ppermute | solution.py:18
  7.4 1.6 slice_bitcast_fusion
  9.0 1.6 collective-permute-start.1
  10.7 2.5 %collective-permute-start = (f32[2,512,256]{2,1,0:T(8,128)}, f32[2,512,256]{2,1,0:T(8,128)S(1)}, u32[]{:S(2)}, u32[]{:S(2)}) collective-permute-start(f32[2,512,256]{2,1,0:T(8,128)} %get-tuple-element.53), channel_id=1, source_target_pairs={{1,0},{2,1},{3,2},{4,3},{5,4},{6,5},{7,6},{9,8},{10,9},{11,10},{12... | collective-permute-start | bytes 3145736 | tf_op jit(solution)/shard_map/ppermute | solution.py:290
  13.2 1.1 slice.31
  14.3 1.7 collective-permute-start.5
  16.0 8.0 %shard_map.86.measured = f32[8,256,256]{2,1,0:T(8,128)} custom-call(f32[8,256,256]{2,1,0:T(8,128)} %measured.1, bf16[256,256]{1,0:T(8,128)(2,1)} %constant.59.clone.picks), custom_call_target="tpu_custom_call" | custom-call | bytes 419430400 | tf_op jit(solution)/shard_map/pallas_call | solution.py:375
  24.0 0.0 collective-permute-done.1
  24.0 2.4 %broadcast_select_fusion.1 = f32[2,512,256]{2,1,0:T(8,128)} fusion(f32[2,512,256]{2,1,0:T(8,128)} %collective-permute-done.1, pred[]{:T(512)S(6)} %eq.26, f32[2,2,512,512]{3,2,1,0:T(8,128)} %obj.1), kind=kLoop, calls=%fused_computation.4 | loop fusion | flops 262144 | bytes 3145729 | tf_op jit(solution)/shard_map/jit(_where)/select_n | solution.py:371
  26.4 6.4 %collective-permute-start.2 = (f32[2,512,256]{2,1,0:T(8,128)}, f32[2,512,256]{2,1,0:T(8,128)}, u32[]{:S(2)}, u32[]{:S(2)}) collective-permute-start(f32[2,512,256]{2,1,0:T(8,128)} %broadcast_select_fusion.1), channel_id=1, source_target_pairs={{1,0},{2,1},{3,2},{4,3},{5,4},{6,5},{7,6},{9,8},{10,9},{11,10},{12... | collective-permute-start | bytes 3145736 | tf_op jit(solution)/shard_map/ppermute | solution.py:290
  32.8 20.1 %collective-permute-done.3.lower = f32[2,2,256,512]{3,2,1,0:T(8,128)S(1)} collective-permute-done((f32[2,2,256,512]{3,2,1,0:T(8,128)}, f32[2,2,256,512]{3,2,1,0:T(8,128)S(1)}, u32[]{:S(2)}, u32[]{:S(2)}) %collective-permute-start.3) | collective-permute-done | bytes 2097184 | tf_op jit(solution)/shard_map/ppermute | solution.py:18
  52.9 1.2 slice.30
  54.1 3.2 %collective-permute-start.4 = (f32[2,2,256,256]{3,2,1,0:T(8,128)}, f32[2,2,256,256]{3,2,1,0:T(8,128)}, u32[]{:S(2)}, u32[]{:S(2)}) collective-permute-start(f32[2,2,256,256]{3,2,1,0:T(8,128)} %slice.30), channel_id=1, source_target_pairs={{1,0},{2,1},{3,2},{4,3},{5,4},{6,5},{7,6},{9,8},{10,9},{11,10},{12... | collective-permute-start | bytes 3145736 | tf_op jit(solution)/shard_map/ppermute | solution.py:290
  57.3 0.7 copy.13.offsets
  58.7 0.0 collective-permute-done.right0
  58.7 0.0 collective-permute-done.5.middle
  58.7 0.0 collective-permute-done.2.right1
  58.7 12.6 %collective-permute-done.4.corner = f32[2,2,256,256]{3,2,1,0:T(8,128)} collective-permute-done((f32[2,2,256,256]{3,2,1,0:T(8,128)}, f32[2,2,256,256]{3,2,1,0:T(8,128)}, u32[]{:S(2)}, u32[]{:S(2)}) %collective-permute-start.4) | collective-permute-done | bytes 1048608 | tf_op jit(solution)/shard_map/ppermute | solution.py:290
  71.3 32.7 %shard_map.87 = (f32[2,2,512,512]{3,2,1,0:T(8,128)}, f32[2,512,256]{2,1,0:T(8,128)}, f32[2,512,256]{2,1,0:T(8,128)}, f32[2,2,256,256]{3,2,1,0:T(8,128)}, f32[2,2...) custom-call(s32[8,2]{1,0:T(8,128)} %copy.13.offsets, s32[1]{0:T(128)S(6)} %copy.18.counts, ...), custom_call_target="tpu_custom_call" | custom-call | bytes 419430400 | tf_op jit(solution)/shard_map/pallas_call | solution.py:384
  103.9 2.0 shard_map.88
  105.9 0.0 collective-permute-start.6
  105.9 1.9 collective-permute-start.9
  107.8 5.3 %collective-permute-start.10 = (f32[2,2,256,256]{3,2,1,0:T(8,128)}, f32[2,2,256,256]{3,2,1,0:T(8,128)S(1)}, u32[]{:S(2)}, u32[]{:S(2)}) collective-permute-start(f32[2,2,256,256]{3,2,1,0:T(8,128)} %get-tuple-element.41), channel_id=1, source_target_pairs={{0,1},{1,2},{2,3},{3,4},{4,5},{5,6},{6,7},{8,9},{9,10},{10,11},{11... | collective-permute-start | bytes 3145736 | tf_op jit(solution)/shard_map/ppermute | solution.py:290
  113.2 1.7 collective-permute-start.11
  114.9 0.0 collective-permute-done.6
  114.9 1.0 add.36
  115.9 16.8 %collective-permute-start.7 = (f32[128,256]{1,0:T(8,128)S(1)}, f32[128,256]{1,0:T(8,128)S(1)}, u32[]{:S(2)}, u32[]{:S(2)}) collective-permute-start(f32[128,256]{1,0:T(8,128)S(1)} %slice_select_fusion), channel_id=1, source_target_pairs={{0,2},{1,3},{2,0},{3,1},{4,6},{5,7},{6,4},{7,5},{8,10},{9,11},{10,... | collective-permute-start | bytes 393224 | tf_op jit(solution)/shard_map/ppermute | solution.py:290
  132.8 2.4 %collective-permute-done.7 = f32[128,256]{1,0:T(8,128)S(1)} collective-permute-done((f32[128,256]{1,0:T(8,128)S(1)}, f32[128,256]{1,0:T(8,128)S(1)}, u32[]{:S(2)}, u32[]{:S(2)}) %collective-permute-start.7) | collective-permute-done | bytes 131104 | tf_op jit(solution)/shard_map/ppermute | solution.py:290
  135.2 10.0 %collective-permute-start.8 = (f32[64,256]{1,0:T(8,128)S(1)}, f32[64,256]{1,0:T(8,128)S(1)}, u32[]{:S(2)}, u32[]{:S(2)}) collective-permute-start(f32[64,256]{1,0:T(8,128)S(1)} %slice_select_fusion.1), channel_id=1, source_target_pairs={{0,6},{1,7},{2,4},{3,5},{4,2},{5,3},{6,0},{7,1},{8,14},{9,15},{10,... | collective-permute-start | bytes 196616 | tf_op jit(solution)/shard_map/ppermute | solution.py:290
  145.2 1.7 collective-permute-done.8
  146.9 0.0 collective-permute-done.9.low_right
  146.9 0.0 collective-permute-done.10
  146.9 0.0 collective-permute-done.11
  146.9 1.9 collective-permute-start.16
  148.8 1.4 broadcast_select_fusion
  150.2 1.9 collective-permute-start.17
  152.1 1.6 collective-permute-start.18
  153.8 1.7 collective-permute-start.12
  155.5 1.7 collective-permute-done.12
  157.1 5.3 %collective-permute-start.13 = (f32[64,256]{1,0:T(8,128)S(1)}, f32[64,256]{1,0:T(8,128)S(1)}, u32[]{:S(2)}, u32[]{:S(2)}) collective-permute-start(f32[64,256]{1,0:T(8,128)S(1)} %add.39), channel_id=1, source_target_pairs={{0,96},{1,97},{2,98},{3,99},{4,100},{5,101},{6,102},{7,103},{8,104... | collective-permute-start | bytes 196616 | tf_op jit(solution)/shard_map/ppermute | solution.py:290
  162.4 1.7 collective-permute-done.13
  164.1 0.1 collective-permute-start.14
  164.2 3.8 %collective-permute-done.14 = f32[64,256]{1,0:T(8,128)S(1)} collective-permute-done((f32[64,256]{1,0:T(8,128)S(1)}, f32[64,256]{1,0:T(8,128)S(1)}, u32[]{:S(2)}, u32[]{:S(2)}) %collective-permute-start.14) | collective-permute-done | bytes 65568 | tf_op jit(solution)/shard_map/ppermute | solution.py:290
  168.0 0.0 copy-start.6
  168.0 0.9 collective-permute-start.15
  168.9 1.1 add.42
  170.0 14.2 %collective-permute-done.15.refs_1_ = f32[64,256]{1,0:T(8,128)S(1)} collective-permute-done((f32[64,256]{1,0:T(8,128)S(1)}, f32[64,256]{1,0:T(8,128)S(1)}, u32[]{:S(2)}, u32[]{:S(2)}) %collective-permute-start.15) | collective-permute-done | bytes 65568 | tf_op jit(solution)/shard_map/ppermute | solution.py:290
  184.3 0.0 collective-permute-done.16.left0
  184.3 0.0 collective-permute-done.17.left1
  184.3 0.0 collective-permute-done.18.middle
  184.3 1.9 collective-permute-start.21
  186.2 1.5 shard_map.90
  187.7 7.1 %collective-permute-start.19 = (f32[64,256]{1,0:T(8,128)}, f32[64,256]{1,0:T(8,128)S(1)}, u32[]{:S(2)}, u32[]{:S(2)}) collective-permute-start(f32[64,256]{1,0:T(8,128)} %shard_map.90), channel_id=1, source_target_pairs={{0,6},{1,7},{2,4},{3,5},{4,2},{5,3},{6,0},{7,1},{8,14},{9,15},{10,... | collective-permute-start | bytes 196616 | tf_op jit(solution)/shard_map/ppermute | solution.py:290
  194.8 2.0 collective-permute-done.19
  196.8 0.9 broadcast_select_fusion.7
  197.7 0.1 collective-permute-start.20
  197.8 4.1 %collective-permute-done.20 = f32[128,256]{1,0:T(8,128)S(1)} collective-permute-done((f32[128,256]{1,0:T(8,128)S(1)}, f32[128,256]{1,0:T(8,128)S(1)}, u32[]{:S(2)}, u32[]{:S(2)}) %collective-permute-start.20) | collective-permute-done | bytes 131104 | tf_op jit(solution)/shard_map/ppermute | solution.py:290
  202.0 9.4 %collective-permute-done.21.low_left = f32[2,2,256,256]{3,2,1,0:T(8,128)S(1)} collective-permute-done((f32[2,2,256,256]{3,2,1,0:T(8,128)}, f32[2,2,256,256]{3,2,1,0:T(8,128)S(1)}, u32[]{:S(2)}, u32[]{:S(2)}) %collective-permute-start.21) | collective-permute-done | bytes 1048608 | tf_op jit(solution)/shard_map/ppermute | solution.py:18
  211.4 1.5 collective-permute-start.22
  212.9 4.3 %shard_map.89.held = f32[2,2,512,512]{3,2,1,0:T(8,128)} custom-call(f32[2,2,512,512]{3,2,1,0:T(8,128)} %get-tuple-element.29.held, f32[2,512,256]{2,1,0:T(8,128)} %copy-done.3, f32[2,512,256]{2,1,0:T(8,128)} %collective-permute-done.17.left1), custom_call_target="tpu_custom_call", output_to_operand_aliasing={{}: (0, {})} | custom-call | bytes 1024 | tf_op jit(solution)/shard_map/pallas_call | solution.py:432
  217.1 4.3 %shard_map.91 = f32[2,2,512,512]{3,2,1,0:T(8,128)} custom-call(f32[2,2,512,512]{3,2,1,0:T(8,128)} %shard_map.89.held, f32[2,2,256,256]{3,2,1,0:T(8,128)} %collective-permute-done.18.middle, f32[2,2,256,256]{3,2,1,0:T(8,128)} %copy-done.5, f32[2,2,256,256]{3,2,1,0:T(8,128)} %collective-permute-done.9.low_right), custom_call_target="tpu_custom_call", output_to_operand_aliasing={{}: (0, {})} | custom-call | tf_op jit(solution)/shard_map/pallas_call | solution.py:436
  221.5 0.8 pad_maximum_fusion
  (28 shorter events, 0.2 us)
Async XLA Ops:
  0.6 6.8 %copy-start = (f32[2,2,512,512]{3,2,1,0:T(8,128)S(1)}, f32[2,2,512,512]{3,2,1,0:T(8,128)}, u32[]{:S(2)}) copy-start(f32[2,2,512,512]{3,2,1,0:T(8,128)} %obj.1) | copy-start | bytes 12582916
  3.9 49.0 %collective-permute-start.3 = (f32[2,2,256,512]{3,2,1,0:T(8,128)}, f32[2,2,256,512]{3,2,1,0:T(8,128)S(1)}, u32[]{:S(2)}, u32[]{:S(2)}) collective-permute-start(f32[2,2,256,512]{3,2,1,0:T(8,128)} %slice.29), channel_id=1, source_target_pairs={{16,0},{32,16},{48,32},{64,48},{80,64},{96,80},{112,96},{17,1},{33... | collective-permute-start | bytes 6291464 | tf_op jit(solution)/shard_map/ppermute | solution.py:18
  9.0 15.0 %collective-permute-start.1 = (f32[2,512,256]{2,1,0:T(8,128)}, f32[2,512,256]{2,1,0:T(8,128)}, u32[]{:S(2)}, u32[]{:S(2)}) collective-permute-start(f32[2,512,256]{2,1,0:T(8,128)} %get-tuple-element.52), channel_id=1, source_target_pairs={{8,16},{24,0},{40,48},{56,32},{72,80},{88,64},{104,112},{120,96}} | collective-permute-start | bytes 3145736 | tf_op jit(solution)/shard_map/ppermute | solution.py:290
  10.7 48.0 %collective-permute-start = (f32[2,512,256]{2,1,0:T(8,128)}, f32[2,512,256]{2,1,0:T(8,128)S(1)}, u32[]{:S(2)}, u32[]{:S(2)}) collective-permute-start(f32[2,512,256]{2,1,0:T(8,128)} %get-tuple-element.53), channel_id=1, source_target_pairs={{1,0},{2,1},{3,2},{4,3},{5,4},{6,5},{7,6},{9,8},{10,9},{11,10},{12... | collective-permute-start | bytes 3145736 | tf_op jit(solution)/shard_map/ppermute | solution.py:290
  14.3 44.4 %collective-permute-start.5 = (f32[2,2,256,256]{3,2,1,0:T(8,128)}, f32[2,2,256,256]{3,2,1,0:T(8,128)}, u32[]{:S(2)}, u32[]{:S(2)}) collective-permute-start(f32[2,2,256,256]{3,2,1,0:T(8,128)} %slice.31), channel_id=1, source_target_pairs={{24,7},{40,23},{56,39},{72,55},{88,71},{104,87},{120,103}} | collective-permute-start | bytes 3145736 | tf_op jit(solution)/shard_map/ppermute | solution.py:290
  16.0 41.3 %copy-start.8 = (s32[8,2]{0,1:T(2,128)S(1)}, s32[8,2]{0,1:T(2,128)}, u32[]{:S(2)}) copy-start(s32[8,2]{0,1:T(2,128)} %param.10) | copy-start | bytes 196
  26.4 32.3 %collective-permute-start.2 = (f32[2,512,256]{2,1,0:T(8,128)}, f32[2,512,256]{2,1,0:T(8,128)}, u32[]{:S(2)}, u32[]{:S(2)}) collective-permute-start(f32[2,512,256]{2,1,0:T(8,128)} %broadcast_select_fusion.1), channel_id=1, source_target_pairs={{1,0},{2,1},{3,2},{4,3},{5,4},{6,5},{7,6},{9,8},{10,9},{11,10},{12... | collective-permute-start | bytes 3145736 | tf_op jit(solution)/shard_map/ppermute | solution.py:290
  52.9 18.4 %copy-start.1 = (f32[2,2,256,512]{3,2,1,0:T(8,128)}, f32[2,2,256,512]{3,2,1,0:T(8,128)S(1)}, u32[]{:S(2)}) copy-start(f32[2,2,256,512]{3,2,1,0:T(8,128)S(1)} %collective-permute-done.3.lower) | copy-start | bytes 6291460
  54.1 17.2 %collective-permute-start.4 = (f32[2,2,256,256]{3,2,1,0:T(8,128)}, f32[2,2,256,256]{3,2,1,0:T(8,128)}, u32[]{:S(2)}, u32[]{:S(2)}) collective-permute-start(f32[2,2,256,256]{3,2,1,0:T(8,128)} %slice.30), channel_id=1, source_target_pairs={{1,0},{2,1},{3,2},{4,3},{5,4},{6,5},{7,6},{9,8},{10,9},{11,10},{12... | collective-permute-start | bytes 3145736 | tf_op jit(solution)/shard_map/ppermute | solution.py:290
  58.7 12.6 %copy-start.4 = (f32[2,512,256]{2,1,0:T(8,128)}, f32[2,512,256]{2,1,0:T(8,128)S(1)}, u32[]{:S(2)}) copy-start(f32[2,512,256]{2,1,0:T(8,128)S(1)} %collective-permute-done.right0) | copy-start | bytes 3145732
  103.9 65.0 %copy-start.2 = (f32[2,2,256,256]{3,2,1,0:T(8,128)S(1)}, f32[2,2,256,256]{3,2,1,0:T(8,128)}, u32[]{:S(2)}) copy-start(f32[2,2,256,256]{3,2,1,0:T(8,128)} %get-tuple-element.42) | copy-start | bytes 3145732
  105.9 9.0 %collective-permute-start.6 = (f32[256,256]{1,0:T(8,128)}, f32[256,256]{1,0:T(8,128)S(1)}, u32[]{:S(2)}, u32[]{:S(2)}) collective-permute-start(f32[256,256]{1,0:T(8,128)} %get-tuple-element.32), channel_id=1, source_target_pairs={{0,1},{1,0},{2,3},{3,2},{4,5},{5,4},{6,7},{7,6},{8,9},{9,8},{10,11... | collective-permute-start | bytes 786440 | tf_op jit(solution)/shard_map/ppermute | solution.py:290
  105.9 41.0 %collective-permute-start.9 = (f32[2,2,256,256]{3,2,1,0:T(8,128)}, f32[2,2,256,256]{3,2,1,0:T(8,128)}, u32[]{:S(2)}, u32[]{:S(2)}) collective-permute-start(f32[2,2,256,256]{3,2,1,0:T(8,128)} %get-tuple-element.33), channel_id=1, source_target_pairs={{0,16},{16,32},{32,48},{48,64},{64,80},{80,96},{96,112},{1,17},{17... | collective-permute-start | bytes 3145736 | tf_op jit(solution)/shard_map/ppermute | solution.py:18
  107.8 39.0 %collective-permute-start.10 = (f32[2,2,256,256]{3,2,1,0:T(8,128)}, f32[2,2,256,256]{3,2,1,0:T(8,128)S(1)}, u32[]{:S(2)}, u32[]{:S(2)}) collective-permute-start(f32[2,2,256,256]{3,2,1,0:T(8,128)} %get-tuple-element.41), channel_id=1, source_target_pairs={{0,1},{1,2},{2,3},{3,4},{4,5},{5,6},{6,7},{8,9},{9,10},{10,11},{11... | collective-permute-start | bytes 3145736 | tf_op jit(solution)/shard_map/ppermute | solution.py:290
  113.2 33.7 %collective-permute-start.11 = (f32[2,512,256]{2,1,0:T(8,128)}, f32[2,512,256]{2,1,0:T(8,128)}, u32[]{:S(2)}, u32[]{:S(2)}) collective-permute-start(f32[2,512,256]{2,1,0:T(8,128)} %get-tuple-element.40), channel_id=1, source_target_pairs={{7,31},{23,15},{39,63},{55,47},{71,95},{87,79},{103,127},{119,111}} | collective-permute-start | bytes 3145736 | tf_op jit(solution)/shard_map/ppermute | solution.py:290
  115.9 19.2 %collective-permute-start.7 = (f32[128,256]{1,0:T(8,128)S(1)}, f32[128,256]{1,0:T(8,128)S(1)}, u32[]{:S(2)}, u32[]{:S(2)}) collective-permute-start(f32[128,256]{1,0:T(8,128)S(1)} %slice_select_fusion), channel_id=1, source_target_pairs={{0,2},{1,3},{2,0},{3,1},{4,6},{5,7},{6,4},{7,5},{8,10},{9,11},{10,... | collective-permute-start | bytes 393224 | tf_op jit(solution)/shard_map/ppermute | solution.py:290
  135.2 11.7 %collective-permute-start.8 = (f32[64,256]{1,0:T(8,128)S(1)}, f32[64,256]{1,0:T(8,128)S(1)}, u32[]{:S(2)}, u32[]{:S(2)}) collective-permute-start(f32[64,256]{1,0:T(8,128)S(1)} %slice_select_fusion.1), channel_id=1, source_target_pairs={{0,6},{1,7},{2,4},{3,5},{4,2},{5,3},{6,0},{7,1},{8,14},{9,15},{10,... | collective-permute-start | bytes 196616 | tf_op jit(solution)/shard_map/ppermute | solution.py:290
  146.9 37.4 %collective-permute-start.16 = (f32[2,512,256]{2,1,0:T(8,128)}, f32[2,512,256]{2,1,0:T(8,128)S(1)}, u32[]{:S(2)}, u32[]{:S(2)}) collective-permute-start(f32[2,512,256]{2,1,0:T(8,128)} %get-tuple-element.38), channel_id=1, source_target_pairs={{0,1},{1,2},{2,3},{3,4},{4,5},{5,6},{6,7},{8,9},{9,10},{10,11},{11... | collective-permute-start | bytes 3145736 | tf_op jit(solution)/shard_map/ppermute | solution.py:290
  150.2 34.1 %collective-permute-start.17 = (f32[2,512,256]{2,1,0:T(8,128)S(1)}, f32[2,512,256]{2,1,0:T(8,128)}, u32[]{:S(2)}, u32[]{:S(2)}) collective-permute-start(f32[2,512,256]{2,1,0:T(8,128)S(1)} %broadcast_select_fusion), channel_id=1, source_target_pairs={{0,1},{1,2},{2,3},{3,4},{4,5},{5,6},{6,7},{8,9},{9,10},{10,11},{11... | collective-permute-start | bytes 3145736 | tf_op jit(solution)/shard_map/ppermute | solution.py:290
  152.1 32.2 %collective-permute-start.18 = (f32[2,2,256,256]{3,2,1,0:T(8,128)}, f32[2,2,256,256]{3,2,1,0:T(8,128)}, u32[]{:S(2)}, u32[]{:S(2)}) collective-permute-start(f32[2,2,256,256]{3,2,1,0:T(8,128)} %get-tuple-element.41), channel_id=1, source_target_pairs={{7,24},{23,40},{39,56},{55,72},{71,88},{87,104},{103,120}} | collective-permute-start | bytes 3145736 | tf_op jit(solution)/shard_map/ppermute | solution.py:290
  153.8 3.4 %collective-permute-start.12 = (f32[64,256]{1,0:T(8,128)S(1)}, f32[64,256]{1,0:T(8,128)S(1)}, u32[]{:S(2)}, u32[]{:S(2)}) collective-permute-start(f32[64,256]{1,0:T(8,128)S(1)} %select_add_fusion.1), channel_id=1, source_target_pairs={{0,32},{1,33},{2,34},{3,35},{4,36},{5,37},{6,38},{7,39},{8,40},{9,... | collective-permute-start | bytes 196616 | tf_op jit(solution)/shard_map/ppermute | solution.py:290
  157.1 6.9 %collective-permute-start.13 = (f32[64,256]{1,0:T(8,128)S(1)}, f32[64,256]{1,0:T(8,128)S(1)}, u32[]{:S(2)}, u32[]{:S(2)}) collective-permute-start(f32[64,256]{1,0:T(8,128)S(1)} %add.39), channel_id=1, source_target_pairs={{0,96},{1,97},{2,98},{3,99},{4,100},{5,101},{6,102},{7,103},{8,104... | collective-permute-start | bytes 196616 | tf_op jit(solution)/shard_map/ppermute | solution.py:290
  164.1 3.9 %collective-permute-start.14 = (f32[64,256]{1,0:T(8,128)S(1)}, f32[64,256]{1,0:T(8,128)S(1)}, u32[]{:S(2)}, u32[]{:S(2)}) collective-permute-start(f32[64,256]{1,0:T(8,128)S(1)} %add.40), channel_id=1, source_target_pairs={{0,16},{1,17},{2,18},{3,19},{4,20},{5,21},{6,22},{7,23},{8,24},{9,... | collective-permute-start | bytes 196616 | tf_op jit(solution)/shard_map/ppermute | solution.py:290
  168.0 18.2 %copy-start.6 = (f32[64,256]{1,0:T(8,128)}, f32[64,256]{1,0:T(8,128)S(1)}, u32[]{:S(2)}) copy-start(f32[64,256]{1,0:T(8,128)S(1)} %add.41.refs_0_) | copy-start | bytes 196612
  168.0 16.3 %collective-permute-start.15 = (f32[64,256]{1,0:T(8,128)S(1)}, f32[64,256]{1,0:T(8,128)S(1)}, u32[]{:S(2)}, u32[]{:S(2)}) collective-permute-start(f32[64,256]{1,0:T(8,128)S(1)} %add.41.refs_0_), channel_id=1, source_target_pairs={{0,24},{1,25},{2,26},{3,27},{4,28},{5,29},{6,30},{7,31},{8,16},{9,... | collective-permute-start | bytes 196616 | tf_op jit(solution)/shard_map/ppermute | solution.py:290
  184.3 2.0 copy-start.7
  184.3 28.6 %copy-start.3 = (f32[2,512,256]{2,1,0:T(8,128)}, f32[2,512,256]{2,1,0:T(8,128)S(1)}, u32[]{:S(2)}) copy-start(f32[2,512,256]{2,1,0:T(8,128)S(1)} %collective-permute-done.16.left0) | copy-start | bytes 3145732
  184.3 27.1 %collective-permute-start.21 = (f32[2,2,256,256]{3,2,1,0:T(8,128)}, f32[2,2,256,256]{3,2,1,0:T(8,128)S(1)}, u32[]{:S(2)}, u32[]{:S(2)}) collective-permute-start(f32[2,2,256,256]{3,2,1,0:T(8,128)} %add.42), channel_id=1, source_target_pairs={{0,16},{16,32},{32,48},{48,64},{64,80},{80,96},{96,112},{1,17},{17... | collective-permute-start | bytes 3145736 | tf_op jit(solution)/shard_map/ppermute | solution.py:18
  187.7 9.1 %collective-permute-start.19 = (f32[64,256]{1,0:T(8,128)}, f32[64,256]{1,0:T(8,128)S(1)}, u32[]{:S(2)}, u32[]{:S(2)}) collective-permute-start(f32[64,256]{1,0:T(8,128)} %shard_map.90), channel_id=1, source_target_pairs={{0,6},{1,7},{2,4},{3,5},{4,2},{5,3},{6,0},{7,1},{8,14},{9,15},{10,... | collective-permute-start | bytes 196616 | tf_op jit(solution)/shard_map/ppermute | solution.py:290
  197.7 4.2 %collective-permute-start.20 = (f32[128,256]{1,0:T(8,128)S(1)}, f32[128,256]{1,0:T(8,128)S(1)}, u32[]{:S(2)}, u32[]{:S(2)}) collective-permute-start(f32[128,256]{1,0:T(8,128)S(1)} %pad_maximum_fusion.2), channel_id=1, source_target_pairs={{0,2},{1,3},{2,0},{3,1},{4,6},{5,7},{6,4},{7,5},{8,10},{9,11},{10,... | collective-permute-start | bytes 393224 | tf_op jit(solution)/shard_map/ppermute | solution.py:290
  211.4 5.8 %copy-start.5 = (f32[2,2,256,256]{3,2,1,0:T(8,128)}, f32[2,2,256,256]{3,2,1,0:T(8,128)S(1)}, u32[]{:S(2)}) copy-start(f32[2,2,256,256]{3,2,1,0:T(8,128)S(1)} %collective-permute-done.21.low_left) | copy-start | bytes 3145732
  211.4 10.1 %collective-permute-start.22 = (f32[256,256]{1,0:T(8,128)S(1)}, f32[256,256]{1,0:T(8,128)S(1)}, u32[]{:S(2)}, u32[]{:S(2)}) collective-permute-start(f32[256,256]{1,0:T(8,128)S(1)} %pad_maximum_fusion.1), channel_id=1, source_target_pairs={{0,1},{1,0},{2,3},{3,2},{4,5},{5,4},{6,7},{7,6},{8,9},{9,8},{10,11... | collective-permute-start | bytes 786440 | tf_op jit(solution)/shard_map/ppermute | solution.py:290

commit v3 on v2

--- a/solution.py
+++ b/solution.py
@@ -178,7 +178,7 @@
 
 
 def gradient_kernel(
-    offsets, counts, obj, right0, right1, lower, corner, middle, probe, measured, tables,
+    offsets, counts, obj, right0, right1, low_left, low_right, corner, middle, probe, measured, tables,
     main_out, right0_out, right1_out, low_left_out, low_right_out, corner_out, probe_out, ext, grid,
 ):
     height, width = obj.shape[2:]
@@ -186,7 +186,8 @@
     ext[:, :, :height, :width] = obj[...]
     ext[:, 0, :height, width:] = right0[...]
     ext[:, 1, :height, width:] = right1[...]
-    ext[:, :, height:, :width] = lower[...]
+    ext[:, :, height:, :side] = low_left[...]
+    ext[:, :, height:, side:width] = low_right[...]
     ext[:, :, height:, width:] = corner[...] + middle[...]
     grid[...] = jnp.zeros_like(grid)
     probe_out[...] = jnp.zeros_like(probe_out)
@@ -364,7 +365,8 @@
 
     here = lax.axis_index("col")
     wait = lax.optimization_barrier
-    lower = passed_along(object_field[:, :, :side], "row", -1)
+    low_left = passed_along(object_field[:, :, :side, :side], "row", -1)
+    low_right = passed_along(object_field[:, :, :side, side:], "row", -1)
     rim = [object_field[:, i, :, :side] for i in range(layers)]
     half = to_end(rim[1], -1)
     right0 = along_columns(rim[0], -1, "direct")
@@ -376,14 +378,14 @@
         order_kernel, grid=(slots,), in_specs=[per_slot(side, side), fixed((side, side))],
         out_specs=per_slot(side, side), out_shape=struct(slots, side, side), cost_estimate=BESIDE,
     )(measured, picks)
-    pattern, lower = wait((pattern, lower))
-    corner = along_columns(lower[:, :, :, :side], -1, "nothing")
+    pattern, low_left = wait((pattern, low_left))
+    corner = along_columns(low_left, -1, "nothing")
 
     vmem = pl.BlockSpec(memory_space=pltpu.VMEM)
     extended = pltpu.VMEM((2, layers, height + side, width + side), jnp.float32)
     main, rim0, rim1, low_left, low_right, corner, probe_terms = pl.pallas_call(
         gradient_kernel,
-        in_specs=[SCALARS, SCALARS] + [vmem] * 9,
+        in_specs=[SCALARS, SCALARS] + [vmem] * 10,
         out_specs=[vmem] * 7,
         out_shape=[
             struct(2, layers, height, width), struct(2, height, side), struct(2, height, side),
@@ -393,7 +395,7 @@
         compiler_params=pltpu.CompilerParams(vmem_limit_bytes=60 * MIB),
         cost_estimate=BESIDE,
     )(
-        offsets, counts, object_field, right0, right1, lower, corner, middle, probe, pattern,
+        offsets, counts, object_field, right0, right1, low_left, low_right, corner, middle, probe, pattern,
         jnp.asarray(make_tables(side)),
     )
 
@@ -405,10 +407,8 @@
     own, other = halved(me["core"], probe_terms)
     own, other = split_rows(own + exchanged(other, core=1), low_bit)
     own, other = split_rows(own + exchanged(other, y=1), high_bit)
-    arrived, down_right, from_corner, half, rim0, rim1, corner = wait(
-        (exchanged(other, y=3), down_right, from_corner, half, rim0, rim1, corner)
-    )
     from_left0 = along_columns(rim0, 1, "direct")
+    arrived, down_right, corner = wait((exchanged(other, y=3), down_right, corner))
     from_left1 = along_columns(jnp.where(here == cols - 1, half, rim1), 1, "relay")
     middle = across_middle(corner, 1)
     share = own + arrived
@@ -422,9 +422,6 @@
     share = added(share, arrived)
     share = joined(high_bit, share, exchanged(share, y=3))
     share = joined(low_bit, share, exchanged(share, y=1))
-    share, down_left = wait((share, down_left))
-    probe_grad = joined(me["core"], share, exchanged(share, core=1)).reshape(probe.shape)
-
     edge = pl.BlockSpec((None, height, side), lambda i, j: (i, 0, 0))
     corner = pl.BlockSpec((None, None, side, side), lambda i, j: (i, j, 0, 0))
     upper = pl.BlockSpec((None, None, side, width), lambda i, j: (i, j, 0, 0))
@@ -433,6 +430,8 @@
         side_kernel, grid=(2, layers), in_specs=[left, edge, edge], out_specs=left,
         out_shape=struct(*object_field.shape), input_output_aliases={0: 0}, cost_estimate=SMALL,
     )(main, from_left0, from_left1)
+    share, down_left, result = wait((share, down_left, result))
+    probe_grad = joined(me["core"], share, exchanged(share, core=1)).reshape(probe.shape)
     result = pl.pallas_call(
         top_kernel, grid=(2, layers), in_specs=[upper, corner, corner, corner], out_specs=upper,
         out_shape=struct(*object_field.shape), input_output_aliases={0: 0},

time: 225 us -> 200 us (0.89); the launches traced: 222 us -> 202 us
  waiting for transfers between devices: 73.5 us -> 52.6 us
  Pallas kernels: 52.7 us -> 56.5 us
    ppermute x20, waiting for transfers between devices: 44.1 us -> 19.4 us  [moved(): return lax.ppermute(shard, ('row', 'col'), flat)]
    ppermute x20, starting transfers between devices: 71.6 us -> 61.9 us  [moved(): return lax.ppermute(shard, ('row', 'col'), flat)]
    ppermute x3 -> x4, starting transfers between devices: 7.33 us -> 15.2 us  [passed_along(): return lax.ppermute(shard, axis, pairs)]
    slice x3 -> x1, local copies, waits for them, and re-layouts: 5.52 us -> 1.49 us  [per_device(): low_right = passed_along(object_field[:, :, :side, side:], 'row', -1)]
    pallas_call x1, Pallas kernels: 32.7 us -> 36.5 us  [per_device(): pl.pallas_call(gradient_kernel, in_specs=[SCALARS, SCALARS] + [vmem] * 10...]
    ppermute x3 -> x4, waiting for transfers between devices: 29.5 us -> 33.1 us  [passed_along(): return lax.ppermute(shard, axis, pairs)]
  transfers between devices with their start and end apart: 23 -> 24, of which waited for: 11 -> 10; matrix products, arithmetic and copies ran while one was open for 5% -> 4% of each run, Pallas kernels for 8% -> 9%
where the time goes in v3:
time: 200 us; the launch traced here: 202 us
  starting transfers between devices  77.1 us (39%)
  Pallas kernels  56.5 us (28%)
  waiting for transfers between devices  52.6 us (26%)
  other arithmetic  7.67 us (4%)
  local copies, waits for them, and re-layouts  6.39 us (3%)
    ppermute x20, starting transfers between devices, moved(): return lax.ppermute(shard, ('row', 'col'), flat)  61.9 us
    pallas_call x1, Pallas kernels, per_device(): pl.pallas_call(gradient_kernel, in_specs=[SCALARS, SCALARS] + [vmem] * 10...  36.5 us
    ppermute x4, waiting for transfers between devices, passed_along(): return lax.ppermute(shard, axis, pairs)  33.1 us
    ppermute x20, waiting for transfers between devices, moved(): return lax.ppermute(shard, ('row', 'col'), flat)  19.4 us
    ppermute x4, starting transfers between devices, passed_along(): return lax.ppermute(shard, axis, pairs)  15.2 us
    pallas_call x1, Pallas kernels, per_device(): pl.pallas_call(order_kernel, grid=(slots,), in_specs=[per_slot(side, side...  7.99 us
    pallas_call x1, Pallas kernels, per_device(): pl.pallas_call(top_kernel, grid=(2, layers), in_specs=[upper, corner, cor...  4.32 us
    pallas_call x1, Pallas kernels, per_device(): pl.pallas_call(side_kernel, grid=(2, layers), in_specs=[left, edge, edge]...  4.3 us
  transfers between devices with their start and end apart: 24, of which 10 were waited for; matrix products, arithmetic and copies ran while one was open for 4% of the time, Pallas kernels for 9%

profile of v3, /device:TPU:3, one launch (start us, length us, event | category | flops | bytes accessed | tf_op | source)
XLA Modules:
  0.0 202.0 jit_solution(18295909660941199148)
XLA Ops:
  0.6 0.0 copy-start
  0.6 3.2 %slice_bitcast_fusion = (f32[2,512,256]{2,1,0:T(8,128)}, f32[2,512,256]{2,1,0:T(8,128)}) fusion(f32[2,2,512,512]{3,2,1,0:T(8,128)} %obj.1), kind=kLoop, calls=%fused_computation | loop fusion | bytes 4194304 | tf_op jit(solution)/shard_map/squeeze | solution.py:370
  3.8 1.6 collective-permute-start.1
  5.5 1.5 fusion
  7.0 3.6 %collective-permute-start.3 = (f32[2,2,256,256]{3,2,1,0:T(8,128)}, f32[2,2,256,256]{3,2,1,0:T(8,128)S(1)}, u32[]{:S(2)}, u32[]{:S(2)}) collective-permute-start(f32[2,2,256,256]{3,2,1,0:T(8,128)} %get-tuple-element.47), channel_id=1, source_target_pairs={{16,0},{32,16},{48,32},{64,48},{80,64},{96,80},{112,96},{17,1},{33... | collective-permute-start | bytes 3145736 | tf_op jit(solution)/shard_map/ppermute | solution.py:18
  10.6 0.7 collective-permute-start.6
  11.3 2.5 %collective-permute-start = (f32[2,512,256]{2,1,0:T(8,128)}, f32[2,512,256]{2,1,0:T(8,128)S(1)}, u32[]{:S(2)}, u32[]{:S(2)}) collective-permute-start(f32[2,512,256]{2,1,0:T(8,128)} %get-tuple-element.49), channel_id=1, source_target_pairs={{1,0},{2,1},{3,2},{4,3},{5,4},{6,5},{7,6},{9,8},{10,9},{11,10},{12... | collective-permute-start | bytes 3145736 | tf_op jit(solution)/shard_map/ppermute | solution.py:291
  13.9 1.9 collective-permute-start.4
  15.8 8.0 %shard_map.86.measured = f32[8,256,256]{2,1,0:T(8,128)} custom-call(f32[8,256,256]{2,1,0:T(8,128)} %measured.1, bf16[256,256]{1,0:T(8,128)(2,1)} %constant.59.clone.picks), custom_call_target="tpu_custom_call" | custom-call | bytes 419430400 | tf_op jit(solution)/shard_map/pallas_call | solution.py:377
  23.8 0.0 collective-permute-done.1
  23.8 2.4 %broadcast_select_fusion.1 = f32[2,512,256]{2,1,0:T(8,128)} fusion(f32[2,512,256]{2,1,0:T(8,128)} %collective-permute-done.1, pred[]{:T(512)S(6)} %eq.28, f32[2,2,512,512]{3,2,1,0:T(8,128)} %obj.1), kind=kLoop, calls=%fused_computation.4 | loop fusion | flops 262144 | bytes 3145729 | tf_op jit(solution)/shard_map/jit(_where)/select_n | solution.py:373
  26.2 1.9 collective-permute-start.2
  28.1 5.9 %collective-permute-done.3.low_left = f32[2,2,256,256]{3,2,1,0:T(8,128)S(1)} collective-permute-done((f32[2,2,256,256]{3,2,1,0:T(8,128)}, f32[2,2,256,256]{3,2,1,0:T(8,128)S(1)}, u32[]{:S(2)}, u32[]{:S(2)}) %collective-permute-start.3) | collective-permute-done | bytes 1048608 | tf_op jit(solution)/shard_map/ppermute | solution.py:18
  34.0 3.4 %collective-permute-start.5 = (f32[2,2,256,256]{3,2,1,0:T(8,128)S(1)}, f32[2,2,256,256]{3,2,1,0:T(8,128)}, u32[]{:S(2)}, u32[]{:S(2)}) collective-permute-start(f32[2,2,256,256]{3,2,1,0:T(8,128)S(1)} %collective-permute-done.3.low_left), channel_id=1, source_target_pairs={{1,0},{2,1},{3,2},{4,3},{5,4},{6,5},{7,6},{9,8},{10,9},{11,10},{12... | collective-permute-start | bytes 3145736 | tf_op jit(solution)/shard_map/ppermute | solution.py:291
  37.4 0.7 copy.13.offsets
  38.8 0.0 collective-permute-done.6.middle
  38.8 0.0 collective-permute-done.right0
  38.8 17.8 %collective-permute-done.4.low_right = f32[2,2,256,256]{3,2,1,0:T(8,128)} collective-permute-done((f32[2,2,256,256]{3,2,1,0:T(8,128)}, f32[2,2,256,256]{3,2,1,0:T(8,128)}, u32[]{:S(2)}, u32[]{:S(2)}) %collective-permute-start.4) | collective-permute-done | bytes 1048608 | tf_op jit(solution)/shard_map/ppermute | solution.py:18
  56.6 0.0 collective-permute-done.2.right1
  56.6 0.0 collective-permute-done.5.corner
  56.6 36.5 %shard_map.87 = (f32[2,2,512,512]{3,2,1,0:T(8,128)}, f32[2,512,256]{2,1,0:T(8,128)}, f32[2,512,256]{2,1,0:T(8,128)}, f32[2,2,256,256]{3,2,1,0:T(8,128)}, f32[2,2...) custom-call(s32[8,2]{1,0:T(8,128)} %copy.13.offsets, s32[1]{0:T(128)S(6)} %copy.18.counts, ...), custom_call_target="tpu_custom_call" | custom-call | bytes 419430400 | tf_op jit(solution)/shard_map/pallas_call | solution.py:386
  93.1 2.0 shard_map.88
  95.0 0.0 collective-permute-start.7
  95.0 7.7 %collective-permute-start.10 = (f32[2,2,256,256]{3,2,1,0:T(8,128)}, f32[2,2,256,256]{3,2,1,0:T(8,128)}, u32[]{:S(2)}, u32[]{:S(2)}) collective-permute-start(f32[2,2,256,256]{3,2,1,0:T(8,128)} %get-tuple-element.29), channel_id=1, source_target_pairs={{0,16},{16,32},{32,48},{48,64},{64,80},{80,96},{96,112},{1,17},{17... | collective-permute-start | bytes 3145736 | tf_op jit(solution)/shard_map/ppermute | solution.py:18
  102.8 0.7 collective-permute-start.16
  103.5 0.0 collective-permute-done.7
  103.6 1.0 add.36
  104.6 0.2 collective-permute-start.8
  104.8 4.2 %collective-permute-done.8 = f32[128,256]{1,0:T(8,128)S(1)} collective-permute-done((f32[128,256]{1,0:T(8,128)S(1)}, f32[128,256]{1,0:T(8,128)S(1)}, u32[]{:S(2)}, u32[]{:S(2)}) %collective-permute-start.8) | collective-permute-done | bytes 131104 | tf_op jit(solution)/shard_map/ppermute | solution.py:291
  109.0 18.5 %collective-permute-start.9 = (f32[64,256]{1,0:T(8,128)S(1)}, f32[64,256]{1,0:T(8,128)S(1)}, u32[]{:S(2)}, u32[]{:S(2)}) collective-permute-start(f32[64,256]{1,0:T(8,128)S(1)} %slice_select_fusion.1), channel_id=1, source_target_pairs={{0,6},{1,7},{2,4},{3,5},{4,2},{5,3},{6,0},{7,1},{8,14},{9,15},{10,... | collective-permute-start | bytes 196616 | tf_op jit(solution)/shard_map/ppermute | solution.py:291
  127.5 1.9 collective-permute-start.19
  129.4 1.9 collective-permute-start.15
  131.3 0.0 collective-permute-done.9
  131.3 0.0 collective-permute-done.10.low_right
  131.4 0.7 collective-permute-start.18
  132.1 0.0 collective-permute-done.16
  132.1 1.4 broadcast_select_fusion
  133.5 1.9 collective-permute-start.17
  135.4 0.1 collective-permute-start.11
  135.5 3.1 %collective-permute-done.11 = f32[64,256]{1,0:T(8,128)S(1)} collective-permute-done((f32[64,256]{1,0:T(8,128)S(1)}, f32[64,256]{1,0:T(8,128)S(1)}, u32[]{:S(2)}, u32[]{:S(2)}) %collective-permute-start.11) | collective-permute-done | bytes 65568 | tf_op jit(solution)/shard_map/ppermute | solution.py:291
  138.6 1.2 collective-permute-start.12
  139.9 1.9 collective-permute-done.12
  141.8 0.9 collective-permute-start.13
  142.8 6.2 %collective-permute-done.13 = f32[64,256]{1,0:T(8,128)S(1)} collective-permute-done((f32[64,256]{1,0:T(8,128)S(1)}, f32[64,256]{1,0:T(8,128)S(1)}, u32[]{:S(2)}, u32[]{:S(2)}) %collective-permute-start.13) | collective-permute-done | bytes 65568 | tf_op jit(solution)/shard_map/ppermute | solution.py:291
  149.0 0.0 copy-start.8
  149.0 16.2 %collective-permute-start.14 = (f32[64,256]{1,0:T(8,128)S(1)}, f32[64,256]{1,0:T(8,128)S(1)}, u32[]{:S(2)}, u32[]{:S(2)}) collective-permute-start(f32[64,256]{1,0:T(8,128)S(1)} %add.41.refs_0_), channel_id=1, source_target_pairs={{0,24},{1,25},{2,26},{3,27},{4,28},{5,29},{6,30},{7,31},{8,16},{9,... | collective-permute-start | bytes 196616 | tf_op jit(solution)/shard_map/ppermute | solution.py:291
  165.1 0.0 collective-permute-done.19
  165.1 1.1 add.42
  166.2 0.9 collective-permute-done.14.refs_1_
  167.2 0.0 collective-permute-done.18.middle
  167.2 1.0 copy-done.7
  168.2 1.9 collective-permute-start.22
  170.1 1.5 shard_map.89
  171.6 5.4 %collective-permute-start.20 = (f32[64,256]{1,0:T(8,128)}, f32[64,256]{1,0:T(8,128)S(1)}, u32[]{:S(2)}, u32[]{:S(2)}) collective-permute-start(f32[64,256]{1,0:T(8,128)} %shard_map.89), channel_id=1, source_target_pairs={{0,6},{1,7},{2,4},{3,5},{4,2},{5,3},{6,0},{7,1},{8,14},{9,15},{10,... | collective-permute-start | bytes 196616 | tf_op jit(solution)/shard_map/ppermute | solution.py:291
  177.0 2.1 %collective-permute-done.20 = f32[64,256]{1,0:T(8,128)S(1)} collective-permute-done((f32[64,256]{1,0:T(8,128)}, f32[64,256]{1,0:T(8,128)S(1)}, u32[]{:S(2)}, u32[]{:S(2)}) %collective-permute-start.20) | collective-permute-done | bytes 65568 | tf_op jit(solution)/shard_map/ppermute | solution.py:291
  179.1 0.9 broadcast_select_fusion.7
  180.0 0.1 collective-permute-start.21
  180.1 4.3 %shard_map.90.held = f32[2,2,512,512]{3,2,1,0:T(8,128)} custom-call(f32[2,2,512,512]{3,2,1,0:T(8,128)} %get-tuple-element.38.held, f32[2,512,256]{2,1,0:T(8,128)} %copy-done.2, f32[2,512,256]{2,1,0:T(8,128)} %copy-done.4), custom_call_target="tpu_custom_call", output_to_operand_aliasing={{}: (0, {})} | custom-call | bytes 1024 | tf_op jit(solution)/shard_map/pallas_call | solution.py:429
  184.4 1.0 collective-permute-done.21
  185.4 9.5 %collective-permute-done.22.low_left = f32[2,2,256,256]{3,2,1,0:T(8,128)} collective-permute-done((f32[2,2,256,256]{3,2,1,0:T(8,128)}, f32[2,2,256,256]{3,2,1,0:T(8,128)}, u32[]{:S(2)}, u32[]{:S(2)}) %collective-permute-start.22) | collective-permute-done | bytes 1048608 | tf_op jit(solution)/shard_map/ppermute | solution.py:18
  194.9 1.9 collective-permute-start.23
  196.8 4.3 %shard_map.91 = f32[2,2,512,512]{3,2,1,0:T(8,128)} custom-call(f32[2,2,512,512]{3,2,1,0:T(8,128)} %shard_map.90.held, f32[2,2,256,256]{3,2,1,0:T(8,128)} %copy-done.7, f32[2,2,256,256]{3,2,1,0:T(8,128)} %collective-permute-done.22.low_left, f32[2,2,256,256]{3,2,1,0:T(8,128)} %collective-permute-done.10.low_right), custom_call_target="tpu_custom_call", output_to_operand_aliasing={{}: (0, {})} | custom-call | tf_op jit(solution)/shard_map/pallas_call | solution.py:435
  201.2 0.0 collective-permute-done.23
  201.2 0.8 pad_maximum_fusion
  (32 shorter events, 0.2 us)
Async XLA Ops:
  0.6 4.8 %copy-start = (f32[2,2,512,512]{3,2,1,0:T(8,128)S(1)}, f32[2,2,512,512]{3,2,1,0:T(8,128)}, u32[]{:S(2)}) copy-start(f32[2,2,512,512]{3,2,1,0:T(8,128)} %obj.1) | copy-start | bytes 12582916
  3.8 20.0 %collective-permute-start.1 = (f32[2,512,256]{2,1,0:T(8,128)}, f32[2,512,256]{2,1,0:T(8,128)}, u32[]{:S(2)}, u32[]{:S(2)}) collective-permute-start(f32[2,512,256]{2,1,0:T(8,128)} %get-tuple-element.48), channel_id=1, source_target_pairs={{8,16},{24,0},{40,48},{56,32},{72,80},{88,64},{104,112},{120,96}} | collective-permute-start | bytes 3145736 | tf_op jit(solution)/shard_map/ppermute | solution.py:291
  7.0 30.5 %copy-start.10 = (s32[8,2]{0,1:T(2,128)S(1)}, s32[8,2]{0,1:T(2,128)}, u32[]{:S(2)}) copy-start(s32[8,2]{0,1:T(2,128)} %param.10) | copy-start | bytes 196
  7.0 27.0 %collective-permute-start.3 = (f32[2,2,256,256]{3,2,1,0:T(8,128)}, f32[2,2,256,256]{3,2,1,0:T(8,128)S(1)}, u32[]{:S(2)}, u32[]{:S(2)}) collective-permute-start(f32[2,2,256,256]{3,2,1,0:T(8,128)} %get-tuple-element.47), channel_id=1, source_target_pairs={{16,0},{32,16},{48,32},{64,48},{80,64},{96,80},{112,96},{17,1},{33... | collective-permute-start | bytes 3145736 | tf_op jit(solution)/shard_map/ppermute | solution.py:18
  10.6 28.2 %collective-permute-start.6 = (f32[2,2,256,256]{3,2,1,0:T(8,128)}, f32[2,2,256,256]{3,2,1,0:T(8,128)S(1)}, u32[]{:S(2)}, u32[]{:S(2)}) collective-permute-start(f32[2,2,256,256]{3,2,1,0:T(8,128)} %get-tuple-element.47), channel_id=1, source_target_pairs={{24,7},{40,23},{56,39},{72,55},{88,71},{104,87},{120,103}} | collective-permute-start | bytes 3145736 | tf_op jit(solution)/shard_map/ppermute | solution.py:291
  11.3 27.4 %collective-permute-start = (f32[2,512,256]{2,1,0:T(8,128)}, f32[2,512,256]{2,1,0:T(8,128)S(1)}, u32[]{:S(2)}, u32[]{:S(2)}) collective-permute-start(f32[2,512,256]{2,1,0:T(8,128)} %get-tuple-element.49), channel_id=1, source_target_pairs={{1,0},{2,1},{3,2},{4,3},{5,4},{6,5},{7,6},{9,8},{10,9},{11,10},{12... | collective-permute-start | bytes 3145736 | tf_op jit(solution)/shard_map/ppermute | solution.py:291
  13.9 42.7 %collective-permute-start.4 = (f32[2,2,256,256]{3,2,1,0:T(8,128)}, f32[2,2,256,256]{3,2,1,0:T(8,128)}, u32[]{:S(2)}, u32[]{:S(2)}) collective-permute-start(f32[2,2,256,256]{3,2,1,0:T(8,128)} %get-tuple-element.46), channel_id=1, source_target_pairs={{16,0},{32,16},{48,32},{64,48},{80,64},{96,80},{112,96},{17,1},{33... | collective-permute-start | bytes 3145736 | tf_op jit(solution)/shard_map/ppermute | solution.py:18
  26.2 30.4 %collective-permute-start.2 = (f32[2,512,256]{2,1,0:T(8,128)}, f32[2,512,256]{2,1,0:T(8,128)}, u32[]{:S(2)}, u32[]{:S(2)}) collective-permute-start(f32[2,512,256]{2,1,0:T(8,128)} %broadcast_select_fusion.1), channel_id=1, source_target_pairs={{1,0},{2,1},{3,2},{4,3},{5,4},{6,5},{7,6},{9,8},{10,9},{11,10},{12... | collective-permute-start | bytes 3145736 | tf_op jit(solution)/shard_map/ppermute | solution.py:291
  34.0 22.6 %copy-start.3 = (f32[2,2,256,256]{3,2,1,0:T(8,128)}, f32[2,2,256,256]{3,2,1,0:T(8,128)S(1)}, u32[]{:S(2)}) copy-start(f32[2,2,256,256]{3,2,1,0:T(8,128)S(1)} %collective-permute-done.3.low_left) | copy-start | bytes 3145732
  34.0 22.6 %collective-permute-start.5 = (f32[2,2,256,256]{3,2,1,0:T(8,128)S(1)}, f32[2,2,256,256]{3,2,1,0:T(8,128)}, u32[]{:S(2)}, u32[]{:S(2)}) collective-permute-start(f32[2,2,256,256]{3,2,1,0:T(8,128)S(1)} %collective-permute-done.3.low_left), channel_id=1, source_target_pairs={{1,0},{2,1},{3,2},{4,3},{5,4},{6,5},{7,6},{9,8},{10,9},{11,10},{12... | collective-permute-start | bytes 3145736 | tf_op jit(solution)/shard_map/ppermute | solution.py:291
  38.8 17.8 %copy-start.5 = (f32[2,2,256,256]{3,2,1,0:T(8,128)}, f32[2,2,256,256]{3,2,1,0:T(8,128)S(1)}, u32[]{:S(2)}) copy-start(f32[2,2,256,256]{3,2,1,0:T(8,128)S(1)} %collective-permute-done.6.middle) | copy-start | bytes 3145732
  38.8 17.8 %copy-start.6 = (f32[2,512,256]{2,1,0:T(8,128)}, f32[2,512,256]{2,1,0:T(8,128)S(1)}, u32[]{:S(2)}) copy-start(f32[2,512,256]{2,1,0:T(8,128)S(1)} %collective-permute-done.right0) | copy-start | bytes 3145732
  93.1 72.1 %copy-start.1 = (f32[2,2,256,256]{3,2,1,0:T(8,128)S(1)}, f32[2,2,256,256]{3,2,1,0:T(8,128)}, u32[]{:S(2)}) copy-start(f32[2,2,256,256]{3,2,1,0:T(8,128)} %get-tuple-element.35) | copy-start | bytes 3145732
  95.0 8.5 %collective-permute-start.7 = (f32[256,256]{1,0:T(8,128)}, f32[256,256]{1,0:T(8,128)S(1)}, u32[]{:S(2)}, u32[]{:S(2)}) collective-permute-start(f32[256,256]{1,0:T(8,128)} %get-tuple-element.28), channel_id=1, source_target_pairs={{0,1},{1,0},{2,3},{3,2},{4,5},{5,4},{6,7},{7,6},{8,9},{9,8},{10,11... | collective-permute-start | bytes 786440 | tf_op jit(solution)/shard_map/ppermute | solution.py:291
  95.0 36.3 %collective-permute-start.10 = (f32[2,2,256,256]{3,2,1,0:T(8,128)}, f32[2,2,256,256]{3,2,1,0:T(8,128)}, u32[]{:S(2)}, u32[]{:S(2)}) collective-permute-start(f32[2,2,256,256]{3,2,1,0:T(8,128)} %get-tuple-element.29), channel_id=1, source_target_pairs={{0,16},{16,32},{32,48},{48,64},{64,80},{80,96},{96,112},{1,17},{17... | collective-permute-start | bytes 3145736 | tf_op jit(solution)/shard_map/ppermute | solution.py:18
  102.8 29.3 %collective-permute-start.16 = (f32[2,512,256]{2,1,0:T(8,128)}, f32[2,512,256]{2,1,0:T(8,128)S(1)}, u32[]{:S(2)}, u32[]{:S(2)}) collective-permute-start(f32[2,512,256]{2,1,0:T(8,128)} %get-tuple-element.33), channel_id=1, source_target_pairs={{7,31},{23,15},{39,63},{55,47},{71,95},{87,79},{103,127},{119,111}} | collective-permute-start | bytes 3145736 | tf_op jit(solution)/shard_map/ppermute | solution.py:291
  104.6 4.4 %collective-permute-start.8 = (f32[128,256]{1,0:T(8,128)S(1)}, f32[128,256]{1,0:T(8,128)S(1)}, u32[]{:S(2)}, u32[]{:S(2)}) collective-permute-start(f32[128,256]{1,0:T(8,128)S(1)} %slice_select_fusion), channel_id=1, source_target_pairs={{0,2},{1,3},{2,0},{3,1},{4,6},{5,7},{6,4},{7,5},{8,10},{9,11},{10,... | collective-permute-start | bytes 393224 | tf_op jit(solution)/shard_map/ppermute | solution.py:291
  109.0 22.3 %collective-permute-start.9 = (f32[64,256]{1,0:T(8,128)S(1)}, f32[64,256]{1,0:T(8,128)S(1)}, u32[]{:S(2)}, u32[]{:S(2)}) collective-permute-start(f32[64,256]{1,0:T(8,128)S(1)} %slice_select_fusion.1), channel_id=1, source_target_pairs={{0,6},{1,7},{2,4},{3,5},{4,2},{5,3},{6,0},{7,1},{8,14},{9,15},{10,... | collective-permute-start | bytes 196616 | tf_op jit(solution)/shard_map/ppermute | solution.py:291
  127.5 37.6 %collective-permute-start.19 = (f32[2,2,256,256]{3,2,1,0:T(8,128)}, f32[2,2,256,256]{3,2,1,0:T(8,128)S(1)}, u32[]{:S(2)}, u32[]{:S(2)}) collective-permute-start(f32[2,2,256,256]{3,2,1,0:T(8,128)} %get-tuple-element.34), channel_id=1, source_target_pairs={{0,1},{1,2},{2,3},{3,4},{4,5},{5,6},{6,7},{8,9},{9,10},{10,11},{11... | collective-permute-start | bytes 3145736 | tf_op jit(solution)/shard_map/ppermute | solution.py:291
  129.4 36.8 %collective-permute-start.15 = (f32[2,512,256]{2,1,0:T(8,128)}, f32[2,512,256]{2,1,0:T(8,128)S(1)}, u32[]{:S(2)}, u32[]{:S(2)}) collective-permute-start(f32[2,512,256]{2,1,0:T(8,128)} %get-tuple-element.32), channel_id=1, source_target_pairs={{0,1},{1,2},{2,3},{3,4},{4,5},{5,6},{6,7},{8,9},{9,10},{10,11},{11... | collective-permute-start | bytes 3145736 | tf_op jit(solution)/shard_map/ppermute | solution.py:291
  131.4 35.8 %collective-permute-start.18 = (f32[2,2,256,256]{3,2,1,0:T(8,128)}, f32[2,2,256,256]{3,2,1,0:T(8,128)S(1)}, u32[]{:S(2)}, u32[]{:S(2)}) collective-permute-start(f32[2,2,256,256]{3,2,1,0:T(8,128)} %get-tuple-element.34), channel_id=1, source_target_pairs={{7,24},{23,40},{39,56},{55,72},{71,88},{87,104},{103,120}} | collective-permute-start | bytes 3145736 | tf_op jit(solution)/shard_map/ppermute | solution.py:291
  133.5 33.7 %collective-permute-start.17 = (f32[2,512,256]{2,1,0:T(8,128)S(1)}, f32[2,512,256]{2,1,0:T(8,128)S(1)}, u32[]{:S(2)}, u32[]{:S(2)}) collective-permute-start(f32[2,512,256]{2,1,0:T(8,128)S(1)} %broadcast_select_fusion), channel_id=1, source_target_pairs={{0,1},{1,2},{2,3},{3,4},{4,5},{5,6},{6,7},{8,9},{9,10},{10,11},{11... | collective-permute-start | bytes 3145736 | tf_op jit(solution)/shard_map/ppermute | solution.py:291
  135.4 3.2 %collective-permute-start.11 = (f32[64,256]{1,0:T(8,128)S(1)}, f32[64,256]{1,0:T(8,128)S(1)}, u32[]{:S(2)}, u32[]{:S(2)}) collective-permute-start(f32[64,256]{1,0:T(8,128)S(1)} %select_add_fusion.1), channel_id=1, source_target_pairs={{0,32},{1,33},{2,34},{3,35},{4,36},{5,37},{6,38},{7,39},{8,40},{9,... | collective-permute-start | bytes 196616 | tf_op jit(solution)/shard_map/ppermute | solution.py:291
  138.6 3.2 %collective-permute-start.12 = (f32[64,256]{1,0:T(8,128)S(1)}, f32[64,256]{1,0:T(8,128)S(1)}, u32[]{:S(2)}, u32[]{:S(2)}) collective-permute-start(f32[64,256]{1,0:T(8,128)S(1)} %add.39), channel_id=1, source_target_pairs={{0,96},{1,97},{2,98},{3,99},{4,100},{5,101},{6,102},{7,103},{8,104... | collective-permute-start | bytes 196616 | tf_op jit(solution)/shard_map/ppermute | solution.py:291
  141.8 7.1 %collective-permute-start.13 = (f32[64,256]{1,0:T(8,128)S(1)}, f32[64,256]{1,0:T(8,128)S(1)}, u32[]{:S(2)}, u32[]{:S(2)}) collective-permute-start(f32[64,256]{1,0:T(8,128)S(1)} %add.40), channel_id=1, source_target_pairs={{0,16},{1,17},{2,18},{3,19},{4,20},{5,21},{6,22},{7,23},{8,24},{9,... | collective-permute-start | bytes 196616 | tf_op jit(solution)/shard_map/ppermute | solution.py:291
  149.0 21.1 %copy-start.8 = (f32[64,256]{1,0:T(8,128)}, f32[64,256]{1,0:T(8,128)S(1)}, u32[]{:S(2)}) copy-start(f32[64,256]{1,0:T(8,128)S(1)} %add.41.refs_0_) | copy-start | bytes 196612
  149.0 18.2 %collective-permute-start.14 = (f32[64,256]{1,0:T(8,128)S(1)}, f32[64,256]{1,0:T(8,128)S(1)}, u32[]{:S(2)}, u32[]{:S(2)}) collective-permute-start(f32[64,256]{1,0:T(8,128)S(1)} %add.41.refs_0_), channel_id=1, source_target_pairs={{0,24},{1,25},{2,26},{3,27},{4,28},{5,29},{6,30},{7,31},{8,16},{9,... | collective-permute-start | bytes 196616 | tf_op jit(solution)/shard_map/ppermute | solution.py:291
  166.2 13.8 %copy-start.2 = (f32[2,512,256]{2,1,0:T(8,128)}, f32[2,512,256]{2,1,0:T(8,128)S(1)}, u32[]{:S(2)}) copy-start(f32[2,512,256]{2,1,0:T(8,128)S(1)} %collective-permute-done.15.left0) | copy-start | bytes 3145732
  167.2 2.9 %copy-start.9 = (f32[64,256]{1,0:T(8,128)}, f32[64,256]{1,0:T(8,128)S(1)}, u32[]{:S(2)}) copy-start(f32[64,256]{1,0:T(8,128)S(1)} %collective-permute-done.14.refs_1_) | copy-start | bytes 196612
  167.2 1.0 copy-start.7
  168.2 11.9 %copy-start.4 = (f32[2,512,256]{2,1,0:T(8,128)}, f32[2,512,256]{2,1,0:T(8,128)S(1)}, u32[]{:S(2)}) copy-start(f32[2,512,256]{2,1,0:T(8,128)S(1)} %collective-permute-done.17.left1) | copy-start | bytes 3145732
  168.2 26.7 %collective-permute-start.22 = (f32[2,2,256,256]{3,2,1,0:T(8,128)}, f32[2,2,256,256]{3,2,1,0:T(8,128)}, u32[]{:S(2)}, u32[]{:S(2)}) collective-permute-start(f32[2,2,256,256]{3,2,1,0:T(8,128)} %add.42), channel_id=1, source_target_pairs={{0,16},{16,32},{32,48},{48,64},{64,80},{80,96},{96,112},{1,17},{17... | collective-permute-start | bytes 3145736 | tf_op jit(solution)/shard_map/ppermute | solution.py:18
  171.6 7.5 %collective-permute-start.20 = (f32[64,256]{1,0:T(8,128)}, f32[64,256]{1,0:T(8,128)S(1)}, u32[]{:S(2)}, u32[]{:S(2)}) collective-permute-start(f32[64,256]{1,0:T(8,128)} %shard_map.89), channel_id=1, source_target_pairs={{0,6},{1,7},{2,4},{3,5},{4,2},{5,3},{6,0},{7,1},{8,14},{9,15},{10,... | collective-permute-start | bytes 196616 | tf_op jit(solution)/shard_map/ppermute | solution.py:291
  180.0 5.4 %collective-permute-start.21 = (f32[128,256]{1,0:T(8,128)S(1)}, f32[128,256]{1,0:T(8,128)S(1)}, u32[]{:S(2)}, u32[]{:S(2)}) collective-permute-start(f32[128,256]{1,0:T(8,128)S(1)} %pad_maximum_fusion.2), channel_id=1, source_target_pairs={{0,2},{1,3},{2,0},{3,1},{4,6},{5,7},{6,4},{7,5},{8,10},{9,11},{10,... | collective-permute-start | bytes 393224 | tf_op jit(solution)/shard_map/ppermute | solution.py:291
  194.9 6.3 %collective-permute-start.23 = (f32[256,256]{1,0:T(8,128)S(1)}, f32[256,256]{1,0:T(8,128)S(1)}, u32[]{:S(2)}, u32[]{:S(2)}) collective-permute-start(f32[256,256]{1,0:T(8,128)S(1)} %pad_maximum_fusion.1), channel_id=1, source_target_pairs={{0,1},{1,0},{2,3},{3,2},{4,5},{5,4},{6,7},{7,6},{8,9},{9,8},{10,11... | collective-permute-start | bytes 786440 | tf_op jit(solution)/shard_map/ppermute | solution.py:291

commit v4 on v3

--- a/solution.py
+++ b/solution.py
@@ -177,6 +177,14 @@
     return jnp.concatenate(out, axis=1)
 
 
+def times(x, y):
+    return x[0] * y[0] - x[1] * y[1], x[0] * y[1] + x[1] * y[0]
+
+
+def times_conj(x, y):
+    return x[0] * y[0] + x[1] * y[1], x[0] * y[1] - x[1] * y[0]
+
+
 def gradient_kernel(
     offsets, counts, obj, right0, right1, low_left, low_right, corner, middle, probe, measured, tables,
     main_out, right0_out, right1_out, low_left_out, low_right_out, corner_out, probe_out, ext, grid,
@@ -192,35 +200,46 @@
     grid[...] = jnp.zeros_like(grid)
     probe_out[...] = jnp.zeros_like(probe_out)
 
-    def visit(slot, carry):
-        top, edge = offsets[slot, 0], offsets[slot, 1]
-        p_re, p_im = (turned(probe[i], top % ROWS, edge % LANES) for i in range(2))
-        a_re, a_im = (window(ext, (i, 0), top, edge, side) for i in range(2))
-        psi_re = p_re * a_re - p_im * a_im
-        psi_im = p_re * a_im + p_im * a_re
-        y_re, y_im = two_sided(fold(psi_re), fold(psi_im), tables, 0, 2)
-        phi_re, phi_im = unfold(y_re), unfold(y_im)
-        b_re, b_im = (window(ext, (i, 1), top, edge, side) for i in range(2))
-        psi_re = phi_re * b_re - phi_im * b_im
-        psi_im = phi_re * b_im + phi_im * b_re
-        y_re, y_im = two_sided(fold(psi_re), fold(psi_im), tables, 4, 6)
-        far_re, far_im = whole(y_re), whole(y_im)
-        misfit = 2.0 * (far_re * far_re + far_im * far_im - measured[slot])
-        y_re, y_im = two_sided(quarters(misfit * far_re), quarters(misfit * far_im), tables, 6, 4)
-        d_re, d_im = unfold(y_re), unfold(y_im)
-        add_window(grid, (0, 1), top, edge, phi_re * d_re + phi_im * d_im)
-        add_window(grid, (1, 1), top, edge, phi_re * d_im - phi_im * d_re)
-        e_re = b_re * d_re + b_im * d_im
-        e_im = b_re * d_im - b_im * d_re
-        y_re, y_im = two_sided(fold(e_re), fold(e_im), tables, 2, 0)
-        d_re, d_im = unfold(y_re), unfold(y_im)
-        add_window(grid, (0, 0), top, edge, p_re * d_re + p_im * d_im)
-        add_window(grid, (1, 0), top, edge, p_re * d_im - p_im * d_re)
-        probe_out[0] += turned_back(a_re * d_re + a_im * d_im, top % ROWS, edge % LANES)
-        probe_out[1] += turned_back(a_re * d_im - a_im * d_re, top % ROWS, edge % LANES)
+    def visit(slots):
+        places_of = [(offsets[slot, 0], offsets[slot, 1]) for slot in slots]
+        turns = [(top % ROWS, edge % LANES) for top, edge in places_of]
+        p = [[turned(probe[i], *turn) for i in range(2)] for turn in turns]
+        a = [[window(ext, (i, 0), *at, side) for i in range(2)] for at in places_of]
+        psi = [times(x, y) for x, y in zip(p, a)]
+        y = [two_sided(fold(x[0]), fold(x[1]), tables, 0, 2) for x in psi]
+        phi = [[unfold(part) for part in x] for x in y]
+        b = [[window(ext, (i, 1), *at, side) for i in range(2)] for at in places_of]
+        psi = [times(x, z) for x, z in zip(phi, b)]
+        y = [two_sided(fold(x[0]), fold(x[1]), tables, 4, 6) for x in psi]
+        far = [[whole(part) for part in x] for x in y]
+        misfit = [2.0 * (x[0] * x[0] + x[1] * x[1] - measured[slot]) for x, slot in zip(far, slots)]
+        y = [two_sided(quarters(m * x[0]), quarters(m * x[1]), tables, 6, 4) for m, x in zip(misfit, far)]
+        d = [[unfold(part) for part in x] for x in y]
+        e = [times_conj(x, z) for x, z in zip(b, d)]
+        y = [two_sided(fold(x[0]), fold(x[1]), tables, 2, 0) for x in e]
+        for at, x, z in zip(places_of, phi, d):
+            for i, value in enumerate(times_conj(x, z)):
+                add_window(grid, (i, 1), *at, value)
+        d = [[unfold(part) for part in x] for x in y]
+        for at, x, z in zip(places_of, p, d):
+            for i, value in enumerate(times_conj(x, z)):
+                add_window(grid, (i, 0), *at, value)
+        for turn, x, z in zip(turns, a, d):
+            for i, value in enumerate(times_conj(x, z)):
+                probe_out[i] += turned_back(value, *turn)
+
+    live = jnp.minimum(counts[0], measured.shape[0])
+
+    def visit_two(pair, carry):
+        visit((2 * pair, 2 * pair + 1))
         return carry
 
-    lax.fori_loop(0, jnp.minimum(counts[0], measured.shape[0]), visit, 0)
+    lax.fori_loop(0, live // 2, visit_two, 0)
+
+    @pl.when(live % 2 == 1)
+    def _():
+        visit((live - 1,))
+
     main_out[...] = grid[:, :, :height, :width]
     right0_out[...] = grid[:, 0, :height, width:]
     right1_out[...] = grid[:, 1, :height, width:]
@@ -229,17 +248,18 @@
     corner_out[...] = grid[:, :, height:, width:]
 
 
-def side_kernel(held, left0, left1, out):
-    for layer, left in enumerate((left0, left1)):
+def side_kernel(held, left0, middle0, left1, out):
+    for layer, terms in enumerate(((left0, middle0), (left1,))):
 
         @pl.when(layer == pl.program_id(1))
         def _():
-            out[...] = held[...] + left[...]
-
-
-def top_kernel(held, middle, low_left, low_right, out):
+            out[...] = held[...] + sum(term[...] for term in terms)
+
+
+def top_kernel(own_corner, held, corner, low_left, low_right, out):
     side = low_right.shape[1]
-    out[:, :side] = held[:, :side] + (low_left[...] + middle[...])
+    middle = jnp.where(own_corner[0] == 1, corner[...], 0.0)
+    out[:, :side] = held[:, :side] + (low_left[...] + middle)
     out[:, side:] = held[:, side:] + low_right[...]
 
 
@@ -299,6 +319,7 @@
     pairs += [(first, second)] if middle == "direct" else []
     pairs = [((r, c), (r, to)) for r in range(rows) for c, to in pairs]
     pairs += [((r ^ 1, end), (r, second)) for r in range(rows)] if middle == "relay" else []
+    pairs += [((r, first), (r + 1, second)) for r in range(rows - 1)] if middle == "diagonal" else []
     return moved(shard, pairs)
 
 
@@ -308,10 +329,10 @@
     return moved(shard, [((r, first), (r ^ 1, end)) for r in range(rows)])
 
 
-def across_middle(shard, by):
+def across_middle(shard, by, down):
     rows, cols = lax.axis_size("row"), lax.axis_size("col")
     first, second = (cols // 2, cols // 2 - 1) if by < 0 else (cols // 2 - 1, cols // 2)
-    return moved(shard, [((r, first), (r + by, second)) for r in range(rows) if 0 <= r + by < rows])
+    return moved(shard, [((r, first), (r + down, second)) for r in range(rows) if 0 <= r + down < rows])
 
 
 def after(first, then):
@@ -371,7 +392,7 @@
     half = to_end(rim[1], -1)
     right0 = along_columns(rim[0], -1, "direct")
     right1 = along_columns(jnp.where(here == 0, half, rim[1]), -1, "relay")
-    middle = across_middle(object_field[:, :, :side, :side], -1)
+    middle = across_middle(object_field[:, :, :side, :side], -1, -1)
     order = np.concatenate([np.arange(0, side, 2), np.arange(1, side, 2)])
     picks = jnp.asarray(np.eye(side)[order].astype(ml_dtypes.bfloat16))
     pattern = pl.pallas_call(
@@ -402,23 +423,25 @@
     me = physical(lax.axis_index("row"), lax.axis_index("col"))
     low_bit, high_bit = me["y"] % 2 ^ me["y"] // 2, me["y"] // 2
     down_right = passed_along(low_right, "row", 1)
-    from_corner = along_columns(corner, 1, "nothing")
+    from_corner = along_columns(corner, 1, "diagonal")
     half = to_end(rim1, 1)
     own, other = halved(me["core"], probe_terms)
     own, other = split_rows(own + exchanged(other, core=1), low_bit)
     own, other = split_rows(own + exchanged(other, y=1), high_bit)
-    from_left0 = along_columns(rim0, 1, "direct")
-    arrived, down_right, corner = wait((exchanged(other, y=3), down_right, corner))
+    from_left0 = along_columns(rim0, 1, "nothing")
+    arrived, down_right, from_left0, rim0 = wait((exchanged(other, y=3), down_right, from_left0, rim0))
+    over_middle = across_middle(rim0, 1, 0)
     from_left1 = along_columns(jnp.where(here == cols - 1, half, rim1), 1, "relay")
-    middle = across_middle(corner, 1)
     share = own + arrived
     share = share + exchanged(share, x=1)
     share = share + exchanged(share, x=3)
     share = share + exchanged(share, z_lo=1)
-    arrived, from_left0, from_left1, middle, low_left = wait(
-        (exchanged(share, z_lo=1, z_hi=1), from_left0, from_left1, middle, low_left + from_corner)
-    )
-    down_left = passed_along(low_left, "row", 1)
+    own_corner = here == cut
+    passed_on = low_left + jnp.where(own_corner, 0.0, from_corner)
+    arrived, over_middle, from_left1, passed_on = wait(
+        (exchanged(share, z_lo=1, z_hi=1), over_middle, from_left1, passed_on)
+    )
+    down_left = passed_along(passed_on, "row", 1)
     share = added(share, arrived)
     share = joined(high_bit, share, exchanged(share, y=3))
     share = joined(low_bit, share, exchanged(share, y=1))
@@ -427,15 +450,15 @@
     upper = pl.BlockSpec((None, None, side, width), lambda i, j: (i, j, 0, 0))
     left = pl.BlockSpec((None, None, height, side), lambda i, j: (i, j, 0, 0))
     result = pl.pallas_call(
-        side_kernel, grid=(2, layers), in_specs=[left, edge, edge], out_specs=left,
+        side_kernel, grid=(2, layers), in_specs=[left, edge, edge, edge], out_specs=left,
         out_shape=struct(*object_field.shape), input_output_aliases={0: 0}, cost_estimate=SMALL,
-    )(main, from_left0, from_left1)
+    )(main, from_left0, over_middle, from_left1)
     share, down_left, result = wait((share, down_left, result))
     probe_grad = joined(me["core"], share, exchanged(share, core=1)).reshape(probe.shape)
     result = pl.pallas_call(
-        top_kernel, grid=(2, layers), in_specs=[upper, corner, corner, corner], out_specs=upper,
-        out_shape=struct(*object_field.shape), input_output_aliases={0: 0},
-    )(result, middle, down_left, down_right)
+        top_kernel, grid=(2, layers), in_specs=[SCALARS, upper, corner, corner, corner], out_specs=upper,
+        out_shape=struct(*object_field.shape), input_output_aliases={1: 0},
+    )(own_corner.astype(jnp.int32).reshape(1), result, from_corner, down_left, down_right)
     return (result, probe_grad)
 
 

time: 200 us -> 194 us (0.970); the launches traced: 202 us -> 192 us
  Pallas kernels: 56.5 us -> 40.5 us
  starting transfers between devices: 77.1 us -> 84.6 us
    pallas_call x1, Pallas kernels: 36.5 us -> 20 us  [per_device(): pl.pallas_call(gradient_kernel, in_specs=[SCALARS, SCALARS] + [vmem] * 10...]
    ppermute x20, starting transfers between devices: 61.9 us -> 73.8 us  [moved(): return lax.ppermute(shard, ('row', 'col'), flat)]
    ppermute x4, starting transfers between devices: 15.2 us -> 10.8 us  [passed_along(): return lax.ppermute(shard, axis, pairs)]
    ppermute x20, waiting for transfers between devices: 19.4 us -> 16 us  [moved(): return lax.ppermute(shard, ('row', 'col'), flat)]
    ppermute x4, waiting for transfers between devices: 33.1 us -> 35.3 us  [passed_along(): return lax.ppermute(shard, axis, pairs)]
  transfers between devices with their start and end apart: 24 -> 24, of which waited for: 10 -> 9; matrix products, arithmetic and copies ran while one was open for 4% -> 5% of each run, Pallas kernels for 9% -> 10%
where the time goes in v4:
time: 194 us; the launch traced here: 192 us
  starting transfers between devices  84.6 us (44%)
  waiting for transfers between devices  51.3 us (26%)
  Pallas kernels  40.5 us (21%)
  other arithmetic  8.92 us (5%)
  local copies, waits for them, and re-layouts  5.42 us (3%)
    ppermute x20, starting transfers between devices, moved(): return lax.ppermute(shard, ('row', 'col'), flat)  73.8 us
    ppermute x4, waiting for transfers between devices, passed_along(): return lax.ppermute(shard, axis, pairs)  35.3 us
    pallas_call x1, Pallas kernels, per_device(): pl.pallas_call(gradient_kernel, in_specs=[SCALARS, SCALARS] + [vmem] * 10...  20 us
    ppermute x20, waiting for transfers between devices, moved(): return lax.ppermute(shard, ('row', 'col'), flat)  16 us
    ppermute x4, starting transfers between devices, passed_along(): return lax.ppermute(shard, axis, pairs)  10.8 us
    pallas_call x1, Pallas kernels, per_device(): pl.pallas_call(order_kernel, grid=(slots,), in_specs=[per_slot(side, side...  8 us
    pallas_call x1, Pallas kernels, per_device(): pl.pallas_call(side_kernel, grid=(2, layers), in_specs=[left, edge, edge,...  4.64 us
    pallas_call x1, Pallas kernels, per_device(): pl.pallas_call(top_kernel, grid=(2, layers), in_specs=[SCALARS, upper, co...  4.34 us
  transfers between devices with their start and end apart: 24, of which 9 were waited for; matrix products, arithmetic and copies ran while one was open for 5% of the time, Pallas kernels for 10%

profile of v4, /device:TPU:3, one launch (start us, length us, event | category | flops | bytes accessed | tf_op | source)
XLA Modules:
  0.0 192.4 jit_solution(8410106159185129032)
XLA Ops:
  0.6 0.0 copy-start
  0.6 3.2 %slice_bitcast_fusion = (f32[2,512,256]{2,1,0:T(8,128)}, f32[2,512,256]{2,1,0:T(8,128)}) fusion(f32[2,2,512,512]{3,2,1,0:T(8,128)} %obj.1), kind=kLoop, calls=%fused_computation.1 | loop fusion | bytes 4194304 | tf_op jit(solution)/shard_map/squeeze | solution.py:391
  3.8 1.7 collective-permute-start.1
  5.5 1.5 fusion
  7.0 3.6 %collective-permute-start.3 = (f32[2,2,256,256]{3,2,1,0:T(8,128)}, f32[2,2,256,256]{3,2,1,0:T(8,128)S(1)}, u32[]{:S(2)}, u32[]{:S(2)}) collective-permute-start(f32[2,2,256,256]{3,2,1,0:T(8,128)} %get-tuple-element.47), channel_id=1, source_target_pairs={{16,0},{32,16},{48,32},{64,48},{80,64},{96,80},{112,96},{17,1},{33... | collective-permute-start | bytes 3145736 | tf_op jit(solution)/shard_map/ppermute | solution.py:18
  10.7 0.7 collective-permute-start.6
  11.4 2.5 %collective-permute-start = (f32[2,512,256]{2,1,0:T(8,128)}, f32[2,512,256]{2,1,0:T(8,128)S(1)}, u32[]{:S(2)}, u32[]{:S(2)}) collective-permute-start(f32[2,512,256]{2,1,0:T(8,128)} %get-tuple-element.49), channel_id=1, source_target_pairs={{1,0},{2,1},{3,2},{4,3},{5,4},{6,5},{7,6},{9,8},{10,9},{11,10},{12... | collective-permute-start | bytes 3145736 | tf_op jit(solution)/shard_map/ppermute | solution.py:311
  13.9 1.9 collective-permute-start.4
  15.8 8.0 %shard_map.86.measured = f32[8,256,256]{2,1,0:T(8,128)} custom-call(f32[8,256,256]{2,1,0:T(8,128)} %measured.1, bf16[256,256]{1,0:T(8,128)(2,1)} %constant.63.clone.picks), custom_call_target="tpu_custom_call" | custom-call | bytes 419430400 | tf_op jit(solution)/shard_map/pallas_call | solution.py:398
  23.8 0.0 collective-permute-done.1
  23.8 2.4 %broadcast_select_fusion.1 = f32[2,512,256]{2,1,0:T(8,128)} fusion(f32[2,512,256]{2,1,0:T(8,128)} %collective-permute-done.1, pred[]{:T(512)S(6)} %eq.32, f32[2,2,512,512]{3,2,1,0:T(8,128)} %obj.1), kind=kLoop, calls=%fused_computation.5 | loop fusion | flops 262144 | bytes 3145729 | tf_op jit(solution)/shard_map/jit(_where)/select_n | solution.py:394
  26.2 1.9 collective-permute-start.2
  28.1 6.0 %collective-permute-done.3.low_left = f32[2,2,256,256]{3,2,1,0:T(8,128)S(1)} collective-permute-done((f32[2,2,256,256]{3,2,1,0:T(8,128)}, f32[2,2,256,256]{3,2,1,0:T(8,128)S(1)}, u32[]{:S(2)}, u32[]{:S(2)}) %collective-permute-start.3) | collective-permute-done | bytes 1048608 | tf_op jit(solution)/shard_map/ppermute | solution.py:18
  34.1 3.4 %collective-permute-start.5 = (f32[2,2,256,256]{3,2,1,0:T(8,128)S(1)}, f32[2,2,256,256]{3,2,1,0:T(8,128)}, u32[]{:S(2)}, u32[]{:S(2)}) collective-permute-start(f32[2,2,256,256]{3,2,1,0:T(8,128)S(1)} %collective-permute-done.3.low_left), channel_id=1, source_target_pairs={{1,0},{2,1},{3,2},{4,3},{5,4},{6,5},{7,6},{9,8},{10,9},{11,10},{12... | collective-permute-start | bytes 3145736 | tf_op jit(solution)/shard_map/ppermute | solution.py:311
  37.4 0.7 copy.13.offsets
  38.8 0.0 collective-permute-done.6.middle
  38.8 0.0 collective-permute-done.right0
  38.8 17.8 %collective-permute-done.4.low_right = f32[2,2,256,256]{3,2,1,0:T(8,128)} collective-permute-done((f32[2,2,256,256]{3,2,1,0:T(8,128)}, f32[2,2,256,256]{3,2,1,0:T(8,128)}, u32[]{:S(2)}, u32[]{:S(2)}) %collective-permute-start.4) | collective-permute-done | bytes 1048608 | tf_op jit(solution)/shard_map/ppermute | solution.py:18
  56.6 0.0 collective-permute-done.2.right1
  56.6 0.0 collective-permute-done.5.corner
  56.7 20.0 %shard_map.87 = (f32[2,2,512,512]{3,2,1,0:T(8,128)}, f32[2,512,256]{2,1,0:T(8,128)}, f32[2,512,256]{2,1,0:T(8,128)}, f32[2,2,256,256]{3,2,1,0:T(8,128)}, f32[2,2...) custom-call(s32[8,2]{1,0:T(8,128)} %copy.13.offsets, s32[1]{0:T(128)S(6)} %copy.18.counts, ...), custom_call_target="tpu_custom_call" | custom-call | bytes 419430400 | tf_op jit(solution)/shard_map/pallas_call | solution.py:407
  76.7 1.9 %shard_map.88 = (f32[256,256]{1,0:T(8,128)}, f32[256,256]{1,0:T(8,128)}) custom-call(s32[1]{0:T(128)} %bitcast.1.mine, f32[2,256,256]{2,1,0:T(8,128)} %get-tuple-element.26.value), custom_call_target="tpu_custom_call" | custom-call | bytes 419430400 | tf_op jit(solution)/shard_map/pallas_call | solution.py:365
  78.7 11.9 %collective-permute-start.7 = (f32[256,256]{1,0:T(8,128)}, f32[256,256]{1,0:T(8,128)S(1)}, u32[]{:S(2)}, u32[]{:S(2)}) collective-permute-start(f32[256,256]{1,0:T(8,128)} %get-tuple-element.28), channel_id=1, source_target_pairs={{0,1},{1,0},{2,3},{3,2},{4,5},{5,4},{6,7},{7,6},{8,9},{9,8},{10,11... | collective-permute-start | bytes 786440 | tf_op jit(solution)/shard_map/ppermute | solution.py:311
  90.6 3.4 %collective-permute-start.11 = (f32[2,512,256]{2,1,0:T(8,128)}, f32[2,512,256]{2,1,0:T(8,128)}, u32[]{:S(2)}, u32[]{:S(2)}) collective-permute-start(f32[2,512,256]{2,1,0:T(8,128)} %get-tuple-element.32), channel_id=1, source_target_pairs={{0,1},{1,2},{2,3},{3,4},{4,5},{5,6},{6,7},{8,9},{9,10},{10,11},{11... | collective-permute-start | bytes 3145736 | tf_op jit(solution)/shard_map/ppermute | solution.py:311
  94.0 1.9 collective-permute-start.10
  95.9 1.6 collective-permute-start.17
  97.5 0.0 collective-permute-done.7
  97.5 1.0 add.36
  98.6 5.7 %collective-permute-start.8 = (f32[128,256]{1,0:T(8,128)S(1)}, f32[128,256]{1,0:T(8,128)S(1)}, u32[]{:S(2)}, u32[]{:S(2)}) collective-permute-start(f32[128,256]{1,0:T(8,128)S(1)} %slice_select_fusion), channel_id=1, source_target_pairs={{0,2},{1,3},{2,0},{3,1},{4,6},{5,7},{6,4},{7,5},{8,10},{9,11},{10,... | collective-permute-start | bytes 393224 | tf_op jit(solution)/shard_map/ppermute | solution.py:311
  104.3 4.4 %collective-permute-done.8 = f32[128,256]{1,0:T(8,128)S(1)} collective-permute-done((f32[128,256]{1,0:T(8,128)S(1)}, f32[128,256]{1,0:T(8,128)S(1)}, u32[]{:S(2)}, u32[]{:S(2)}) %collective-permute-start.8) | collective-permute-done | bytes 131104 | tf_op jit(solution)/shard_map/ppermute | solution.py:311
  108.7 9.4 %collective-permute-start.9 = (f32[64,256]{1,0:T(8,128)S(1)}, f32[64,256]{1,0:T(8,128)S(1)}, u32[]{:S(2)}, u32[]{:S(2)}) collective-permute-start(f32[64,256]{1,0:T(8,128)S(1)} %slice_select_fusion.1), channel_id=1, source_target_pairs={{0,6},{1,7},{2,4},{3,5},{4,2},{5,3},{6,0},{7,1},{8,14},{9,15},{10,... | collective-permute-start | bytes 196616 | tf_op jit(solution)/shard_map/ppermute | solution.py:311
  118.1 3.8 %collective-permute-start.19 = (f32[2,2,256,256]{3,2,1,0:T(8,128)}, f32[2,2,256,256]{3,2,1,0:T(8,128)S(1)}, u32[]{:S(2)}, u32[]{:S(2)}) collective-permute-start(f32[2,2,256,256]{3,2,1,0:T(8,128)} %get-tuple-element.35), channel_id=1, source_target_pairs={{0,1},{1,2},{2,3},{3,4},{4,5},{5,6},{6,7},{8,9},{9,10},{10,11},{11... | collective-permute-start | bytes 3145736 | tf_op jit(solution)/shard_map/ppermute | solution.py:311
  121.9 0.0 collective-permute-done.9
  121.9 0.0 collective-permute-done.11.left0
  121.9 0.0 collective-permute-done.10.low_right
  121.9 1.6 collective-permute-start.16
  123.6 0.0 collective-permute-done.17
  123.6 2.4 %broadcast_select_fusion = f32[2,512,256]{2,1,0:T(8,128)} fusion(f32[2,512,256]{2,1,0:T(8,128)} %collective-permute-done.17, f32[2,512,256]{2,1,0:T(8,128)} %get-tuple-element.33, pred[]{:T(512)S(6)} %eq.33), kind=kLoop, calls=%fused_computation.4 | loop fusion | flops 262144 | bytes 3145729 | tf_op jit(solution)/shard_map/jit(_where)/select_n | solution.py:434
  126.0 2.5 %collective-permute-start.18 = (f32[2,512,256]{2,1,0:T(8,128)}, f32[2,512,256]{2,1,0:T(8,128)}, u32[]{:S(2)}, u32[]{:S(2)}) collective-permute-start(f32[2,512,256]{2,1,0:T(8,128)} %broadcast_select_fusion), channel_id=1, source_target_pairs={{0,1},{1,2},{2,3},{3,4},{4,5},{5,6},{6,7},{8,9},{9,10},{10,11},{11... | collective-permute-start | bytes 3145736 | tf_op jit(solution)/shard_map/ppermute | solution.py:311
  128.6 0.6 collective-permute-start.12
  129.2 2.6 %collective-permute-done.12 = f32[64,256]{1,0:T(8,128)S(1)} collective-permute-done((f32[64,256]{1,0:T(8,128)S(1)}, f32[64,256]{1,0:T(8,128)S(1)}, u32[]{:S(2)}, u32[]{:S(2)}) %collective-permute-start.12) | collective-permute-done | bytes 65568 | tf_op jit(solution)/shard_map/ppermute | solution.py:311
  131.8 4.4 %collective-permute-start.13 = (f32[64,256]{1,0:T(8,128)S(1)}, f32[64,256]{1,0:T(8,128)S(1)}, u32[]{:S(2)}, u32[]{:S(2)}) collective-permute-start(f32[64,256]{1,0:T(8,128)S(1)} %add.39), channel_id=1, source_target_pairs={{0,96},{1,97},{2,98},{3,99},{4,100},{5,101},{6,102},{7,103},{8,104... | collective-permute-start | bytes 196616 | tf_op jit(solution)/shard_map/ppermute | solution.py:311
  136.2 1.7 collective-permute-done.13
  137.9 2.6 %collective-permute-start.14 = (f32[64,256]{1,0:T(8,128)S(1)}, f32[64,256]{1,0:T(8,128)S(1)}, u32[]{:S(2)}, u32[]{:S(2)}) collective-permute-start(f32[64,256]{1,0:T(8,128)S(1)} %add.40), channel_id=1, source_target_pairs={{0,16},{1,17},{2,18},{3,19},{4,20},{5,21},{6,22},{7,23},{8,24},{9,... | collective-permute-start | bytes 196616 | tf_op jit(solution)/shard_map/ppermute | solution.py:311
  140.5 1.8 collective-permute-done.14
  142.3 0.0 copy-start.8
  142.3 14.1 %collective-permute-start.15 = (f32[64,256]{1,0:T(8,128)S(1)}, f32[64,256]{1,0:T(8,128)S(1)}, u32[]{:S(2)}, u32[]{:S(2)}) collective-permute-start(f32[64,256]{1,0:T(8,128)S(1)} %add.41.refs_0_), channel_id=1, source_target_pairs={{0,24},{1,25},{2,26},{3,27},{4,28},{5,29},{6,30},{7,31},{8,16},{9,... | collective-permute-start | bytes 196616 | tf_op jit(solution)/shard_map/ppermute | solution.py:311
  156.4 0.0 collective-permute-done.19.corner
  156.4 1.3 select_add_fusion
  157.7 0.9 collective-permute-done.15.refs_1_
  158.6 0.0 collective-permute-done.16.middle0
  158.6 0.0 collective-permute-done.18.left1
  158.6 3.3 %collective-permute-start.22 = (f32[2,2,256,256]{3,2,1,0:T(8,128)}, f32[2,2,256,256]{3,2,1,0:T(8,128)S(1)}, u32[]{:S(2)}, u32[]{:S(2)}) collective-permute-start(f32[2,2,256,256]{3,2,1,0:T(8,128)} %select_add_fusion), channel_id=1, source_target_pairs={{0,16},{16,32},{32,48},{48,64},{64,80},{80,96},{96,112},{1,17},{17... | collective-permute-start | bytes 3145736 | tf_op jit(solution)/shard_map/ppermute | solution.py:18
  161.9 1.5 shard_map.89
  163.4 0.0 collective-permute-start.20
  163.4 4.7 %collective-permute-done.20 = f32[64,256]{1,0:T(8,128)S(1)} collective-permute-done((f32[64,256]{1,0:T(8,128)}, f32[64,256]{1,0:T(8,128)S(1)}, u32[]{:S(2)}, u32[]{:S(2)}) %collective-permute-start.20) | collective-permute-done | bytes 65568 | tf_op jit(solution)/shard_map/ppermute | solution.py:311
  168.1 0.9 broadcast_select_fusion.7
  169.0 0.1 collective-permute-start.21
  169.1 4.6 %shard_map.90.held = f32[2,2,512,512]{3,2,1,0:T(8,128)} custom-call(f32[2,2,512,512]{3,2,1,0:T(8,128)} %get-tuple-element.38.held, f32[2,512,256]{2,1,0:T(8,128)} %collective-permute-done.11.left0, f32[2,512,256]{2,1,0:T(8,128)} %collective-permute-done.16.middle0, f32[2,512,256]{2,1,0:T(8,128)} %collective-permute-done.18.left1), custom_call_target="tpu_custom_call", output_to_operand_aliasing={{}: (0, {})} | custom-call | bytes 1024 | tf_op jit(solution)/shard_map/pallas_call | solution.py:452
  173.7 0.0 collective-permute-done.21
  173.8 11.5 %collective-permute-done.22.low_left = f32[2,2,256,256]{3,2,1,0:T(8,128)S(1)} collective-permute-done((f32[2,2,256,256]{3,2,1,0:T(8,128)}, f32[2,2,256,256]{3,2,1,0:T(8,128)S(1)}, u32[]{:S(2)}, u32[]{:S(2)}) %collective-permute-start.22) | collective-permute-done | bytes 1048608 | tf_op jit(solution)/shard_map/ppermute | solution.py:18
  185.3 1.8 collective-permute-start.23
  187.2 4.3 %shard_map.91 = f32[2,2,512,512]{3,2,1,0:T(8,128)} custom-call(s32[1]{0:T(128)} %bitcast.own_corner, f32[2,2,512,512]{3,2,1,0:T(8,128)} %shard_map.90.held, f32[2,2,256,256]{3,2,1,0:T(8,128)} %copy-done.1, f32[2,2,256,256]{3,2,1,0:T(8,128)} %copy-done.6, f32[2,2,256,256]{3,2,1,0:T(8,128)} %copy-done.2), custom_call_target="tpu_custom_call", output_to_operand_aliasing={{}: (1, {})} | custom-call | tf_op jit(solution)/shard_map/pallas_call | solution.py:458
  191.5 0.8 pad_maximum_fusion
  (32 shorter events, 0.2 us)
Async XLA Ops:
  0.6 4.9 %copy-start = (f32[2,2,512,512]{3,2,1,0:T(8,128)S(1)}, f32[2,2,512,512]{3,2,1,0:T(8,128)}, u32[]{:S(2)}) copy-start(f32[2,2,512,512]{3,2,1,0:T(8,128)} %obj.1) | copy-start | bytes 12582916
  3.8 20.0 %collective-permute-start.1 = (f32[2,512,256]{2,1,0:T(8,128)}, f32[2,512,256]{2,1,0:T(8,128)}, u32[]{:S(2)}, u32[]{:S(2)}) collective-permute-start(f32[2,512,256]{2,1,0:T(8,128)} %get-tuple-element.48), channel_id=1, source_target_pairs={{8,16},{24,0},{40,48},{56,32},{72,80},{88,64},{104,112},{120,96}} | collective-permute-start | bytes 3145736 | tf_op jit(solution)/shard_map/ppermute | solution.py:311
  7.0 30.4 %copy-start.10 = (s32[8,2]{0,1:T(2,128)S(1)}, s32[8,2]{0,1:T(2,128)}, u32[]{:S(2)}) copy-start(s32[8,2]{0,1:T(2,128)} %param.10) | copy-start | bytes 196
  7.0 27.0 %collective-permute-start.3 = (f32[2,2,256,256]{3,2,1,0:T(8,128)}, f32[2,2,256,256]{3,2,1,0:T(8,128)S(1)}, u32[]{:S(2)}, u32[]{:S(2)}) collective-permute-start(f32[2,2,256,256]{3,2,1,0:T(8,128)} %get-tuple-element.47), channel_id=1, source_target_pairs={{16,0},{32,16},{48,32},{64,48},{80,64},{96,80},{112,96},{17,1},{33... | collective-permute-start | bytes 3145736 | tf_op jit(solution)/shard_map/ppermute | solution.py:18
  10.7 28.1 %collective-permute-start.6 = (f32[2,2,256,256]{3,2,1,0:T(8,128)}, f32[2,2,256,256]{3,2,1,0:T(8,128)S(1)}, u32[]{:S(2)}, u32[]{:S(2)}) collective-permute-start(f32[2,2,256,256]{3,2,1,0:T(8,128)} %get-tuple-element.47), channel_id=1, source_target_pairs={{24,7},{40,23},{56,39},{72,55},{88,71},{104,87},{120,103}} | collective-permute-start | bytes 3145736 | tf_op jit(solution)/shard_map/ppermute | solution.py:311
  11.4 27.4 %collective-permute-start = (f32[2,512,256]{2,1,0:T(8,128)}, f32[2,512,256]{2,1,0:T(8,128)S(1)}, u32[]{:S(2)}, u32[]{:S(2)}) collective-permute-start(f32[2,512,256]{2,1,0:T(8,128)} %get-tuple-element.49), channel_id=1, source_target_pairs={{1,0},{2,1},{3,2},{4,3},{5,4},{6,5},{7,6},{9,8},{10,9},{11,10},{12... | collective-permute-start | bytes 3145736 | tf_op jit(solution)/shard_map/ppermute | solution.py:311
  13.9 42.7 %collective-permute-start.4 = (f32[2,2,256,256]{3,2,1,0:T(8,128)}, f32[2,2,256,256]{3,2,1,0:T(8,128)}, u32[]{:S(2)}, u32[]{:S(2)}) collective-permute-start(f32[2,2,256,256]{3,2,1,0:T(8,128)} %get-tuple-element.46), channel_id=1, source_target_pairs={{16,0},{32,16},{48,32},{64,48},{80,64},{96,80},{112,96},{17,1},{33... | collective-permute-start | bytes 3145736 | tf_op jit(solution)/shard_map/ppermute | solution.py:18
  26.2 30.4 %collective-permute-start.2 = (f32[2,512,256]{2,1,0:T(8,128)}, f32[2,512,256]{2,1,0:T(8,128)}, u32[]{:S(2)}, u32[]{:S(2)}) collective-permute-start(f32[2,512,256]{2,1,0:T(8,128)} %broadcast_select_fusion.1), channel_id=1, source_target_pairs={{1,0},{2,1},{3,2},{4,3},{5,4},{6,5},{7,6},{9,8},{10,9},{11,10},{12... | collective-permute-start | bytes 3145736 | tf_op jit(solution)/shard_map/ppermute | solution.py:311
  34.1 22.6 %copy-start.3 = (f32[2,2,256,256]{3,2,1,0:T(8,128)}, f32[2,2,256,256]{3,2,1,0:T(8,128)S(1)}, u32[]{:S(2)}) copy-start(f32[2,2,256,256]{3,2,1,0:T(8,128)S(1)} %collective-permute-done.3.low_left) | copy-start | bytes 3145732
  34.1 22.6 %collective-permute-start.5 = (f32[2,2,256,256]{3,2,1,0:T(8,128)S(1)}, f32[2,2,256,256]{3,2,1,0:T(8,128)}, u32[]{:S(2)}, u32[]{:S(2)}) collective-permute-start(f32[2,2,256,256]{3,2,1,0:T(8,128)S(1)} %collective-permute-done.3.low_left), channel_id=1, source_target_pairs={{1,0},{2,1},{3,2},{4,3},{5,4},{6,5},{7,6},{9,8},{10,9},{11,10},{12... | collective-permute-start | bytes 3145736 | tf_op jit(solution)/shard_map/ppermute | solution.py:311
  38.8 17.9 %copy-start.4 = (f32[2,2,256,256]{3,2,1,0:T(8,128)}, f32[2,2,256,256]{3,2,1,0:T(8,128)S(1)}, u32[]{:S(2)}) copy-start(f32[2,2,256,256]{3,2,1,0:T(8,128)S(1)} %collective-permute-done.6.middle) | copy-start | bytes 3145732
  38.8 17.9 %copy-start.5 = (f32[2,512,256]{2,1,0:T(8,128)}, f32[2,512,256]{2,1,0:T(8,128)S(1)}, u32[]{:S(2)}) copy-start(f32[2,512,256]{2,1,0:T(8,128)S(1)} %collective-permute-done.right0) | copy-start | bytes 3145732
  76.7 79.7 %copy-start.7 = (f32[2,2,256,256]{3,2,1,0:T(8,128)S(1)}, f32[2,2,256,256]{3,2,1,0:T(8,128)}, u32[]{:S(2)}) copy-start(f32[2,2,256,256]{3,2,1,0:T(8,128)} %get-tuple-element.34) | copy-start | bytes 3145732
  78.7 18.9 %collective-permute-start.7 = (f32[256,256]{1,0:T(8,128)}, f32[256,256]{1,0:T(8,128)S(1)}, u32[]{:S(2)}, u32[]{:S(2)}) collective-permute-start(f32[256,256]{1,0:T(8,128)} %get-tuple-element.28), channel_id=1, source_target_pairs={{0,1},{1,0},{2,3},{3,2},{4,5},{5,4},{6,7},{7,6},{8,9},{9,8},{10,11... | collective-permute-start | bytes 786440 | tf_op jit(solution)/shard_map/ppermute | solution.py:311
  90.6 31.4 %collective-permute-start.11 = (f32[2,512,256]{2,1,0:T(8,128)}, f32[2,512,256]{2,1,0:T(8,128)}, u32[]{:S(2)}, u32[]{:S(2)}) collective-permute-start(f32[2,512,256]{2,1,0:T(8,128)} %get-tuple-element.32), channel_id=1, source_target_pairs={{0,1},{1,2},{2,3},{3,4},{4,5},{5,6},{6,7},{8,9},{9,10},{10,11},{11... | collective-permute-start | bytes 3145736 | tf_op jit(solution)/shard_map/ppermute | solution.py:311
  94.0 28.0 %collective-permute-start.10 = (f32[2,2,256,256]{3,2,1,0:T(8,128)}, f32[2,2,256,256]{3,2,1,0:T(8,128)S(1)}, u32[]{:S(2)}, u32[]{:S(2)}) collective-permute-start(f32[2,2,256,256]{3,2,1,0:T(8,128)} %get-tuple-element.29), channel_id=1, source_target_pairs={{0,16},{16,32},{32,48},{48,64},{64,80},{80,96},{96,112},{1,17},{17... | collective-permute-start | bytes 3145736 | tf_op jit(solution)/shard_map/ppermute | solution.py:18
  95.9 27.7 %collective-permute-start.17 = (f32[2,512,256]{2,1,0:T(8,128)}, f32[2,512,256]{2,1,0:T(8,128)}, u32[]{:S(2)}, u32[]{:S(2)}) collective-permute-start(f32[2,512,256]{2,1,0:T(8,128)} %get-tuple-element.33), channel_id=1, source_target_pairs={{7,31},{23,15},{39,63},{55,47},{71,95},{87,79},{103,127},{119,111}} | collective-permute-start | bytes 3145736 | tf_op jit(solution)/shard_map/ppermute | solution.py:311
  98.6 10.1 %collective-permute-start.8 = (f32[128,256]{1,0:T(8,128)S(1)}, f32[128,256]{1,0:T(8,128)S(1)}, u32[]{:S(2)}, u32[]{:S(2)}) collective-permute-start(f32[128,256]{1,0:T(8,128)S(1)} %slice_select_fusion), channel_id=1, source_target_pairs={{0,2},{1,3},{2,0},{3,1},{4,6},{5,7},{6,4},{7,5},{8,10},{9,11},{10,... | collective-permute-start | bytes 393224 | tf_op jit(solution)/shard_map/ppermute | solution.py:311
  108.7 13.2 %collective-permute-start.9 = (f32[64,256]{1,0:T(8,128)S(1)}, f32[64,256]{1,0:T(8,128)S(1)}, u32[]{:S(2)}, u32[]{:S(2)}) collective-permute-start(f32[64,256]{1,0:T(8,128)S(1)} %slice_select_fusion.1), channel_id=1, source_target_pairs={{0,6},{1,7},{2,4},{3,5},{4,2},{5,3},{6,0},{7,1},{8,14},{9,15},{10,... | collective-permute-start | bytes 196616 | tf_op jit(solution)/shard_map/ppermute | solution.py:311
  118.1 38.3 %collective-permute-start.19 = (f32[2,2,256,256]{3,2,1,0:T(8,128)}, f32[2,2,256,256]{3,2,1,0:T(8,128)S(1)}, u32[]{:S(2)}, u32[]{:S(2)}) collective-permute-start(f32[2,2,256,256]{3,2,1,0:T(8,128)} %get-tuple-element.35), channel_id=1, source_target_pairs={{0,1},{1,2},{2,3},{3,4},{4,5},{5,6},{6,7},{8,9},{9,10},{10,11},{11... | collective-permute-start | bytes 3145736 | tf_op jit(solution)/shard_map/ppermute | solution.py:311
  121.9 51.8 %copy-start.2 = (f32[2,2,256,256]{3,2,1,0:T(8,128)}, f32[2,2,256,256]{3,2,1,0:T(8,128)S(1)}, u32[]{:S(2)}) copy-start(f32[2,2,256,256]{3,2,1,0:T(8,128)S(1)} %collective-permute-done.10.low_right) | copy-start | bytes 3145732
  121.9 36.6 %collective-permute-start.16 = (f32[2,512,256]{2,1,0:T(8,128)}, f32[2,512,256]{2,1,0:T(8,128)}, u32[]{:S(2)}, u32[]{:S(2)}) collective-permute-start(f32[2,512,256]{2,1,0:T(8,128)} %get-tuple-element.32), channel_id=1, source_target_pairs={{7,8},{23,24},{39,40},{55,56},{71,72},{87,88},{103,104},{119,120}} | collective-permute-start | bytes 3145736 | tf_op jit(solution)/shard_map/ppermute | solution.py:311
  126.0 32.5 %collective-permute-start.18 = (f32[2,512,256]{2,1,0:T(8,128)}, f32[2,512,256]{2,1,0:T(8,128)}, u32[]{:S(2)}, u32[]{:S(2)}) collective-permute-start(f32[2,512,256]{2,1,0:T(8,128)} %broadcast_select_fusion), channel_id=1, source_target_pairs={{0,1},{1,2},{2,3},{3,4},{4,5},{5,6},{6,7},{8,9},{9,10},{10,11},{11... | collective-permute-start | bytes 3145736 | tf_op jit(solution)/shard_map/ppermute | solution.py:311
  128.6 3.2 %collective-permute-start.12 = (f32[64,256]{1,0:T(8,128)S(1)}, f32[64,256]{1,0:T(8,128)S(1)}, u32[]{:S(2)}, u32[]{:S(2)}) collective-permute-start(f32[64,256]{1,0:T(8,128)S(1)} %select_add_fusion.2), channel_id=1, source_target_pairs={{0,32},{1,33},{2,34},{3,35},{4,36},{5,37},{6,38},{7,39},{8,40},{9,... | collective-permute-start | bytes 196616 | tf_op jit(solution)/shard_map/ppermute | solution.py:311
  131.8 6.1 %collective-permute-start.13 = (f32[64,256]{1,0:T(8,128)S(1)}, f32[64,256]{1,0:T(8,128)S(1)}, u32[]{:S(2)}, u32[]{:S(2)}) collective-permute-start(f32[64,256]{1,0:T(8,128)S(1)} %add.39), channel_id=1, source_target_pairs={{0,96},{1,97},{2,98},{3,99},{4,100},{5,101},{6,102},{7,103},{8,104... | collective-permute-start | bytes 196616 | tf_op jit(solution)/shard_map/ppermute | solution.py:311
  137.9 4.4 %collective-permute-start.14 = (f32[64,256]{1,0:T(8,128)S(1)}, f32[64,256]{1,0:T(8,128)S(1)}, u32[]{:S(2)}, u32[]{:S(2)}) collective-permute-start(f32[64,256]{1,0:T(8,128)S(1)} %add.40), channel_id=1, source_target_pairs={{0,16},{1,17},{2,18},{3,19},{4,20},{5,21},{6,22},{7,23},{8,24},{9,... | collective-permute-start | bytes 196616 | tf_op jit(solution)/shard_map/ppermute | solution.py:311
  142.3 19.6 %copy-start.8 = (f32[64,256]{1,0:T(8,128)}, f32[64,256]{1,0:T(8,128)S(1)}, u32[]{:S(2)}) copy-start(f32[64,256]{1,0:T(8,128)S(1)} %add.41.refs_0_) | copy-start | bytes 196612
  142.3 16.3 %collective-permute-start.15 = (f32[64,256]{1,0:T(8,128)S(1)}, f32[64,256]{1,0:T(8,128)S(1)}, u32[]{:S(2)}, u32[]{:S(2)}) collective-permute-start(f32[64,256]{1,0:T(8,128)S(1)} %add.41.refs_0_), channel_id=1, source_target_pairs={{0,24},{1,25},{2,26},{3,27},{4,28},{5,29},{6,30},{7,31},{8,16},{9,... | collective-permute-start | bytes 196616 | tf_op jit(solution)/shard_map/ppermute | solution.py:311
  156.4 17.3 %copy-start.1 = (f32[2,2,256,256]{3,2,1,0:T(8,128)}, f32[2,2,256,256]{3,2,1,0:T(8,128)S(1)}, u32[]{:S(2)}) copy-start(f32[2,2,256,256]{3,2,1,0:T(8,128)S(1)} %collective-permute-done.19.corner) | copy-start | bytes 3145732
  158.6 3.4 %copy-start.9 = (f32[64,256]{1,0:T(8,128)}, f32[64,256]{1,0:T(8,128)S(1)}, u32[]{:S(2)}) copy-start(f32[64,256]{1,0:T(8,128)S(1)} %collective-permute-done.15.refs_1_) | copy-start | bytes 196612
  158.6 26.8 %collective-permute-start.22 = (f32[2,2,256,256]{3,2,1,0:T(8,128)}, f32[2,2,256,256]{3,2,1,0:T(8,128)S(1)}, u32[]{:S(2)}, u32[]{:S(2)}) collective-permute-start(f32[2,2,256,256]{3,2,1,0:T(8,128)} %select_add_fusion), channel_id=1, source_target_pairs={{0,16},{16,32},{32,48},{48,64},{64,80},{80,96},{96,112},{1,17},{17... | collective-permute-start | bytes 3145736 | tf_op jit(solution)/shard_map/ppermute | solution.py:18
  163.4 4.7 %collective-permute-start.20 = (f32[64,256]{1,0:T(8,128)}, f32[64,256]{1,0:T(8,128)S(1)}, u32[]{:S(2)}, u32[]{:S(2)}) collective-permute-start(f32[64,256]{1,0:T(8,128)} %shard_map.89), channel_id=1, source_target_pairs={{0,6},{1,7},{2,4},{3,5},{4,2},{5,3},{6,0},{7,1},{8,14},{9,15},{10,... | collective-permute-start | bytes 196616 | tf_op jit(solution)/shard_map/ppermute | solution.py:311
  169.0 4.7 %collective-permute-start.21 = (f32[128,256]{1,0:T(8,128)S(1)}, f32[128,256]{1,0:T(8,128)S(1)}, u32[]{:S(2)}, u32[]{:S(2)}) collective-permute-start(f32[128,256]{1,0:T(8,128)S(1)} %pad_maximum_fusion.2), channel_id=1, source_target_pairs={{0,2},{1,3},{2,0},{3,1},{4,6},{5,7},{6,4},{7,5},{8,10},{9,11},{10,... | collective-permute-start | bytes 393224 | tf_op jit(solution)/shard_map/ppermute | solution.py:311
  185.3 1.8 copy-start.6
  185.3 6.2 %collective-permute-start.23 = (f32[256,256]{1,0:T(8,128)S(1)}, f32[256,256]{1,0:T(8,128)S(1)}, u32[]{:S(2)}, u32[]{:S(2)}) collective-permute-start(f32[256,256]{1,0:T(8,128)S(1)} %pad_maximum_fusion.1), channel_id=1, source_target_pairs={{0,1},{1,0},{2,3},{3,2},{4,5},{5,4},{6,7},{7,6},{8,9},{9,8},{10,11... | collective-permute-start | bytes 786440 | tf_op jit(solution)/shard_map/ppermute | solution.py:311

commit v5 on v4

--- a/solution.py
+++ b/solution.py
@@ -429,9 +429,12 @@
     own, other = split_rows(own + exchanged(other, core=1), low_bit)
     own, other = split_rows(own + exchanged(other, y=1), high_bit)
     from_left0 = along_columns(rim0, 1, "nothing")
-    arrived, down_right, from_left0, rim0 = wait((exchanged(other, y=3), down_right, from_left0, rim0))
+    relayed = jnp.where(here == cols - 1, half, rim1)
+    arrived, down_right, from_left0, rim0, relayed = wait(
+        (exchanged(other, y=3), down_right, from_left0, rim0, relayed)
+    )
     over_middle = across_middle(rim0, 1, 0)
-    from_left1 = along_columns(jnp.where(here == cols - 1, half, rim1), 1, "relay")
+    from_left1 = along_columns(relayed, 1, "relay")
     share = own + arrived
     share = share + exchanged(share, x=1)
     share = share + exchanged(share, x=3)

time: 194 us -> 199 us (1.026)
  waiting for transfers between devices: 51.3 us -> 58.6 us
  Pallas kernels: 40.5 us -> 34.9 us
  starting transfers between devices: 84.6 us -> 87.2 us
    ppermute x4, starting transfers between devices: 10.8 us -> 18.2 us  [passed_along(): return lax.ppermute(shard, axis, pairs)]
    ppermute x20, waiting for transfers between devices: 16 us -> 22.6 us  [moved(): return lax.ppermute(shard, ('row', 'col'), flat)]
    pallas_call x1, Pallas kernels: 20 us -> 14.4 us  [per_device(): pl.pallas_call(gradient_kernel, in_specs=[SCALARS, SCALARS] + [vmem] * 10...]
    ppermute x20, starting transfers between devices: 73.8 us -> 68.9 us  [moved(): return lax.ppermute(shard, ('row', 'col'), flat)]
  transfers between devices with their start and end apart: 24 -> 24, of which waited for: 9 -> 10; matrix products, arithmetic and copies ran while one was open for 5% -> 6% of each run, Pallas kernels for 10% -> 9%
where the time goes in v5:
time: 199 us; the launch traced here: 197 us
  starting transfers between devices  87.2 us (44%)
  waiting for transfers between devices  58.6 us (29%)
  Pallas kernels  34.9 us (18%)
  other arithmetic  9.57 us (5%)
  local copies, waits for them, and re-layouts  5.42 us (3%)
    ppermute x20, starting transfers between devices, moved(): return lax.ppermute(shard, ('row', 'col'), flat)  68.9 us
    ppermute x4, waiting for transfers between devices, passed_along(): return lax.ppermute(shard, axis, pairs)  36.1 us
    ppermute x20, waiting for transfers between devices, moved(): return lax.ppermute(shard, ('row', 'col'), flat)  22.6 us
    ppermute x4, starting transfers between devices, passed_along(): return lax.ppermute(shard, axis, pairs)  18.2 us
    pallas_call x1, Pallas kernels, per_device(): pl.pallas_call(gradient_kernel, in_specs=[SCALARS, SCALARS] + [vmem] * 10...  14.4 us
    pallas_call x1, Pallas kernels, per_device(): pl.pallas_call(order_kernel, grid=(slots,), in_specs=[per_slot(side, side...  8 us
    pallas_call x1, Pallas kernels, per_device(): pl.pallas_call(side_kernel, grid=(2, layers), in_specs=[left, edge, edge,...  4.64 us
    pallas_call x1, Pallas kernels, per_device(): pl.pallas_call(top_kernel, grid=(2, layers), in_specs=[SCALARS, upper, co...  4.34 us
  transfers between devices with their start and end apart: 24, of which 10 were waited for; matrix products, arithmetic and copies ran while one was open for 6% of the time, Pallas kernels for 9%

profile of v5, /device:TPU:3, one launch (start us, length us, event | category | flops | bytes accessed | tf_op | source)
XLA Modules:
  0.0 197.3 jit_solution(8590400460979757299)
XLA Ops:
  0.6 0.0 copy-start
  0.6 3.2 %slice_bitcast_fusion = (f32[2,512,256]{2,1,0:T(8,128)}, f32[2,512,256]{2,1,0:T(8,128)}) fusion(f32[2,2,512,512]{3,2,1,0:T(8,128)} %obj.1), kind=kLoop, calls=%fused_computation.1 | loop fusion | bytes 4194304 | tf_op jit(solution)/shard_map/squeeze | solution.py:391
  3.8 1.7 collective-permute-start.1
  5.5 1.5 fusion
  7.0 3.6 %collective-permute-start.3 = (f32[2,2,256,256]{3,2,1,0:T(8,128)}, f32[2,2,256,256]{3,2,1,0:T(8,128)S(1)}, u32[]{:S(2)}, u32[]{:S(2)}) collective-permute-start(f32[2,2,256,256]{3,2,1,0:T(8,128)} %get-tuple-element.49), channel_id=1, source_target_pairs={{16,0},{32,16},{48,32},{64,48},{80,64},{96,80},{112,96},{17,1},{33... | collective-permute-start | bytes 3145736 | tf_op jit(solution)/shard_map/ppermute | solution.py:18
  10.7 0.7 collective-permute-start.6
  11.4 2.5 %collective-permute-start = (f32[2,512,256]{2,1,0:T(8,128)}, f32[2,512,256]{2,1,0:T(8,128)S(1)}, u32[]{:S(2)}, u32[]{:S(2)}) collective-permute-start(f32[2,512,256]{2,1,0:T(8,128)} %get-tuple-element.51), channel_id=1, source_target_pairs={{1,0},{2,1},{3,2},{4,3},{5,4},{6,5},{7,6},{9,8},{10,9},{11,10},{12... | collective-permute-start | bytes 3145736 | tf_op jit(solution)/shard_map/ppermute | solution.py:311
  13.9 1.9 collective-permute-start.4
  15.8 8.0 %shard_map.86.measured = f32[8,256,256]{2,1,0:T(8,128)} custom-call(f32[8,256,256]{2,1,0:T(8,128)} %measured.1, bf16[256,256]{1,0:T(8,128)(2,1)} %constant.63.clone.picks), custom_call_target="tpu_custom_call" | custom-call | bytes 419430400 | tf_op jit(solution)/shard_map/pallas_call | solution.py:398
  23.8 0.0 collective-permute-done.1
  23.8 2.4 %broadcast_select_fusion.1 = f32[2,512,256]{2,1,0:T(8,128)} fusion(f32[2,512,256]{2,1,0:T(8,128)} %collective-permute-done.1, pred[]{:T(512)S(6)} %eq.32, f32[2,2,512,512]{3,2,1,0:T(8,128)} %obj.1), kind=kLoop, calls=%fused_computation.5 | loop fusion | flops 262144 | bytes 3145729 | tf_op jit(solution)/shard_map/jit(_where)/select_n | solution.py:394
  26.2 1.9 collective-permute-start.2
  28.1 6.0 %collective-permute-done.3.low_left = f32[2,2,256,256]{3,2,1,0:T(8,128)S(1)} collective-permute-done((f32[2,2,256,256]{3,2,1,0:T(8,128)}, f32[2,2,256,256]{3,2,1,0:T(8,128)S(1)}, u32[]{:S(2)}, u32[]{:S(2)}) %collective-permute-start.3) | collective-permute-done | bytes 1048608 | tf_op jit(solution)/shard_map/ppermute | solution.py:18
  34.1 3.4 %collective-permute-start.5 = (f32[2,2,256,256]{3,2,1,0:T(8,128)S(1)}, f32[2,2,256,256]{3,2,1,0:T(8,128)}, u32[]{:S(2)}, u32[]{:S(2)}) collective-permute-start(f32[2,2,256,256]{3,2,1,0:T(8,128)S(1)} %collective-permute-done.3.low_left), channel_id=1, source_target_pairs={{1,0},{2,1},{3,2},{4,3},{5,4},{6,5},{7,6},{9,8},{10,9},{11,10},{12... | collective-permute-start | bytes 3145736 | tf_op jit(solution)/shard_map/ppermute | solution.py:311
  37.4 0.7 copy.13.offsets
  38.8 0.0 collective-permute-done.6.middle
  38.8 0.0 collective-permute-done.right0
  38.8 17.8 %collective-permute-done.4.low_right = f32[2,2,256,256]{3,2,1,0:T(8,128)} collective-permute-done((f32[2,2,256,256]{3,2,1,0:T(8,128)}, f32[2,2,256,256]{3,2,1,0:T(8,128)}, u32[]{:S(2)}, u32[]{:S(2)}) %collective-permute-start.4) | collective-permute-done | bytes 1048608 | tf_op jit(solution)/shard_map/ppermute | solution.py:18
  56.6 0.0 collective-permute-done.2.right1
  56.6 0.0 collective-permute-done.5.corner
  56.7 14.4 %shard_map.87 = (f32[2,2,512,512]{3,2,1,0:T(8,128)}, f32[2,512,256]{2,1,0:T(8,128)}, f32[2,512,256]{2,1,0:T(8,128)}, f32[2,2,256,256]{3,2,1,0:T(8,128)}, f32[2,2...) custom-call(s32[8,2]{1,0:T(8,128)} %copy.13.offsets, s32[1]{0:T(128)S(6)} %copy.18.counts, ...), custom_call_target="tpu_custom_call" | custom-call | bytes 419430400 | tf_op jit(solution)/shard_map/pallas_call | solution.py:407
  71.1 2.0 %shard_map.88 = (f32[256,256]{1,0:T(8,128)}, f32[256,256]{1,0:T(8,128)}) custom-call(s32[1]{0:T(128)} %bitcast.1.mine, f32[2,256,256]{2,1,0:T(8,128)} %get-tuple-element.27.value), custom_call_target="tpu_custom_call" | custom-call | bytes 419430400 | tf_op jit(solution)/shard_map/pallas_call | solution.py:365
  73.1 2.9 %collective-permute-start.7 = (f32[256,256]{1,0:T(8,128)}, f32[256,256]{1,0:T(8,128)S(1)}, u32[]{:S(2)}, u32[]{:S(2)}) collective-permute-start(f32[256,256]{1,0:T(8,128)} %get-tuple-element.29), channel_id=1, source_target_pairs={{0,1},{1,0},{2,3},{3,2},{4,5},{5,4},{6,7},{7,6},{8,9},{9,8},{10,11... | collective-permute-start | bytes 786440 | tf_op jit(solution)/shard_map/ppermute | solution.py:311
  76.0 1.6 collective-permute-start.12
  77.6 13.4 %collective-permute-start.11 = (f32[2,512,256]{2,1,0:T(8,128)}, f32[2,512,256]{2,1,0:T(8,128)}, u32[]{:S(2)}, u32[]{:S(2)}) collective-permute-start(f32[2,512,256]{2,1,0:T(8,128)} %get-tuple-element.34), channel_id=1, source_target_pairs={{0,1},{1,2},{2,3},{3,4},{4,5},{5,6},{6,7},{8,9},{9,10},{10,11},{11... | collective-permute-start | bytes 3145736 | tf_op jit(solution)/shard_map/ppermute | solution.py:311
  91.0 9.8 %collective-permute-start.10 = (f32[2,2,256,256]{3,2,1,0:T(8,128)}, f32[2,2,256,256]{3,2,1,0:T(8,128)S(1)}, u32[]{:S(2)}, u32[]{:S(2)}) collective-permute-start(f32[2,2,256,256]{3,2,1,0:T(8,128)} %get-tuple-element.30), channel_id=1, source_target_pairs={{0,16},{16,32},{32,48},{48,64},{64,80},{80,96},{96,112},{1,17},{17... | collective-permute-start | bytes 3145736 | tf_op jit(solution)/shard_map/ppermute | solution.py:18
  100.8 0.0 collective-permute-done.7
  100.8 1.0 add.36
  101.8 0.7 slice_select_fusion
  102.5 5.0 %collective-permute-start.8 = (f32[128,256]{1,0:T(8,128)}, f32[128,256]{1,0:T(8,128)S(1)}, u32[]{:S(2)}, u32[]{:S(2)}) collective-permute-start(f32[128,256]{1,0:T(8,128)} %slice_select_fusion), channel_id=1, source_target_pairs={{0,2},{1,3},{2,0},{3,1},{4,6},{5,7},{6,4},{7,5},{8,10},{9,11},{10,... | collective-permute-start | bytes 393224 | tf_op jit(solution)/shard_map/ppermute | solution.py:311
  107.5 1.9 collective-permute-start.19
  109.4 0.7 collective-permute-done.8
  110.2 12.0 %collective-permute-start.9 = (f32[64,256]{1,0:T(8,128)S(1)}, f32[64,256]{1,0:T(8,128)S(1)}, u32[]{:S(2)}, u32[]{:S(2)}) collective-permute-start(f32[64,256]{1,0:T(8,128)S(1)} %slice_select_fusion.1), channel_id=1, source_target_pairs={{0,6},{1,7},{2,4},{3,5},{4,2},{5,3},{6,0},{7,1},{8,14},{9,15},{10,... | collective-permute-start | bytes 196616 | tf_op jit(solution)/shard_map/ppermute | solution.py:311
  122.2 0.0 collective-permute-done.12
  122.2 2.4 %broadcast_select_fusion = f32[2,512,256]{2,1,0:T(8,128)} fusion(f32[2,512,256]{2,1,0:T(8,128)} %collective-permute-done.12, f32[2,512,256]{2,1,0:T(8,128)} %get-tuple-element.32, pred[]{:T(512)S(6)} %eq.33), kind=kLoop, calls=%fused_computation.4 | loop fusion | flops 262144 | bytes 3145729 | tf_op jit(solution)/shard_map/jit(_where)/select_n | solution.py:432
  124.7 8.8 %collective-permute-done.9 = f32[64,256]{1,0:T(8,128)S(1)} collective-permute-done((f32[64,256]{1,0:T(8,128)S(1)}, f32[64,256]{1,0:T(8,128)S(1)}, u32[]{:S(2)}, u32[]{:S(2)}) %collective-permute-start.9) | collective-permute-done | bytes 65568 | tf_op jit(solution)/shard_map/ppermute | solution.py:311
  133.5 0.0 collective-permute-done.11.left0
  133.5 1.7 collective-permute-start.17
  135.1 1.9 collective-permute-start.18
  137.1 2.2 %collective-permute-start.13 = (f32[64,256]{1,0:T(8,128)S(1)}, f32[64,256]{1,0:T(8,128)S(1)}, u32[]{:S(2)}, u32[]{:S(2)}) collective-permute-start(f32[64,256]{1,0:T(8,128)S(1)} %select_add_fusion.2), channel_id=1, source_target_pairs={{0,32},{1,33},{2,34},{3,35},{4,36},{5,37},{6,38},{7,39},{8,40},{9,... | collective-permute-start | bytes 196616 | tf_op jit(solution)/shard_map/ppermute | solution.py:311
  139.3 1.7 collective-permute-done.13
  141.0 2.3 %collective-permute-start.14 = (f32[64,256]{1,0:T(8,128)S(1)}, f32[64,256]{1,0:T(8,128)S(1)}, u32[]{:S(2)}, u32[]{:S(2)}) collective-permute-start(f32[64,256]{1,0:T(8,128)S(1)} %add.39), channel_id=1, source_target_pairs={{0,96},{1,97},{2,98},{3,99},{4,100},{5,101},{6,102},{7,103},{8,104... | collective-permute-start | bytes 196616 | tf_op jit(solution)/shard_map/ppermute | solution.py:311
  143.3 1.7 collective-permute-done.14
  145.0 0.1 collective-permute-start.15
  145.1 3.3 %collective-permute-done.15 = f32[64,256]{1,0:T(8,128)S(1)} collective-permute-done((f32[64,256]{1,0:T(8,128)S(1)}, f32[64,256]{1,0:T(8,128)S(1)}, u32[]{:S(2)}, u32[]{:S(2)}) %collective-permute-start.15) | collective-permute-done | bytes 65568 | tf_op jit(solution)/shard_map/ppermute | solution.py:311
  148.4 0.0 copy-start.8
  148.4 9.9 %collective-permute-start.16 = (f32[64,256]{1,0:T(8,128)S(1)}, f32[64,256]{1,0:T(8,128)S(1)}, u32[]{:S(2)}, u32[]{:S(2)}) collective-permute-start(f32[64,256]{1,0:T(8,128)S(1)} %add.41.refs_0_), channel_id=1, source_target_pairs={{0,24},{1,25},{2,26},{3,27},{4,28},{5,29},{6,30},{7,31},{8,16},{9,... | collective-permute-start | bytes 196616 | tf_op jit(solution)/shard_map/ppermute | solution.py:311
  158.3 1.3 select_add_fusion
  159.6 3.9 %collective-permute-done.16.refs_1_ = f32[64,256]{1,0:T(8,128)S(1)} collective-permute-done((f32[64,256]{1,0:T(8,128)S(1)}, f32[64,256]{1,0:T(8,128)S(1)}, u32[]{:S(2)}, u32[]{:S(2)}) %collective-permute-start.16) | collective-permute-done | bytes 65568 | tf_op jit(solution)/shard_map/ppermute | solution.py:311
  163.5 0.0 collective-permute-done.17.middle0
  163.5 0.0 collective-permute-done.18.left1
  163.5 2.9 %collective-permute-start.22 = (f32[2,2,256,256]{3,2,1,0:T(8,128)}, f32[2,2,256,256]{3,2,1,0:T(8,128)S(1)}, u32[]{:S(2)}, u32[]{:S(2)}) collective-permute-start(f32[2,2,256,256]{3,2,1,0:T(8,128)} %select_add_fusion), channel_id=1, source_target_pairs={{0,16},{16,32},{32,48},{48,64},{64,80},{80,96},{96,112},{1,17},{17... | collective-permute-start | bytes 3145736 | tf_op jit(solution)/shard_map/ppermute | solution.py:18
  166.4 1.5 shard_map.89
  167.9 2.1 %collective-permute-start.20 = (f32[64,256]{1,0:T(8,128)}, f32[64,256]{1,0:T(8,128)S(1)}, u32[]{:S(2)}, u32[]{:S(2)}) collective-permute-start(f32[64,256]{1,0:T(8,128)} %shard_map.89), channel_id=1, source_target_pairs={{0,6},{1,7},{2,4},{3,5},{4,2},{5,3},{6,0},{7,1},{8,14},{9,15},{10,... | collective-permute-start | bytes 196616 | tf_op jit(solution)/shard_map/ppermute | solution.py:311
  170.0 2.6 %collective-permute-done.20 = f32[64,256]{1,0:T(8,128)S(1)} collective-permute-done((f32[64,256]{1,0:T(8,128)}, f32[64,256]{1,0:T(8,128)S(1)}, u32[]{:S(2)}, u32[]{:S(2)}) %collective-permute-start.20) | collective-permute-done | bytes 65568 | tf_op jit(solution)/shard_map/ppermute | solution.py:311
  172.6 0.9 broadcast_select_fusion.7
  173.5 0.1 collective-permute-start.21
  173.6 4.6 %shard_map.90.held = f32[2,2,512,512]{3,2,1,0:T(8,128)} custom-call(f32[2,2,512,512]{3,2,1,0:T(8,128)} %get-tuple-element.40.held, f32[2,512,256]{2,1,0:T(8,128)} %collective-permute-done.11.left0, f32[2,512,256]{2,1,0:T(8,128)} %collective-permute-done.17.middle0, f32[2,512,256]{2,1,0:T(8,128)} %collective-permute-done.18.left1), custom_call_target="tpu_custom_call", output_to_operand_aliasing={{}: (0, {})} | custom-call | bytes 1024 | tf_op jit(solution)/shard_map/pallas_call | solution.py:455
  178.2 0.0 collective-permute-done.21
  178.3 12.3 %collective-permute-done.22.low_left = f32[2,2,256,256]{3,2,1,0:T(8,128)S(1)} collective-permute-done((f32[2,2,256,256]{3,2,1,0:T(8,128)}, f32[2,2,256,256]{3,2,1,0:T(8,128)S(1)}, u32[]{:S(2)}, u32[]{:S(2)}) %collective-permute-start.22) | collective-permute-done | bytes 1048608 | tf_op jit(solution)/shard_map/ppermute | solution.py:18
  190.6 1.5 collective-permute-start.23
  192.1 4.3 %shard_map.91 = f32[2,2,512,512]{3,2,1,0:T(8,128)} custom-call(s32[1]{0:T(128)} %bitcast.own_corner, f32[2,2,512,512]{3,2,1,0:T(8,128)} %shard_map.90.held, f32[2,2,256,256]{3,2,1,0:T(8,128)} %copy-done.1, f32[2,2,256,256]{3,2,1,0:T(8,128)} %copy-done.6, f32[2,2,256,256]{3,2,1,0:T(8,128)} %copy-done.2), custom_call_target="tpu_custom_call", output_to_operand_aliasing={{}: (1, {})} | custom-call | tf_op jit(solution)/shard_map/pallas_call | solution.py:461
  196.4 0.0 collective-permute-done.23
  196.5 0.8 pad_maximum_fusion
  (32 shorter events, 0.2 us)
Async XLA Ops:
  0.6 4.9 %copy-start = (f32[2,2,512,512]{3,2,1,0:T(8,128)S(1)}, f32[2,2,512,512]{3,2,1,0:T(8,128)}, u32[]{:S(2)}) copy-start(f32[2,2,512,512]{3,2,1,0:T(8,128)} %obj.1) | copy-start | bytes 12582916
  3.8 20.0 %collective-permute-start.1 = (f32[2,512,256]{2,1,0:T(8,128)}, f32[2,512,256]{2,1,0:T(8,128)}, u32[]{:S(2)}, u32[]{:S(2)}) collective-permute-start(f32[2,512,256]{2,1,0:T(8,128)} %get-tuple-element.50), channel_id=1, source_target_pairs={{8,16},{24,0},{40,48},{56,32},{72,80},{88,64},{104,112},{120,96}} | collective-permute-start | bytes 3145736 | tf_op jit(solution)/shard_map/ppermute | solution.py:311
  7.0 30.4 %copy-start.10 = (s32[8,2]{0,1:T(2,128)S(1)}, s32[8,2]{0,1:T(2,128)}, u32[]{:S(2)}) copy-start(s32[8,2]{0,1:T(2,128)} %param.10) | copy-start | bytes 196
  7.0 27.0 %collective-permute-start.3 = (f32[2,2,256,256]{3,2,1,0:T(8,128)}, f32[2,2,256,256]{3,2,1,0:T(8,128)S(1)}, u32[]{:S(2)}, u32[]{:S(2)}) collective-permute-start(f32[2,2,256,256]{3,2,1,0:T(8,128)} %get-tuple-element.49), channel_id=1, source_target_pairs={{16,0},{32,16},{48,32},{64,48},{80,64},{96,80},{112,96},{17,1},{33... | collective-permute-start | bytes 3145736 | tf_op jit(solution)/shard_map/ppermute | solution.py:18
  10.7 28.1 %collective-permute-start.6 = (f32[2,2,256,256]{3,2,1,0:T(8,128)}, f32[2,2,256,256]{3,2,1,0:T(8,128)S(1)}, u32[]{:S(2)}, u32[]{:S(2)}) collective-permute-start(f32[2,2,256,256]{3,2,1,0:T(8,128)} %get-tuple-element.49), channel_id=1, source_target_pairs={{24,7},{40,23},{56,39},{72,55},{88,71},{104,87},{120,103}} | collective-permute-start | bytes 3145736 | tf_op jit(solution)/shard_map/ppermute | solution.py:311
  11.4 27.4 %collective-permute-start = (f32[2,512,256]{2,1,0:T(8,128)}, f32[2,512,256]{2,1,0:T(8,128)S(1)}, u32[]{:S(2)}, u32[]{:S(2)}) collective-permute-start(f32[2,512,256]{2,1,0:T(8,128)} %get-tuple-element.51), channel_id=1, source_target_pairs={{1,0},{2,1},{3,2},{4,3},{5,4},{6,5},{7,6},{9,8},{10,9},{11,10},{12... | collective-permute-start | bytes 3145736 | tf_op jit(solution)/shard_map/ppermute | solution.py:311
  13.9 42.7 %collective-permute-start.4 = (f32[2,2,256,256]{3,2,1,0:T(8,128)}, f32[2,2,256,256]{3,2,1,0:T(8,128)}, u32[]{:S(2)}, u32[]{:S(2)}) collective-permute-start(f32[2,2,256,256]{3,2,1,0:T(8,128)} %get-tuple-element.48), channel_id=1, source_target_pairs={{16,0},{32,16},{48,32},{64,48},{80,64},{96,80},{112,96},{17,1},{33... | collective-permute-start | bytes 3145736 | tf_op jit(solution)/shard_map/ppermute | solution.py:18
  26.2 30.4 %collective-permute-start.2 = (f32[2,512,256]{2,1,0:T(8,128)}, f32[2,512,256]{2,1,0:T(8,128)}, u32[]{:S(2)}, u32[]{:S(2)}) collective-permute-start(f32[2,512,256]{2,1,0:T(8,128)} %broadcast_select_fusion.1), channel_id=1, source_target_pairs={{1,0},{2,1},{3,2},{4,3},{5,4},{6,5},{7,6},{9,8},{10,9},{11,10},{12... | collective-permute-start | bytes 3145736 | tf_op jit(solution)/shard_map/ppermute | solution.py:311
  34.1 22.6 %copy-start.3 = (f32[2,2,256,256]{3,2,1,0:T(8,128)}, f32[2,2,256,256]{3,2,1,0:T(8,128)S(1)}, u32[]{:S(2)}) copy-start(f32[2,2,256,256]{3,2,1,0:T(8,128)S(1)} %collective-permute-done.3.low_left) | copy-start | bytes 3145732
  34.1 22.6 %collective-permute-start.5 = (f32[2,2,256,256]{3,2,1,0:T(8,128)S(1)}, f32[2,2,256,256]{3,2,1,0:T(8,128)}, u32[]{:S(2)}, u32[]{:S(2)}) collective-permute-start(f32[2,2,256,256]{3,2,1,0:T(8,128)S(1)} %collective-permute-done.3.low_left), channel_id=1, source_target_pairs={{1,0},{2,1},{3,2},{4,3},{5,4},{6,5},{7,6},{9,8},{10,9},{11,10},{12... | collective-permute-start | bytes 3145736 | tf_op jit(solution)/shard_map/ppermute | solution.py:311
  38.8 17.9 %copy-start.4 = (f32[2,2,256,256]{3,2,1,0:T(8,128)}, f32[2,2,256,256]{3,2,1,0:T(8,128)S(1)}, u32[]{:S(2)}) copy-start(f32[2,2,256,256]{3,2,1,0:T(8,128)S(1)} %collective-permute-done.6.middle) | copy-start | bytes 3145732
  38.8 17.9 %copy-start.5 = (f32[2,512,256]{2,1,0:T(8,128)}, f32[2,512,256]{2,1,0:T(8,128)S(1)}, u32[]{:S(2)}) copy-start(f32[2,512,256]{2,1,0:T(8,128)S(1)} %collective-permute-done.right0) | copy-start | bytes 3145732
  71.1 87.3 %copy-start.7 = (f32[2,2,256,256]{3,2,1,0:T(8,128)S(1)}, f32[2,2,256,256]{3,2,1,0:T(8,128)}, u32[]{:S(2)}) copy-start(f32[2,2,256,256]{3,2,1,0:T(8,128)} %get-tuple-element.36) | copy-start | bytes 3145732
  73.1 27.7 %collective-permute-start.7 = (f32[256,256]{1,0:T(8,128)}, f32[256,256]{1,0:T(8,128)S(1)}, u32[]{:S(2)}, u32[]{:S(2)}) collective-permute-start(f32[256,256]{1,0:T(8,128)} %get-tuple-element.29), channel_id=1, source_target_pairs={{0,1},{1,0},{2,3},{3,2},{4,5},{5,4},{6,7},{7,6},{8,9},{9,8},{10,11... | collective-permute-start | bytes 786440 | tf_op jit(solution)/shard_map/ppermute | solution.py:311
  76.0 46.3 %collective-permute-start.12 = (f32[2,512,256]{2,1,0:T(8,128)}, f32[2,512,256]{2,1,0:T(8,128)}, u32[]{:S(2)}, u32[]{:S(2)}) collective-permute-start(f32[2,512,256]{2,1,0:T(8,128)} %get-tuple-element.32), channel_id=1, source_target_pairs={{7,31},{23,15},{39,63},{55,47},{71,95},{87,79},{103,127},{119,111}} | collective-permute-start | bytes 3145736 | tf_op jit(solution)/shard_map/ppermute | solution.py:311
  77.6 55.9 %collective-permute-start.11 = (f32[2,512,256]{2,1,0:T(8,128)}, f32[2,512,256]{2,1,0:T(8,128)}, u32[]{:S(2)}, u32[]{:S(2)}) collective-permute-start(f32[2,512,256]{2,1,0:T(8,128)} %get-tuple-element.34), channel_id=1, source_target_pairs={{0,1},{1,2},{2,3},{3,4},{4,5},{5,6},{6,7},{8,9},{9,10},{10,11},{11... | collective-permute-start | bytes 3145736 | tf_op jit(solution)/shard_map/ppermute | solution.py:311
  91.0 42.4 %collective-permute-start.10 = (f32[2,2,256,256]{3,2,1,0:T(8,128)}, f32[2,2,256,256]{3,2,1,0:T(8,128)S(1)}, u32[]{:S(2)}, u32[]{:S(2)}) collective-permute-start(f32[2,2,256,256]{3,2,1,0:T(8,128)} %get-tuple-element.30), channel_id=1, source_target_pairs={{0,16},{16,32},{32,48},{48,64},{64,80},{80,96},{96,112},{1,17},{17... | collective-permute-start | bytes 3145736 | tf_op jit(solution)/shard_map/ppermute | solution.py:18
  102.5 7.6 %collective-permute-start.8 = (f32[128,256]{1,0:T(8,128)}, f32[128,256]{1,0:T(8,128)S(1)}, u32[]{:S(2)}, u32[]{:S(2)}) collective-permute-start(f32[128,256]{1,0:T(8,128)} %slice_select_fusion), channel_id=1, source_target_pairs={{0,2},{1,3},{2,0},{3,1},{4,6},{5,7},{6,4},{7,5},{8,10},{9,11},{10,... | collective-permute-start | bytes 393224 | tf_op jit(solution)/shard_map/ppermute | solution.py:311
  107.5 50.8 %collective-permute-start.19 = (f32[2,2,256,256]{3,2,1,0:T(8,128)}, f32[2,2,256,256]{3,2,1,0:T(8,128)S(1)}, u32[]{:S(2)}, u32[]{:S(2)}) collective-permute-start(f32[2,2,256,256]{3,2,1,0:T(8,128)} %get-tuple-element.37), channel_id=1, source_target_pairs={{0,1},{1,2},{2,3},{3,4},{4,5},{5,6},{6,7},{8,9},{9,10},{10,11},{11... | collective-permute-start | bytes 3145736 | tf_op jit(solution)/shard_map/ppermute | solution.py:311
  110.2 23.3 %collective-permute-start.9 = (f32[64,256]{1,0:T(8,128)S(1)}, f32[64,256]{1,0:T(8,128)S(1)}, u32[]{:S(2)}, u32[]{:S(2)}) collective-permute-start(f32[64,256]{1,0:T(8,128)S(1)} %slice_select_fusion.1), channel_id=1, source_target_pairs={{0,6},{1,7},{2,4},{3,5},{4,2},{5,3},{6,0},{7,1},{8,14},{9,15},{10,... | collective-permute-start | bytes 196616 | tf_op jit(solution)/shard_map/ppermute | solution.py:311
  133.5 44.8 %copy-start.2 = (f32[2,2,256,256]{3,2,1,0:T(8,128)}, f32[2,2,256,256]{3,2,1,0:T(8,128)S(1)}, u32[]{:S(2)}) copy-start(f32[2,2,256,256]{3,2,1,0:T(8,128)S(1)} %collective-permute-done.10.low_right) | copy-start | bytes 3145732
  133.5 30.0 %collective-permute-start.17 = (f32[2,512,256]{2,1,0:T(8,128)}, f32[2,512,256]{2,1,0:T(8,128)}, u32[]{:S(2)}, u32[]{:S(2)}) collective-permute-start(f32[2,512,256]{2,1,0:T(8,128)} %get-tuple-element.34), channel_id=1, source_target_pairs={{7,8},{23,24},{39,40},{55,56},{71,72},{87,88},{103,104},{119,120}} | collective-permute-start | bytes 3145736 | tf_op jit(solution)/shard_map/ppermute | solution.py:311
  135.1 28.4 %collective-permute-start.18 = (f32[2,512,256]{2,1,0:T(8,128)}, f32[2,512,256]{2,1,0:T(8,128)}, u32[]{:S(2)}, u32[]{:S(2)}) collective-permute-start(f32[2,512,256]{2,1,0:T(8,128)} %broadcast_select_fusion), channel_id=1, source_target_pairs={{0,1},{1,2},{2,3},{3,4},{4,5},{5,6},{6,7},{8,9},{9,10},{10,11},{11... | collective-permute-start | bytes 3145736 | tf_op jit(solution)/shard_map/ppermute | solution.py:311
  137.1 3.9 %collective-permute-start.13 = (f32[64,256]{1,0:T(8,128)S(1)}, f32[64,256]{1,0:T(8,128)S(1)}, u32[]{:S(2)}, u32[]{:S(2)}) collective-permute-start(f32[64,256]{1,0:T(8,128)S(1)} %select_add_fusion.2), channel_id=1, source_target_pairs={{0,32},{1,33},{2,34},{3,35},{4,36},{5,37},{6,38},{7,39},{8,40},{9,... | collective-permute-start | bytes 196616 | tf_op jit(solution)/shard_map/ppermute | solution.py:311
  141.0 4.0 %collective-permute-start.14 = (f32[64,256]{1,0:T(8,128)S(1)}, f32[64,256]{1,0:T(8,128)S(1)}, u32[]{:S(2)}, u32[]{:S(2)}) collective-permute-start(f32[64,256]{1,0:T(8,128)S(1)} %add.39), channel_id=1, source_target_pairs={{0,96},{1,97},{2,98},{3,99},{4,100},{5,101},{6,102},{7,103},{8,104... | collective-permute-start | bytes 196616 | tf_op jit(solution)/shard_map/ppermute | solution.py:311
  145.0 3.4 %collective-permute-start.15 = (f32[64,256]{1,0:T(8,128)S(1)}, f32[64,256]{1,0:T(8,128)S(1)}, u32[]{:S(2)}, u32[]{:S(2)}) collective-permute-start(f32[64,256]{1,0:T(8,128)S(1)} %add.40), channel_id=1, source_target_pairs={{0,16},{1,17},{2,18},{3,19},{4,20},{5,21},{6,22},{7,23},{8,24},{9,... | collective-permute-start | bytes 196616 | tf_op jit(solution)/shard_map/ppermute | solution.py:311
  148.4 18.0 %copy-start.8 = (f32[64,256]{1,0:T(8,128)}, f32[64,256]{1,0:T(8,128)S(1)}, u32[]{:S(2)}) copy-start(f32[64,256]{1,0:T(8,128)S(1)} %add.41.refs_0_) | copy-start | bytes 196612
  148.4 15.1 %collective-permute-start.16 = (f32[64,256]{1,0:T(8,128)S(1)}, f32[64,256]{1,0:T(8,128)S(1)}, u32[]{:S(2)}, u32[]{:S(2)}) collective-permute-start(f32[64,256]{1,0:T(8,128)S(1)} %add.41.refs_0_), channel_id=1, source_target_pairs={{0,24},{1,25},{2,26},{3,27},{4,28},{5,29},{6,30},{7,31},{8,16},{9,... | collective-permute-start | bytes 196616 | tf_op jit(solution)/shard_map/ppermute | solution.py:311
  158.3 19.9 %copy-start.1 = (f32[2,2,256,256]{3,2,1,0:T(8,128)}, f32[2,2,256,256]{3,2,1,0:T(8,128)S(1)}, u32[]{:S(2)}) copy-start(f32[2,2,256,256]{3,2,1,0:T(8,128)S(1)} %collective-permute-done.19.corner) | copy-start | bytes 3145732
  163.5 2.9 %copy-start.9 = (f32[64,256]{1,0:T(8,128)}, f32[64,256]{1,0:T(8,128)S(1)}, u32[]{:S(2)}) copy-start(f32[64,256]{1,0:T(8,128)S(1)} %collective-permute-done.16.refs_1_) | copy-start | bytes 196612
  163.5 27.1 %collective-permute-start.22 = (f32[2,2,256,256]{3,2,1,0:T(8,128)}, f32[2,2,256,256]{3,2,1,0:T(8,128)S(1)}, u32[]{:S(2)}, u32[]{:S(2)}) collective-permute-start(f32[2,2,256,256]{3,2,1,0:T(8,128)} %select_add_fusion), channel_id=1, source_target_pairs={{0,16},{16,32},{32,48},{48,64},{64,80},{80,96},{96,112},{1,17},{17... | collective-permute-start | bytes 3145736 | tf_op jit(solution)/shard_map/ppermute | solution.py:18
  167.9 4.7 %collective-permute-start.20 = (f32[64,256]{1,0:T(8,128)}, f32[64,256]{1,0:T(8,128)S(1)}, u32[]{:S(2)}, u32[]{:S(2)}) collective-permute-start(f32[64,256]{1,0:T(8,128)} %shard_map.89), channel_id=1, source_target_pairs={{0,6},{1,7},{2,4},{3,5},{4,2},{5,3},{6,0},{7,1},{8,14},{9,15},{10,... | collective-permute-start | bytes 196616 | tf_op jit(solution)/shard_map/ppermute | solution.py:311
  173.5 4.7 %collective-permute-start.21 = (f32[128,256]{1,0:T(8,128)S(1)}, f32[128,256]{1,0:T(8,128)S(1)}, u32[]{:S(2)}, u32[]{:S(2)}) collective-permute-start(f32[128,256]{1,0:T(8,128)S(1)} %pad_maximum_fusion.2), channel_id=1, source_target_pairs={{0,2},{1,3},{2,0},{3,1},{4,6},{5,7},{6,4},{7,5},{8,10},{9,11},{10,... | collective-permute-start | bytes 393224 | tf_op jit(solution)/shard_map/ppermute | solution.py:311
  190.6 1.5 copy-start.6
  190.6 5.8 %collective-permute-start.23 = (f32[256,256]{1,0:T(8,128)S(1)}, f32[256,256]{1,0:T(8,128)S(1)}, u32[]{:S(2)}, u32[]{:S(2)}) collective-permute-start(f32[256,256]{1,0:T(8,128)S(1)} %pad_maximum_fusion.1), channel_id=1, source_target_pairs={{0,1},{1,0},{2,3},{3,2},{4,5},{5,4},{6,7},{7,6},{8,9},{9,8},{10,11... | collective-permute-start | bytes 786440 | tf_op jit(solution)/shard_map/ppermute | solution.py:311
